TPU v7x, 256 devices: a whole 4x4x8 slice. The times are simulated.
256 devices in a mesh: dp: 4 (over y), region: 64 (over z, x, core).
Axes of the slice: x: 4, y: 4, z: 8, core: 2. Of those that a mesh axis runs over, the one named last changes fastest.
Arguments:
- query: bfloat16 [4, 16384, 1024], P('dp', 'region'), may hold values from -17 to 17
- key_in: bfloat16 [4, 16384, 1024], P('dp', 'region'), may hold values from -17 to 17
- value: bfloat16 [4, 16384, 1024], P('dp', 'region'), may hold values from -6 to 6
- d_out: bfloat16 [4, 16384, 1024], P('dp', 'region'), may hold values from -6 to 6
- out_weight: bfloat16 [1024, 1024], replicated, may hold values from -0.1875 to 0.1875
- attended: int32 [64, 3], P('region'), may hold values from 0 to 63, as said below
- counts: int32 [64], P('region'), may hold values from 2 to 3, as said below
Outputs:
- layer_out: bfloat16 [4, 16384, 1024], P('dp', 'region')
- d_query: bfloat16 [4, 16384, 1024], P('dp', 'region')
- d_key: bfloat16 [4, 16384, 1024], P('dp', 'region')
- d_value: bfloat16 [4, 16384, 1024], P('dp', 'region')
- d_weight: float32 [1024, 1024], P('region')
Inputs may be any that keep to these rules, and one draw needn't show every extreme that they name: `attended`: row r starts with r; its next counts[r] - 1 entries are distinct regions among r - 1, r + 1 and one hub region common to all rows (never r itself again); the hub stands in some row whose region is not beside it; entries past counts[r] repeat r. `counts`: some region has 3 in every draw.
All inputs are finite; a program needn't handle non-finite values.
Results may differ from a plain program's by a relative error of at most 0.019.
Values may be sent and summed in bfloat16 or wider, within the bound.
No kernel may reach another device: no remote copies, remote signals or barrier semaphores. Data moves between devices by JAX's collectives and lax.ppermute only.
A program may use at most 128 MiB of HBM per device.

v0:
```python
import jax
import jax.numpy as jnp
from jax import lax
from jax.sharding import PartitionSpec as P

HEAD_DIM = 64


def extended(cells, sides, width):
    for axis, dim in sides:
        count = lax.axis_size(axis)
        ends = count - 1
        head = lax.slice_in_dim(cells, 0, width, axis=dim)
        tail = lax.slice_in_dim(cells, cells.shape[dim] - width, cells.shape[dim], axis=dim)
        cells = jnp.concatenate(
            [
                lax.ppermute(tail, axis, [(i, (i + 1) % count) for i in range(ends)]),
                cells,
                lax.ppermute(head, axis, [((i + 1) % count, i) for i in range(ends)]),
            ],
            axis=dim,
        )
    return cells


def from_root(value, axis, source):
    kept = jnp.where(lax.axis_index(axis) == source, value, 0).astype(value.dtype)
    return lax.psum(kept, axis)


def shifted(value, axis, steps):
    count = lax.axis_size(axis)
    leading, last = (max(0, -steps), min(count, count - steps))
    return lax.ppermute(value, axis, [(source, source + steps) for source in range(leading, last)])


def columns(matrix, start, span):
    return lax.dynamic_slice_in_dim(matrix, start, span, 1)


def split_heads(matrix, head_size):
    return matrix.reshape(matrix.shape[0], -1, head_size)


def softmax_rows(query_part, key_part, key_valid, scale):
    scores = (
        jnp.einsum("tgd,kgd->gtk", query_part, key_part, preferred_element_type=jnp.float32) * scale
    )
    scores = jnp.where(key_valid[None, None, :], scores, -1e30)
    largest = jnp.max(scores, axis=-1, keepdims=True)
    weights = jnp.exp(scores - largest)
    return weights / jnp.sum(weights, axis=-1, keepdims=True)


def on_device(query, key_in, value, d_out, out_weight, attended, counts):
    region = lax.axis_index("region")
    tok_rows = query.shape[1]
    width = query.shape[2]
    head_size = HEAD_DIM
    heads = width // head_size
    group = 4
    span = group * head_size
    blocks = heads // group
    scale = head_size ** (-0.5)
    own_query = query[0]
    grad_out = d_out[0]
    listed = attended[0]
    slots = listed.shape[0]
    slot_valid = jnp.arange(slots) < counts[0]
    beside = (listed == region - 1) | (listed == region) | (listed == region + 1)
    far_local = jnp.max(jnp.where(beside | jnp.logical_not(slot_valid), -1, listed))
    far_id = lax.pmax(far_local, "region")
    paired = jnp.stack([key_in[0], value[0]])
    widened = extended(paired, (("region", 1),), tok_rows)
    far_pair = from_root(paired, "region", far_id)
    candidates = jnp.stack([widened[:, :tok_rows], paired, widened[:, 2 * tok_rows :], far_pair])
    which = jnp.where(
        listed == region, 1, jnp.where(listed == far_id, 3, jnp.where(listed == region - 1, 0, 2))
    )
    chosen = jnp.take(candidates, which, axis=0)
    keys = chosen[:, 0].reshape(slots * tok_rows, width)
    values = chosen[:, 1].reshape(slots * tok_rows, width)
    key_valid = jnp.repeat(slot_valid, tok_rows)

    def forward_block(index):
        start = index * span
        query_part = split_heads(columns(own_query, start, span), head_size)
        key_part = split_heads(columns(keys, start, span), head_size)
        value_part = split_heads(columns(values, start, span), head_size)
        probs = softmax_rows(query_part, key_part, key_valid, scale).astype(jnp.bfloat16)
        mixed = jnp.einsum("gtk,kgd->tgd", probs, value_part, preferred_element_type=jnp.float32)
        return mixed.reshape(tok_rows, span)

    pieces = lax.map(forward_block, jnp.arange(blocks))
    attn = jnp.moveaxis(pieces, 0, 1).reshape(tok_rows, width).astype(jnp.bfloat16)
    layer = jnp.dot(attn, out_weight, preferred_element_type=jnp.float32).astype(jnp.bfloat16)
    d_attn = lax.dot_general(
        grad_out, out_weight, (((1,), (1,)), ((), ())), preferred_element_type=jnp.float32
    ).astype(jnp.bfloat16)

    def backward_block(index):
        start = index * span
        query_part = split_heads(columns(own_query, start, span), head_size)
        key_part = split_heads(columns(keys, start, span), head_size)
        value_part = split_heads(columns(values, start, span), head_size)
        grad_part = split_heads(columns(d_attn, start, span), head_size)
        probs_full = softmax_rows(query_part, key_part, key_valid, scale)
        probs = probs_full.astype(jnp.bfloat16)
        dprob = jnp.einsum(
            "tgd,kgd->gtk", grad_part, value_part, preferred_element_type=jnp.float32
        )
        center = jnp.sum(probs_full * dprob, axis=-1, keepdims=True)
        dscore = (probs_full * (dprob - center) * scale).astype(jnp.bfloat16)
        grad_query = jnp.einsum(
            "gtk,kgd->tgd", dscore, key_part, preferred_element_type=jnp.float32
        ).reshape(tok_rows, span)
        grad_key = jnp.einsum(
            "gtk,tgd->kgd", dscore, query_part, preferred_element_type=jnp.float32
        ).reshape(-1, span)
        grad_value = jnp.einsum(
            "gtk,tgd->kgd", probs, grad_part, preferred_element_type=jnp.float32
        ).reshape(-1, span)
        return (grad_query, grad_key, grad_value)

    query_parts, key_parts, value_parts = lax.map(backward_block, jnp.arange(blocks))
    query_rows = jnp.moveaxis(query_parts, 0, 1).reshape(tok_rows, width).astype(jnp.bfloat16)
    key_grad = jnp.moveaxis(key_parts, 0, 1).reshape(slots, tok_rows, width)
    value_grad = jnp.moveaxis(value_parts, 0, 1).reshape(slots, tok_rows, width)
    slot_grads = jnp.stack([key_grad, value_grad], axis=1)

    def to_target(target):
        picked = (which == target) & slot_valid
        return jnp.sum(jnp.where(picked[:, None, None, None], slot_grads, 0.0), axis=0)

    from_right = shifted(to_target(0), "region", -1)
    from_left = shifted(to_target(2), "region", 1)
    far_grad = to_target(3)
    far_total = lax.psum(far_grad, "region")
    total = to_target(1) + from_right + from_left + jnp.where(region == far_id, far_total, 0.0)
    rows_part = lax.psum_scatter(
        lax.dot_general(
            attn, grad_out, (((0,), (0,)), ((), ())), preferred_element_type=jnp.float32
        ),
        "region",
        scatter_dimension=0,
        tiled=True,
    )
    d_weight = lax.psum(rows_part, "dp")
    return (
        layer[None],
        query_rows[None],
        total[0].astype(jnp.bfloat16)[None],
        total[1].astype(jnp.bfloat16)[None],
        d_weight,
    )


def solution(mesh):
    in_specs = (
        P("dp", "region", None),
        P("dp", "region", None),
        P("dp", "region", None),
        P("dp", "region", None),
        P(),
        P("region", None),
        P("region"),
    )
    out_specs = (
        P("dp", "region", None),
        P("dp", "region", None),
        P("dp", "region", None),
        P("dp", "region", None),
        P("region", None),
    )
    return jax.shard_map(
        on_device, mesh=mesh, in_specs=in_specs, out_specs=out_specs, check_vma=False
    )
```

profile of v0, /device:TPU:1, one launch (start us, length us, event | category | flops | bytes accessed | tf_op | source)
XLA Modules:
  0.0 808.6 jit_solution(751732499107161685)
XLA Ops:
  7.2 1.2 constant_dynamic-update-slice_fusion.5
  9.5 5.2 collective-permute-start.1
  15.3 1.3 fusion.46
  16.6 1.9 collective-permute-start
  18.6 27.6 %pmax.7 = s32[]{:T(128)} all-reduce(s32[]{:T(128)} %fusion.46), channel_id=1, replica_groups=mesh['dp'=4,'region'=64] {'region'}, use_global_device_ids=true, to_apply=%region_1.2 | all-reduce | flops 1 | bytes 8 | tf_op jit(solution)/shard_map/pmax | solution.py:72
  47.9 2.0 copy.19
  51.3 2.6 convolution_convert_fusion
  53.9 174.0 %all-reduce.4.cloned.1.call-done = bf16[1,2,256,1024]{3,2,1,0:T(8,128)(2,1)} async-done(((bf16[1,2,256,1024]{3,2,1,0:T(8,128)(2,1)}), bf16[1,2,256,1024]{3,2,1,0:T(8,128)(2,1)}) %all-reduce.4.cloned.1.call-update) | async-done | bytes 1048592 | tf_op jit(solution)/shard_map/psum | solution.py:28
  227.9 3.6 pad_maximum_fusion
  231.5 4.8 gather_fusion
  236.3 2.3 broadcast_select_fusion
  238.5 2.2 fusion.49
  240.8 2.6 copy.21
  243.3 2.6 copy.20
  246.8 141.2 %while.27 = (s32[]{:T(128)}, bf16[4,256,256]{1,2,0:T(8,128)(2,1)}, f32[4,768,256]{1,2,0:T(8,128)}, f32[4,768,256]{1,2,0:T(8,128)}, s32[4]{0:T(128)S(1)}, /*index...) while((s32[]{:T(128)}, bf16[4,256,256]{1,2,0:T(8,128)(2,1)}, ...), condition=%wide.region_11.12_spmd.clone, body=%wide.region_7.11_spmd.clone.sunk | while | flops 519049472 | bytes 31214816 | solution.py:125
  252.2 2.3 fusion.105
  254.5 2.9 fusion.106
  257.4 10.5 %fusion.107 = bf16[4,64,256]{2,1,0:T(8,128)(2,1)S(1)} fusion(bf16[768,4,64]{0,2,1:T(8,128)(2,1)S(1)} %bitcast.128, f32[4,256,768]{2,1,0:T(8,128)} %fusion.105, f32[4,256,768]{2,1,0:T(8,128)} %get-tuple-element.346, f32[4,256]{1,0:T(4,128)S(1)} %get-tuple-element.347), kind=kOutput, calls=%fused_computation.28.clone.1 | convolution fusion | flops 106170112 | bytes 6819840 | tf_op jit(solution)/shard_map/while/body/eval_jaxpr/gtk,kgd->tgd/dot_general | solution.py:114
  267.8 9.8 %fusion.109 = f32[4,64,768]{2,1,0:T(8,128)S(1)} fusion(bf16[256,4,64]{0,2,1:T(8,128)(2,1)S(1)} %bitcast.136, f32[4,256,768]{2,1,0:T(8,128)} %fusion.105, f32[4,256,768]{2,1,0:T(8,128)} %get-tuple-element.346, f32[4,256]{1,0:T(4,128)S(1)} %get-tuple-element.347), kind=kOutput, calls=%fused_computation.27.clone.1 | convolution fusion | flops 106170112 | bytes 7213056 | tf_op jit(solution)/shard_map/while/body/eval_jaxpr/gtk,tgd->kgd/dot_general | solution.py:117
  277.7 2.4 fusion.108
  280.8 1.3 constant_dynamic-update-slice_fusion.13
  287.5 2.3 fusion.105
  289.8 2.9 fusion.106
  292.6 10.4 %fusion.107 = bf16[4,64,256]{2,1,0:T(8,128)(2,1)S(1)} fusion(bf16[768,4,64]{0,2,1:T(8,128)(2,1)S(1)} %bitcast.128, f32[4,256,768]{2,1,0:T(8,128)} %fusion.105, f32[4,256,768]{2,1,0:T(8,128)} %get-tuple-element.346, f32[4,256]{1,0:T(4,128)S(1)} %get-tuple-element.347), kind=kOutput, calls=%fused_computation.28.clone.1 | convolution fusion | flops 106170112 | bytes 6819840 | tf_op jit(solution)/shard_map/while/body/eval_jaxpr/gtk,kgd->tgd/dot_general | solution.py:114
  303.1 9.8 %fusion.109 = f32[4,64,768]{2,1,0:T(8,128)S(1)} fusion(bf16[256,4,64]{0,2,1:T(8,128)(2,1)S(1)} %bitcast.136, f32[4,256,768]{2,1,0:T(8,128)} %fusion.105, f32[4,256,768]{2,1,0:T(8,128)} %get-tuple-element.346, f32[4,256]{1,0:T(4,128)S(1)} %get-tuple-element.347), kind=kOutput, calls=%fused_computation.27.clone.1 | convolution fusion | flops 106170112 | bytes 7213056 | tf_op jit(solution)/shard_map/while/body/eval_jaxpr/gtk,tgd->kgd/dot_general | solution.py:117
  312.9 2.4 fusion.108
  316.0 1.3 constant_dynamic-update-slice_fusion.13
  322.8 2.3 fusion.105
  325.1 2.9 fusion.106
  328.0 10.5 %fusion.107 = bf16[4,64,256]{2,1,0:T(8,128)(2,1)S(1)} fusion(bf16[768,4,64]{0,2,1:T(8,128)(2,1)S(1)} %bitcast.128, f32[4,256,768]{2,1,0:T(8,128)} %fusion.105, f32[4,256,768]{2,1,0:T(8,128)} %get-tuple-element.346, f32[4,256]{1,0:T(4,128)S(1)} %get-tuple-element.347), kind=kOutput, calls=%fused_computation.28.clone.1 | convolution fusion | flops 106170112 | bytes 6819840 | tf_op jit(solution)/shard_map/while/body/eval_jaxpr/gtk,kgd->tgd/dot_general | solution.py:114
  338.4 9.8 %fusion.109 = f32[4,64,768]{2,1,0:T(8,128)S(1)} fusion(bf16[256,4,64]{0,2,1:T(8,128)(2,1)S(1)} %bitcast.136, f32[4,256,768]{2,1,0:T(8,128)} %fusion.105, f32[4,256,768]{2,1,0:T(8,128)} %get-tuple-element.346, f32[4,256]{1,0:T(4,128)S(1)} %get-tuple-element.347), kind=kOutput, calls=%fused_computation.27.clone.1 | convolution fusion | flops 106170112 | bytes 7213056 | tf_op jit(solution)/shard_map/while/body/eval_jaxpr/gtk,tgd->kgd/dot_general | solution.py:117
  348.3 2.4 fusion.108
  351.4 1.3 constant_dynamic-update-slice_fusion.13
  358.2 2.3 fusion.105
  360.4 2.9 fusion.106
  363.3 10.5 %fusion.107 = bf16[4,64,256]{2,1,0:T(8,128)(2,1)S(1)} fusion(bf16[768,4,64]{0,2,1:T(8,128)(2,1)S(1)} %bitcast.128, f32[4,256,768]{2,1,0:T(8,128)} %fusion.105, f32[4,256,768]{2,1,0:T(8,128)} %get-tuple-element.346, f32[4,256]{1,0:T(4,128)S(1)} %get-tuple-element.347), kind=kOutput, calls=%fused_computation.28.clone.1 | convolution fusion | flops 106170112 | bytes 6819840 | tf_op jit(solution)/shard_map/while/body/eval_jaxpr/gtk,kgd->tgd/dot_general | solution.py:114
  373.7 9.8 %fusion.109 = f32[4,64,768]{2,1,0:T(8,128)S(1)} fusion(bf16[256,4,64]{0,2,1:T(8,128)(2,1)S(1)} %bitcast.136, f32[4,256,768]{2,1,0:T(8,128)} %fusion.105, f32[4,256,768]{2,1,0:T(8,128)} %get-tuple-element.346, f32[4,256]{1,0:T(4,128)S(1)} %get-tuple-element.347), kind=kOutput, calls=%fused_computation.27.clone.1 | convolution fusion | flops 106170112 | bytes 7213056 | tf_op jit(solution)/shard_map/while/body/eval_jaxpr/gtk,tgd->kgd/dot_general | solution.py:117
  383.6 2.4 fusion.108
  386.7 1.3 constant_dynamic-update-slice_fusion.13
  387.9 4.9 copy.27
  392.9 5.2 stack_reshape.7
  398.1 4.9 copy.26
  403.0 5.3 stack_reshape.6
  408.2 2.4 constant_dynamic-update-slice_fusion.7
  411.3 6.3 select_reduce_fusion.2
  417.9 35.3 %while.26 = (s32[]{:T(128)}, bf16[4,256,256]{1,2,0:T(8,128)(2,1)S(1)}, s32[4]{0:T(128)S(1)}, bf16[768,1024]{0,1:T(8,128)(2,1)}, bf16[256,1024]{0,1:T(8,128)(2,1)...) while((s32[]{:T(128)}, ...), condition=%wide.region_6.7_spmd.clone, body=%wide.region_3.6_spmd.clone.sunk | while | flops 206045952 | bytes 9448638 | solution.py:94
  421.3 2.8 fusion.93
  424.1 2.6 fusion.94
  430.2 2.8 fusion.93
  432.9 2.6 fusion.94
  437.8 1.2 constant_dynamic-slice_fusion.13
  439.0 2.8 fusion.93
  441.8 2.6 fusion.94
  447.8 2.8 fusion.93
  450.6 2.6 fusion.94
  453.2 3.7 fusion.42
  457.0 4.3 collective-permute-start.2
  461.3 3.0 collective-permute-start.3
  465.3 1.5 fusion.41
  466.8 140.4 %all-reduce.6.cloned.1.call-done = f32[2,256,1024]{2,1,0:T(8,128)} async-done(((f32[2,256,1024]{2,1,0:T(8,128)}), f32[2,256,1024]{2,1,0:T(8,128)}) %all-reduce.6.cloned.1.call-update) | async-done | bytes 2097168 | tf_op jit(solution)/shard_map/psum | solution.py:138
  607.2 3.9 add_convert_fusion
  611.1 139.9 %reduce-scatter.2.cloned.1.call-done = f32[16,1024]{1,0:T(8,128)} async-done(((f32[1024,1024]{1,0:T(8,128)}), f32[16,1024]{1,0:T(8,128)}) %reduce-scatter.2.cloned.1.call-update) | async-done | bytes 65552 | tf_op jit(solution)/shard_map/reduce_scatter | solution.py:140
  752.1 48.5 %all-reduce.8.cloned.1.call-done = f32[16,1024]{1,0:T(8,128)} async-done(((f32[16,1024]{1,0:T(8,128)}), f32[16,1024]{1,0:T(8,128)}) %all-reduce.8.cloned.1.call-update) | async-done | bytes 65552 | tf_op jit(solution)/shard_map/psum | solution.py:148
  800.6 1.5 copy.60
  (95 shorter events, 39.1 us)
Async XLA Ops:
  7.2 44.2 %copy-start = (bf16[1024,1024]{1,0:T(8,128)(2,1)S(1)}, bf16[1024,1024]{1,0:T(8,128)(2,1)}, u32[]{:S(2)}) copy-start(bf16[1024,1024]{1,0:T(8,128)(2,1)} %param.15) | copy-start | bytes 6291460
  7.2 42.8 %copy-start.3 = (s32[1,3]{1,0:T(1,128)S(1)}, s32[1,3]{1,0:T(1,128)}, u32[]{:S(2)}) copy-start(s32[1,3]{1,0:T(1,128)} %param.16) | copy-start | bytes 40
  7.2 220.7 %all-reduce.4.cloned.1.call-start = ((), (), s32[]{:S(2)}) async-start(), calls=%async_computation.1 | async-start | bytes 2097152 | tf_op jit(solution)/shard_map/psum | solution.py:28
  9.5 218.4 %collective-permute-start.1 = (bf16[2,256,1024]{2,1,0:T(8,128)(2,1)S(1)}, bf16[2,256,1024]{2,1,0:T(8,128)(2,1)}, u32[]{:S(2)}, u32[]{:S(2)}) collective-permute-start(bf16[2,256,1024]{2,1,0:T(8,128)(2,1)S(1)} %constant_dynamic-update-slice_fusion.4), channel_id=1, source_target_pairs={{1,0},{2,1},{3,2},{4,3},{5,4},{6,5},{7,6},{8,7},{9,8},{10,9},{11,1... | collective-permute-start | bytes 3145736 | tf_op jit(solution)/shard_map/ppermute | solution.py:19
  16.6 211.2 %collective-permute-start = (bf16[2,256,1024]{2,1,0:T(8,128)(2,1)S(1)}, bf16[2,256,1024]{2,1,0:T(8,128)(2,1)}, u32[]{:S(2)}, u32[]{:S(2)}) collective-permute-start(bf16[2,256,1024]{2,1,0:T(8,128)(2,1)S(1)} %constant_dynamic-update-slice_fusion.4), channel_id=1, source_target_pairs={{0,1},{1,2},{2,3},{3,4},{4,5},{5,6},{6,7},{7,8},{8,9},{9,10},{10,1... | collective-permute-start | bytes 3145736 | tf_op jit(solution)/shard_map/ppermute | solution.py:17
  47.9 559.4 %all-reduce.6.cloned.1.call-start = ((), (), s32[]{:S(2)}) async-start(), calls=%async_computation.2 | async-start | bytes 4194304 | tf_op jit(solution)/shard_map/psum | solution.py:138
  408.2 2.8 copy-start.1
  417.6 333.4 %reduce-scatter.2.cloned.1.call-start = ((), (), s32[]{:S(2)}) async-start(), calls=%async_computation.3 | async-start | bytes 4259840 | tf_op jit(solution)/shard_map/reduce_scatter | solution.py:140
  456.9 7.4 copy-start.2
  456.9 343.7 %all-reduce.8.cloned.1.call-start = ((), (), s32[]{:S(2)}) async-start(), calls=%async_computation.4 | async-start | bytes 131072 | tf_op jit(solution)/shard_map/psum | solution.py:148
  457.0 150.3 %collective-permute-start.2 = (f32[2,256,1024]{2,1,0:T(8,128)}, f32[2,256,1024]{2,1,0:T(8,128)}, u32[]{:S(2)}, u32[]{:S(2)}) collective-permute-start(f32[2,256,1024]{2,1,0:T(8,128)} %get-tuple-element.174), channel_id=1, source_target_pairs={{1,0},{2,1},{3,2},{4,3},{5,4},{6,5},{7,6},{8,7},{9,8},{10,9},{11,1... | collective-permute-start | bytes 6291464 | tf_op jit(solution)/shard_map/ppermute | solution.py:34
  461.3 146.0 %collective-permute-start.3 = (f32[2,256,1024]{2,1,0:T(8,128)}, f32[2,256,1024]{2,1,0:T(8,128)}, u32[]{:S(2)}, u32[]{:S(2)}) collective-permute-start(f32[2,256,1024]{2,1,0:T(8,128)} %get-tuple-element.176), channel_id=1, source_target_pairs={{0,1},{1,2},{2,3},{3,4},{4,5},{5,6},{6,7},{7,8},{8,9},{9,10},{10,1... | collective-permute-start | bytes 6291464 | tf_op jit(solution)/shard_map/ppermute | solution.py:34
Sparse Core Ops, SparseCore 0:
  48.0 179.8 all-reduce.3
  417.7 189.4 all-reduce.5
  611.9 139.0 reduce-scatter.1
  753.2 47.3 all-reduce.7
where the time goes:
time: 812 us; the launch traced here: 809 us
  waiting for transfers between devices  503 us (62%)
  matrix products  140 us (17%)
  local copies, waits for them, and re-layouts  82.3 us (10%)
  blocking collectives  27.6 us (3%)
  other arithmetic  19.7 us (2%)
  between operations  15.3 us (2%)
  starting transfers between devices  14.7 us (2%)
    psum x1, waiting for transfers between devices, from_root(): return lax.psum(kept, axis)  174 us
    psum x1, waiting for transfers between devices, on_device(): far_total = lax.psum(far_grad, 'region')  140 us
    reduce_scatter x1, waiting for transfers between devices, on_device(): lax.psum_scatter(lax.dot_general(attn, grad_out, (((0,), (0,)), ((), ()))...  140 us
    psum x1, waiting for transfers between devices, on_device(): d_weight = lax.psum(rows_part, 'dp')  48.5 us
    dot_general x4, matrix products, backward_block(): jnp.einsum('gtk,kgd->tgd', dscore, key_part, preferred_element_type=jnp.f...  41.8 us
    dot_general x4, matrix products, backward_block(): jnp.einsum('gtk,tgd->kgd', dscore, query_part, preferred_element_type=jnp...  39.3 us
    pmax x1, blocking collectives, on_device(): far_id = lax.pmax(far_local, 'region')  27.6 us
    dynamic_slice x28, local copies, waits for them, and re-layouts, columns(): return lax.dynamic_slice_in_dim(matrix, start, span, 1)  24.3 us
  transfers between devices with their start and end apart: 8, of which 4 were waited for; matrix products, arithmetic and copies ran while one was open for 6% of the time, Pallas kernels for 0%

commit v1 on v0

v1 whole, which is shorter than its diff:
```python
import functools
import jax
import jax.numpy as jnp
from jax import lax
from jax.experimental import pallas as pl
from jax.experimental.pallas import tpu as pltpu
from jax.sharding import PartitionSpec as P

HEAD_DIM = 64
SPAN = 256
F32 = jnp.float32
BF16 = jnp.bfloat16


def nt(a, b):
    return lax.dot_general(a, b, (((1,), (1,)), ((), ())), preferred_element_type=F32)


def tn(a, b):
    return lax.dot_general(a, b, (((0,), (0,)), ((), ())), preferred_element_type=F32)


def nn(a, b):
    return lax.dot_general(a, b, (((1,), (0,)), ((), ())), preferred_element_type=F32)


def half_masks(shape):
    lane = lax.broadcasted_iota(jnp.int32, shape, 1)
    return [lane < HEAD_DIM, lane >= HEAD_DIM]


def local_forward(flags, q, ko, kl, kr, vo, vl, vr, m_out, l_out, o_out):
    seen = [None, flags[0] > 0, flags[1] > 0]
    for g in range(SPAN // 128):
        cols = pl.ds(g * 128, 128)
        queries = q[:, cols] * 0.125
        masks = half_masks(queries.shape)
        keys = [ref[:, cols] for ref in (ko, kl, kr)]
        vals = [ref[:, cols] for ref in (vo, vl, vr)]
        tops, sums, mixes = [], [], []
        for mask in masks:
            part = jnp.where(mask, queries, 0).astype(BF16)
            scores = [nt(part, k) for k in keys]
            scores = [s if f is None else jnp.where(f, s, -1e30) for s, f in zip(scores, seen)]
            top = jnp.max(functools.reduce(jnp.maximum, scores), axis=1, keepdims=True)
            weights = [jnp.exp(s - top) for s in scores]
            sums.append(jnp.sum(weights[0] + weights[1] + weights[2], axis=1, keepdims=True))
            tops.append(top)
            mixes.append(sum(nn(w.astype(BF16), v) for w, v in zip(weights, vals)))
        m_out[:, cols] = jnp.where(masks[0], tops[0], tops[1])
        l_out[:, cols] = jnp.where(masks[0], sums[0], sums[1])
        o_out[:, cols] = jnp.where(masks[0], mixes[0], mixes[1])


def hub_block(flags, q, d, half, rest, m_in, l_in, o_in, attn_out, lse_out, cen_out, dq_out, mine_out, other_out):
    first = flags[2] == 0
    seen = flags[3] > 0
    for g in range(SPAN // 128):
        cols = pl.ds(g * 128, 128)
        queries = q[:, cols] * 0.125
        grads = d[:, cols]
        masks = half_masks(queries.shape)
        a, b = half[:, cols], rest[:, cols]
        key = jnp.where(first, a, b)
        val = jnp.where(first, b, a)
        m_loc, l_loc, o_loc = m_in[:, cols], l_in[:, cols], o_in[:, cols]
        lses, cens, mixes, dqs = [], [], [], []
        dk = dv = 0.0
        for h, mask in enumerate(masks):
            part = jnp.where(mask, queries, 0).astype(BF16)
            gpart = jnp.where(mask, grads, 0).astype(BF16)
            at = slice(h * HEAD_DIM, h * HEAD_DIM + 1)
            scores = jnp.where(seen, nt(part, key), -1e30)
            old = m_loc[:, at]
            top = jnp.maximum(old, jnp.max(scores, axis=1, keepdims=True))
            weights = jnp.exp(scores - top)
            fade = jnp.exp(old - top)
            total = l_loc[:, at] * fade + jnp.sum(weights, axis=1, keepdims=True)
            inv = 1.0 / total
            mix = (o_loc * fade + nn(weights.astype(BF16), val)) * inv
            cen = jnp.sum(jnp.where(mask, mix * grads.astype(F32), 0.0), axis=1, keepdims=True)
            probs = weights * inv
            dscore = (probs * (nt(gpart, val) - cen)).astype(BF16)
            dqs.append(nn(dscore, key))
            dk += tn(dscore, part)
            dv += tn(probs.astype(BF16), gpart)
            lses.append(top + jnp.log(total))
            cens.append(cen)
            mixes.append(mix)
        attn_out[:, cols] = jnp.where(masks[0], mixes[0], mixes[1]).astype(BF16)
        lse_out[:, cols] = jnp.where(masks[0], lses[0], lses[1])
        cen_out[:, cols] = jnp.where(masks[0], cens[0], cens[1])
        dq_out[:, cols] = jnp.where(masks[0], dqs[0], dqs[1])
        mine_out[:, cols] = jnp.where(first, dk, dv).astype(BF16)
        other_out[:, cols] = jnp.where(first, dv, dk).astype(BF16)


def local_backward(flags, q, d, ko, kl, kr, vo, vl, vr, lse_in, cen_in, dq_in, dq_out, own_out, left_out, right_out):
    seen = [None, flags[0] > 0, flags[1] > 0]
    for g in range(SPAN // 128):
        cols = pl.ds(g * 128, 128)
        queries = q[:, cols] * 0.125
        grads = d[:, cols]
        masks = half_masks(queries.shape)
        keys = [ref[:, cols] for ref in (ko, kl, kr)]
        vals = [ref[:, cols] for ref in (vo, vl, vr)]
        lse, cens = lse_in[:, cols], cen_in[:, cols]
        parts = [jnp.where(m, queries, 0).astype(BF16) for m in masks]
        gparts = [jnp.where(m, grads, 0).astype(BF16) for m in masks]
        dq = [0.0, 0.0]
        for key, val, flag, out in zip(keys, vals, seen, (own_out, left_out, right_out)):
            dk = dv = 0.0
            for h in range(2):
                at = slice(h * HEAD_DIM, h * HEAD_DIM + 1)
                scores = nt(parts[h], key)
                if flag is not None:
                    scores = jnp.where(flag, scores, -1e30)
                probs = jnp.exp(scores - lse[:, at])
                dscore = (probs * (nt(gparts[h], val) - cens[:, at])).astype(BF16)
                dq[h] += nn(dscore, key)
                dk += tn(dscore, parts[h])
                dv += tn(probs.astype(BF16), gparts[h])
            out[0, :, cols] = dk.astype(out.dtype)
            out[1, :, cols] = dv.astype(out.dtype)
        total = jnp.where(masks[0], dq[0], dq[1]) + dq_in[:, cols]
        dq_out[:, cols] = (total * 0.125).astype(BF16)


def call(body, ins, outs, flops, name, start=0, count=None):
    width = ins[1].shape[-1]
    steps = width // SPAN if count is None else count

    def spec(shape, shift):
        if len(shape) == 3:
            return pl.BlockSpec((shape[0], shape[1], SPAN), lambda i: (0, 0, i + shift))
        return pl.BlockSpec((shape[0], SPAN), lambda i: (0, i + shift))

    in_specs = [pl.BlockSpec(memory_space=pltpu.SMEM)]
    in_specs += [spec(a.shape, start if a.shape[-1] == width else 0) for a in ins[1:]]
    out_shapes = [jax.ShapeDtypeStruct(tuple(s[:-1]) + (steps * SPAN,), t) for s, t in outs]
    moved = sum(a.size * a.dtype.itemsize for a in ins[1:]) + sum(
        s.size * s.dtype.itemsize for s in out_shapes
    )
    return pl.pallas_call(
        body,
        grid=(steps,),
        in_specs=in_specs,
        out_specs=[spec(s.shape, 0) for s in out_shapes],
        out_shape=out_shapes,
        compiler_params=pltpu.CompilerParams(vmem_limit_bytes=40 * 1024 * 1024),
        cost_estimate=pl.CostEstimate(flops=flops, bytes_accessed=moved, transcendentals=0),
        name=name,
    )(*ins)


NZ, NX, NC = 8, 4, 2


def place(z, x, c):
    return (z % NZ) * NX * NC + (x % NX) * NC + c % NC


def spots():
    return [(z, x, c) for z in range(NZ) for x in range(NX) for c in range(NC)]


def hop(dz=0, dx=0, dc=0):
    return [(place(z, x, c), place(z + dz, x + dx, c + dc)) for z, x, c in spots()]


Z_GROUPS = [[place(z, x, c) for z in range(NZ)] for x in range(NX) for c in range(NC)]


def send(value, pairs):
    return lax.ppermute(value, "region", pairs)


def pick(value, index):
    return lax.dynamic_index_in_dim(value, index, 0, keepdims=False)


def swap_z(value):
    return lax.all_to_all(value, "region", 0, 0, axis_index_groups=Z_GROUPS, tiled=True)


def swap_x(value, x):
    return [pick(value, x)] + [send(pick(value, (x + k) % NX), hop(dx=k)) for k in range(1, NX)]


def gather_x(value, x):
    got = jnp.stack([value] + [send(value, hop(dx=k)) for k in range(1, NX)])
    return jnp.concatenate([pick(got, (x - j) % NX) for j in range(NX)])


def gather_z(value):
    return swap_z(jnp.broadcast_to(value[None], (NZ,) + value.shape))


def shifted(value, step):
    last = NZ * NX * NC
    return send(value, [(i, i + step) for i in range(last) if 0 <= i + step < last])


def on_device(query, key_in, value, d_out, out_weight, attended, counts):
    region = lax.axis_index("region")
    z, x, c = region // (NX * NC), (region // NC) % NX, region % NC
    first = c == 0
    query, key, value, grad_out = query[0], key_in[0], value[0], d_out[0]
    rows, width = query.shape
    listed = attended[0, 1:]
    used = jnp.arange(1, attended.shape[1]) < counts[0]
    left_seen = jnp.any(used & (listed == region - 1))
    right_seen = jnp.any(used & (listed == region + 1))
    far = used & (listed != region - 1) & (listed != region + 1)
    far_local = jnp.max(jnp.where(far, listed, -1))
    flags = jnp.stack([left_seen, right_seen, c, jnp.any(far)]).astype(jnp.int32)

    mine = jnp.where(first, key, value)
    other = jnp.where(first, value, key)
    theirs = send(other, hop(dc=1))
    ids = lax.all_to_all(
        jnp.full((NZ * NX * NC, 1, 128), far_local, jnp.int32), "region", 0, 0, tiled=True
    )
    quarter = rows // NX
    both = jnp.stack(
        [mine.reshape(NX, quarter, width), theirs.reshape(NX, quarter, width)], axis=1
    )
    arrived = jnp.stack(swap_x(both, x))
    hub = jnp.max(ids)
    hub_z, hub_x, hub_c = hub // (NX * NC), (hub // NC) % NX, hub % NC
    picked = pick(arrived, (x - hub_x) % NX)
    piece = jnp.where(hub_c == c, picked[0], picked[1])
    share = pick(swap_z(piece.reshape(NZ, quarter // NZ, width)), hub_z)
    half = gather_x(gather_z(share).reshape(quarter, width), x)
    rest = send(half, hop(dc=1))

    pair = jnp.stack([key, value])
    from_left = shifted(pair, 1)
    from_right = shifted(pair, -1)
    d_attn = lax.dot_general(
        grad_out, out_weight, (((1,), (1,)), ((), ())), preferred_element_type=F32
    ).astype(BF16)

    blocks = [key, from_left[0], from_right[0], value, from_left[1], from_right[1]]
    flat = (rows, width)
    stats = call(
        local_forward, [flags, query, *blocks], [(flat, F32)] * 3, int(1.6e9), "local_forward"
    )
    attn, lse, cen, dq_far, far_mine, far_other = call(
        hub_block,
        [flags, query, d_attn, half, rest, *stats],
        [(flat, BF16), (flat, F32), (flat, F32), (flat, F32), (flat, BF16), (flat, BF16)],
        int(2e9),
        "hub_block",
    )

    summed = (far_mine.astype(F32) + send(far_other, hop(dc=1)).astype(F32)).astype(BF16)
    parts = swap_x(summed.reshape(NX, quarter, width), x)
    summed = sum(p.astype(F32) for p in parts).astype(BF16)
    parts = swap_z(summed.reshape(NZ, quarter // NZ, width))
    total = jnp.sum(parts.astype(F32), axis=0).astype(BF16)
    far_half = gather_x(gather_z(total).reshape(quarter, width), x)
    far_rest = send(far_half, hop(dc=1))

    double = (2,) + flat
    d_query, own, to_left, to_right = call(
        local_backward,
        [flags, query, d_attn, *blocks, lse, cen, dq_far],
        [(flat, BF16), (double, F32), (double, BF16), (double, BF16)],
        int(4e9),
        "local_backward",
    )
    own = own + shifted(to_left, -1).astype(F32) + shifted(to_right, 1).astype(F32)
    at_hub = region == hub
    far_key = jnp.where(first, far_half, far_rest).astype(F32)
    far_value = jnp.where(first, far_rest, far_half).astype(F32)
    d_key = (own[0] + jnp.where(at_hub, far_key, 0.0)).astype(BF16)
    d_value = (own[1] + jnp.where(at_hub, far_value, 0.0)).astype(BF16)

    slab = width // (NZ * NX * NC)
    partial = tn(attn, grad_out).reshape(NZ, NX, NC, slab, width)
    kept = jnp.where(first, partial[:, :, 0], partial[:, :, 1])
    sent = jnp.where(first, partial[:, :, 1], partial[:, :, 0])
    turned = send(sent.astype(BF16), hop(dc=1))
    weight = (kept + turned.astype(F32)).astype(BF16).transpose(1, 0, 2, 3)
    weight = sum(p.astype(F32) for p in swap_x(weight, x)).astype(BF16)
    weight = jnp.sum(swap_z(weight).astype(F32), axis=0)
    dp = lax.axis_size("dp")
    d_weight = weight
    for k in range(1, dp):
        d_weight = d_weight + lax.ppermute(weight, "dp", [(i, (i + k) % dp) for i in range(dp)])

    layer = nn(attn, out_weight).astype(BF16)
    return layer[None], d_query[None], d_key[None], d_value[None], d_weight


def solution(mesh):
    rows = P("dp", "region", None)
    return jax.shard_map(
        on_device,
        mesh=mesh,
        in_specs=(rows, rows, rows, rows, P(), P("region", None), P("region")),
        out_specs=(rows, rows, rows, rows, P("region", None)),
        check_vma=False,
    )
```

time: 812 us -> 234 us (0.29)
  waiting for transfers between devices: 503 us -> 41.8 us
  matrix products: 140 us -> 5.99 us
  local copies, waits for them, and re-layouts: 82.3 us -> 26.3 us
  starting transfers between devices: 14.7 us -> 66.9 us
  Pallas kernels: 0 us -> 36.3 us
  between operations: 15.3 us -> 6.92 us
    psum x3 -> x0, waiting for transfers between devices: 363 us -> none  [the longest x1 174 us: from_root(): return lax.psum(kept, axis)]
    reduce_scatter x1 -> x0, waiting for transfers between devices: 140 us -> none  [on_device(): lax.psum_scatter(lax.dot_general(attn, grad_out, (((0,), (0,)), ((), ()))...]
    dot_general x22 -> x2, matrix products: 115 us -> 3.41 us  [the longest x1 1.91 us: tn(): lax.dot_general(a, b, (((0,), (0,)), ((), ())), preferred_element_type=F32)]
    pallas_call x0 -> x3, Pallas kernels: none -> 36.3 us  [call(): pl.pallas_call(body, grid=(steps,), in_specs=in_specs, out_specs=[spec(s....]
    ppermute x4 -> x27, starting transfers between devices: 14.4 us -> 45.2 us  [the longest x24 41.3 us: send(): return lax.ppermute(value, 'region', pairs)]
    dynamic_slice x36 -> x0, local copies, waits for them, and re-layouts: 29.3 us -> none  [the longest x28 24.3 us: columns(): return lax.dynamic_slice_in_dim(matrix, start, span, 1)]
    pmax x1 -> x0, blocking collectives: 27.6 us -> none  [on_device(): far_id = lax.pmax(far_local, 'region')]
    ppermute x4 -> x27, waiting for transfers between devices: 0.01 us -> 24.2 us  [the longest x24 22.9 us: send(): return lax.ppermute(value, 'region', pairs)]
  transfers between devices with their start and end apart: 8 -> 32, of which waited for: 4 -> 17; matrix products, arithmetic and copies ran while one was open for 6% -> 14% of each run, Pallas kernels for 0% -> 11%
where the time goes in v1:
time: 234 us; the launch traced here: 231 us
  starting transfers between devices  66.9 us (29%)
  waiting for transfers between devices  41.8 us (18%)
  Pallas kernels  36.3 us (16%)
  local copies, waits for them, and re-layouts  26.3 us (11%)
  other arithmetic  26.3 us (11%)
  blocking collectives  20.7 us (9%)
  between operations  6.92 us (3%)
  matrix products  5.99 us (3%)
    ppermute x24, starting transfers between devices, send(): return lax.ppermute(value, 'region', pairs)  41.3 us
    pallas_call x3, Pallas kernels, call(): pl.pallas_call(body, grid=(steps,), in_specs=in_specs, out_specs=[spec(s....  36.3 us
    ppermute x24, waiting for transfers between devices, send(): return lax.ppermute(value, 'region', pairs)  22.9 us
    all_to_all x5, starting transfers between devices, swap_z(): lax.all_to_all(value, 'region', 0, 0, axis_index_groups=Z_GROUPS, tiled=T...  21.7 us
    all_to_all x1, blocking collectives, on_device(): lax.all_to_all(jnp.full((NZ * NX * NC, 1, 128), far_local, jnp.int32), 'r...  20.7 us
    unnamed x67, local copies, waits for them, and re-layouts  18.4 us
    all_to_all x5, waiting for transfers between devices, swap_z(): lax.all_to_all(value, 'region', 0, 0, axis_index_groups=Z_GROUPS, tiled=T...  17.6 us
  transfers between devices with their start and end apart: 32, of which 17 were waited for; matrix products, arithmetic and copies ran while one was open for 14% of the time, Pallas kernels for 11%

profile of v1, /device:TPU:1, one launch (start us, length us, event | category | flops | bytes accessed | tf_op | source)
XLA Modules:
  0.0 231.1 jit_solution(2167751818816131048)
XLA Ops:
  0.7 2.2 broadcast_select_fusion
  2.9 3.2 %collective-permute-start = (bf16[256,1024]{1,0:T(8,128)(2,1)}, bf16[256,1024]{1,0:T(8,128)(2,1)}, u32[]{:S(2)}, u32[]{:S(2)}) collective-permute-start(bf16[256,1024]{1,0:T(8,128)(2,1)} %broadcast_select_fusion), channel_id=1, source_target_pairs={{0,1},{1,0},{2,3},{3,2},{4,5},{5,4},{6,7},{7,6},{8,9},{9,8},{10,11... | collective-permute-start | bytes 1572872 | tf_op jit(solution)/shard_map/ppermute | solution.py:175
  7.1 0.9 collective-permute-done
  8.0 2.0 fusion.21
  11.5 1.0 collective-permute-start.2
  13.9 20.7 %all_to_all.30 = s32[64,1,128]{2,1,0:T(1,128)S(1)} all-to-all(s32[64,1,128]{2,1,0:T(1,128)S(1)} %broadcast_in_dim.39), channel_id=1, replica_groups=mesh['dp'=4,'region'=64] {'region'}, dimensions={0} | all-to-all | bytes 65536 | tf_op jit(solution)/shard_map/all_to_all | solution.py:221
  37.7 1.2 fusion.19
  39.5 3.4 %all-to-all-start.1 = ((bf16[8,8,1024]{2,1,0:T(8,128)(2,1)}), bf16[8,8,1024]{2,1,0:T(8,128)(2,1)S(1)}, u32[]{:S(2)}, u32[]{:S(2)}) async-start(bf16[8,8,1024]{2,1,0:T(8,128)(2,1)} %fusion.31), calls=%async_computation.1 | async-start | bytes 262144 | tf_op jit(solution)/shard_map/all_to_all | solution.py:183
  42.9 2.6 %collective-permute-start.9 = (bf16[2,256,1024]{2,1,0:T(8,128)(2,1)}, bf16[2,256,1024]{2,1,0:T(8,128)(2,1)}, u32[]{:S(2)}, u32[]{:S(2)}) collective-permute-start(bf16[2,256,1024]{2,1,0:T(8,128)(2,1)} %copy-done.31), channel_id=1, source_target_pairs={{1,0},{2,1},{3,2},{4,3},{5,4},{6,5},{7,6},{8,7},{9,8},{10,9},{11,1... | collective-permute-start | bytes 3145736 | tf_op jit(solution)/shard_map/ppermute | solution.py:175
  45.5 3.0 %collective-permute-start.8 = (bf16[2,256,1024]{2,1,0:T(8,128)(2,1)}, bf16[2,256,1024]{2,1,0:T(8,128)(2,1)}, u32[]{:S(2)}, u32[]{:S(2)}) collective-permute-start(bf16[2,256,1024]{2,1,0:T(8,128)(2,1)} %copy-done.31), channel_id=1, source_target_pairs={{0,1},{1,2},{2,3},{3,4},{4,5},{5,6},{6,7},{7,8},{8,9},{9,10},{10,1... | collective-permute-start | bytes 3145736 | tf_op jit(solution)/shard_map/ppermute | solution.py:175
  48.5 2.1 all-to-all-done.1
  51.3 4.4 %all-to-all-start.2 = ((bf16[8,8,1024]{2,1,0:T(8,128)(2,1)}), bf16[8,8,1024]{2,1,0:T(8,128)(2,1)S(1)}, u32[]{:S(2)}, u32[]{:S(2)}) async-start(bf16[8,8,1024]{2,1,0:T(8,128)(2,1)} %broadcast_in_dim.41), calls=%async_computation.2 | async-start | bytes 262144 | tf_op jit(solution)/shard_map/all_to_all | solution.py:183
  55.8 2.6 %convolution_convert_fusion.1.d = bf16[256,1024]{1,0:T(8,128)(2,1)} fusion(bf16[1024,1024]{1,0:T(8,128)(2,1)S(1)} %copy-done, bf16[1,256,1024]{2,1,0:T(8,128)(2,1)} %param.10), kind=kOutput, calls=%fused_computation.15 | convolution fusion | flops 537133056 | bytes 3145728 | tf_op jit(solution)/shard_map/dot_general | solution.py:240
  58.4 5.2 %all-to-all-done.2 = bf16[8,8,1024]{2,1,0:T(8,128)(2,1)S(1)} async-done(((bf16[8,8,1024]{2,1,0:T(8,128)(2,1)}), bf16[8,8,1024]{2,1,0:T(8,128)(2,1)S(1)}, u32[]{:S(2)}, u32[]{:S(2)}) %all-to-all-start.2) | async-done | bytes 131104 | tf_op jit(solution)/shard_map/all_to_all | solution.py:183
  63.5 7.8 %collective-permute-start.6 = (bf16[64,1024]{1,0:T(8,128)(2,1)S(1)}, bf16[64,1024]{1,0:T(8,128)(2,1)S(1)}, u32[]{:S(2)}, u32[]{:S(2)}) collective-permute-start(bf16[64,1024]{1,0:T(8,128)(2,1)S(1)} %bitcast.165), channel_id=1, source_target_pairs={{0,6},{1,7},{2,0},{3,1},{4,2},{5,3},{6,4},{7,5},{8,14},{9,15},{10,... | collective-permute-start | bytes 393224 | tf_op jit(solution)/shard_map/ppermute | solution.py:175
  75.3 1.4 collective-permute-done.5
  76.8 1.1 collective-permute-done.4
  77.9 1.0 pad_maximum_fusion
  79.3 1.3 slice_bitcast_fusion.2
  80.6 1.6 slice_bitcast_fusion.3
  82.3 8.3 %local_forward.1 = (f32[256,1024]{1,0:T(8,128)S(1)}, f32[256,1024]{1,0:T(8,128)S(1)}, f32[256,1024]{1,0:T(8,128)S(1)}) custom-call(s32[4]{0:T(128)S(1)} %pad_add_fusion.flags, bf16[256,1024]{1,0:T(8,128)(2,1)S(1)} %bitcast.158, bf16[256,1024]{1,0:T(8,128)(2,1)S(1)} %bitcast.153, bf16[256,1024]{1,0:T(8,128)(2,1)S(1)} %get-tuple-element.43.kl, ...), custom_call_target="tpu_custom_call" | custom-call | flops 1600000000 | bytes 6815744 | tf_op jit(solution)/shard_map/local_forward/pallas_call | solution.py:144
  90.6 11.9 %hub_block.1 = (bf16[256,1024]{1,0:T(8,128)(2,1)S(1)}, f32[256,1024]{1,0:T(8,128)S(1)}, f32[256,1024]{1,0:T(8,128)S(1)}, f32[256,1024]{1,0:T(8,128)S(1)}, bf16[2...) custom-call(s32[4]{0:T(128)S(1)} %pad_add_fusion.flags, bf16[256,1024]{1,0:T(8,128)(2,1)S(1)} %bitcast.159, ...), custom_call_target="tpu_custom_call" | custom-call | flops 2000000000 | bytes 9961472 | tf_op jit(solution)/shard_map/hub_block/pallas_call | solution.py:144
  105.0 1.0 copy-done.22
  106.0 1.0 copy-done.24
  107.0 1.0 copy-done.26
  108.0 2.0 copy.28
  110.5 1.9 fusion.14
  112.4 1.3 fusion.4
  116.2 2.7 %collective-permute-start.15 = (bf16[64,1024]{1,0:T(8,128)(2,1)}, bf16[64,1024]{1,0:T(8,128)(2,1)S(1)}, u32[]{:S(2)}, u32[]{:S(2)}) collective-permute-start(bf16[64,1024]{1,0:T(8,128)(2,1)} %get-tuple-element.53), channel_id=1, source_target_pairs={{0,6},{1,7},{2,0},{3,1},{4,2},{5,3},{6,4},{7,5},{8,14},{9,15},{10,... | collective-permute-start | bytes 393224 | tf_op jit(solution)/shard_map/ppermute | solution.py:175
  119.5 3.2 %collective-permute-done.13 = bf16[64,1024]{1,0:T(8,128)(2,1)S(1)} collective-permute-done((bf16[64,1024]{1,0:T(8,128)(2,1)}, bf16[64,1024]{1,0:T(8,128)(2,1)S(1)}, u32[]{:S(2)}, u32[]{:S(2)}) %collective-permute-start.13) | collective-permute-done | bytes 131104 | tf_op jit(solution)/shard_map/ppermute | solution.py:175
  122.7 1.7 collective-permute-done.15
  125.0 1.7 fusion.30
  126.7 3.6 %all-to-all-start.3 = ((bf16[8,8,1024]{2,1,0:T(8,128)(2,1)}), bf16[8,8,1024]{2,1,0:T(8,128)(2,1)S(1)}, u32[]{:S(2)}, u32[]{:S(2)}) async-start(bf16[8,8,1024]{2,1,0:T(8,128)(2,1)} %fusion.30), calls=%async_computation.3 | async-start | bytes 262144 | tf_op jit(solution)/shard_map/all_to_all | solution.py:183
  130.3 1.0 copy-done.10
  131.3 1.0 copy-done.12
  132.3 1.0 copy-done.14
  133.4 1.0 copy-done.16
  134.4 1.0 copy-done.18
  135.5 1.0 copy-done.21
  136.5 1.2 copy-done.23
  137.7 1.2 copy-done.25
  139.0 1.2 copy-done.27
  140.2 16.1 %local_backward.1 = (bf16[256,1024]{1,0:T(8,128)(2,1)}, f32[2,256,1024]{2,1,0:T(8,128)S(1)}, bf16[2,256,1024]{2,1,0:T(8,128)(2,1)}, bf16[2,256,1024]{2,1,0:T(8,128)(2,1)}) custom-call(s32[4]{0:T(128)S(1)} %pad_add_fusion.flags, bf16[256,1024]{1,0:T(8,128)(2,1)S(1)} %bitcast.160, bf16[256,1024]{1,0:T(8,128)(2,1)S(1)} %copy-done.21, ...), custom_call_target="tpu_custom_call" | custom-call | flops 4000000000 | bytes 12058624 | tf_op jit(solution)/shard_map/local_backward/pallas_call | solution.py:144
  156.3 1.4 copy-done.2
  157.6 3.7 %collective-permute-start.10 = (bf16[2,256,1024]{2,1,0:T(8,128)(2,1)}, bf16[2,256,1024]{2,1,0:T(8,128)(2,1)}, u32[]{:S(2)}, u32[]{:S(2)}) collective-permute-start(bf16[2,256,1024]{2,1,0:T(8,128)(2,1)} %get-tuple-element.27), channel_id=1, source_target_pairs={{1,0},{2,1},{3,2},{4,3},{5,4},{6,5},{7,6},{8,7},{9,8},{10,9},{11,1... | collective-permute-start | bytes 3145736 | tf_op jit(solution)/shard_map/ppermute | solution.py:175
  161.3 2.4 %collective-permute-start.11 = (bf16[2,256,1024]{2,1,0:T(8,128)(2,1)}, bf16[2,256,1024]{2,1,0:T(8,128)(2,1)}, u32[]{:S(2)}, u32[]{:S(2)}) collective-permute-start(bf16[2,256,1024]{2,1,0:T(8,128)(2,1)} %get-tuple-element.28), channel_id=1, source_target_pairs={{0,1},{1,2},{2,3},{3,4},{4,5},{5,6},{6,7},{7,8},{8,9},{9,10},{10,1... | collective-permute-start | bytes 3145736 | tf_op jit(solution)/shard_map/ppermute | solution.py:175
  164.4 6.9 %all-to-all-start.4 = ((bf16[8,8,1024]{2,1,0:T(8,128)(2,1)}), bf16[8,8,1024]{2,1,0:T(8,128)(2,1)S(1)}, u32[]{:S(2)}, u32[]{:S(2)}) async-start(bf16[8,8,1024]{2,1,0:T(8,128)(2,1)} %broadcast_in_dim.44), calls=%async_computation.4 | async-start | bytes 262144 | tf_op jit(solution)/shard_map/all_to_all | solution.py:183
  171.3 3.2 %fusion.2 = bf16[8,4,16,1024]{3,2,1,0:T(8,128)(2,1)S(1)} fusion(bf16[8,4,16,1024]{3,2,1,0:T(8,128)(2,1)} %collective-permute-done.20, f32[8,4,2,16,1024]{4,3,2,1,0:T(8,128)} %copy-done.28, pred[]{:T(512)S(6)} %eq.49), kind=kLoop, calls=%fused_computation.3 | loop fusion | flops 2097152 | bytes 6291457 | tf_op jit(solution)/shard_map/convert_element_type | solution.py:285
  174.5 4.5 %all-to-all-done.4 = bf16[8,8,1024]{2,1,0:T(8,128)(2,1)S(1)} async-done(((bf16[8,8,1024]{2,1,0:T(8,128)(2,1)}), bf16[8,8,1024]{2,1,0:T(8,128)(2,1)S(1)}, u32[]{:S(2)}, u32[]{:S(2)}) %all-to-all-start.4) | async-done | bytes 131104 | tf_op jit(solution)/shard_map/all_to_all | solution.py:183
  179.1 9.2 %collective-permute-start.18 = (bf16[64,1024]{1,0:T(8,128)(2,1)S(1)}, bf16[64,1024]{1,0:T(8,128)(2,1)S(1)}, u32[]{:S(2)}, u32[]{:S(2)}) collective-permute-start(bf16[64,1024]{1,0:T(8,128)(2,1)S(1)} %bitcast.169), channel_id=1, source_target_pairs={{0,6},{1,7},{2,0},{3,1},{4,2},{5,3},{6,4},{7,5},{8,14},{9,15},{10,... | collective-permute-start | bytes 393224 | tf_op jit(solution)/shard_map/ppermute | solution.py:175
  188.9 2.7 %collective-permute-done.18 = bf16[64,1024]{1,0:T(8,128)(2,1)S(1)} collective-permute-done((bf16[64,1024]{1,0:T(8,128)(2,1)S(1)}, bf16[64,1024]{1,0:T(8,128)(2,1)S(1)}, u32[]{:S(2)}, u32[]{:S(2)}) %collective-permute-start.18) | collective-permute-done | bytes 131104 | tf_op jit(solution)/shard_map/ppermute | solution.py:175
  191.6 2.1 collective-permute-done.17
  193.7 1.0 collective-permute-start.23
  194.7 1.3 collective-permute-done.16
  196.0 1.4 collective-permute-start.22
  198.4 3.8 %collective-permute-done.21 = bf16[8,16,1024]{2,1,0:T(8,128)(2,1)S(1)} collective-permute-done((bf16[8,16,1024]{2,1,0:T(8,128)(2,1)S(1)}, bf16[8,16,1024]{2,1,0:T(8,128)(2,1)S(1)}, u32[]{:S(2)}, u32[]{:S(2)}) %collective-permute-start.21) | collective-permute-done | bytes 262176 | tf_op jit(solution)/shard_map/ppermute | solution.py:175
  202.1 4.1 %collective-permute-done.22 = bf16[8,16,1024]{2,1,0:T(8,128)(2,1)S(1)} collective-permute-done((bf16[8,16,1024]{2,1,0:T(8,128)(2,1)S(1)}, bf16[8,16,1024]{2,1,0:T(8,128)(2,1)S(1)}, u32[]{:S(2)}, u32[]{:S(2)}) %collective-permute-start.22) | collective-permute-done | bytes 262176 | tf_op jit(solution)/shard_map/ppermute | solution.py:175
  206.3 1.8 fusion.13
  208.1 3.4 %all-to-all-start.5 = ((bf16[8,16,1024]{2,1,0:T(8,128)(2,1)}), bf16[8,16,1024]{2,1,0:T(8,128)(2,1)S(1)}, u32[]{:S(2)}, u32[]{:S(2)}) async-start(bf16[8,16,1024]{2,1,0:T(8,128)(2,1)} %fusion.13), calls=%async_computation.5 | async-start | bytes 524288 | tf_op jit(solution)/shard_map/all_to_all | solution.py:183
  211.6 1.5 fusion.3
  213.1 3.4 %convert_add_fusion = f32[2,256,1024]{2,1,0:T(8,128)} fusion(bf16[2,256,1024]{2,1,0:T(8,128)(2,1)} %collective-permute-done.11, f32[2,256,1024]{2,1,0:T(8,128)S(1)} %copy-done.3, bf16[2,256,1024]{2,1,0:T(8,128)(2,1)} %collective-permute-done.10), kind=kLoop, calls=%fused_computation.5 | loop fusion | flops 2097152 | bytes 6291456 | tf_op jit(solution)/shard_map/add | solution.py:273
  216.6 5.7 %all-to-all-done.5 = bf16[8,16,1024]{2,1,0:T(8,128)(2,1)S(1)} async-done(((bf16[8,16,1024]{2,1,0:T(8,128)(2,1)}), bf16[8,16,1024]{2,1,0:T(8,128)(2,1)S(1)}, u32[]{:S(2)}, u32[]{:S(2)}) %all-to-all-start.5) | async-done | bytes 262176 | tf_op jit(solution)/shard_map/all_to_all | solution.py:183
  222.3 2.8 %collective-permute-start.26 = (f32[16,1024]{1,0:T(8,128)S(1)}, f32[16,1024]{1,0:T(8,128)S(1)}, u32[]{:S(2)}, u32[]{:S(2)}) collective-permute-start(f32[16,1024]{1,0:T(8,128)S(1)} %convert_reduce_fusion), channel_id=1, source_target_pairs={{0,192},{64,0},{128,64},{192,128},{1,193},{65,1},{129,65},{193,129... | collective-permute-start | bytes 196616 | tf_op jit(solution)/shard_map/ppermute | solution.py:291
  226.2 3.0 %fusion.10 = (bf16[1,256,1024]{2,1,0:T(8,128)(2,1)}, bf16[1,256,1024]{2,1,0:T(8,128)(2,1)}) fusion(f32[2,256,1024]{2,1,0:T(8,128)} %convert_add_fusion, bf16[256,1024]{1,0:T(8,128)(2,1)} %collective-permute-done.19, pred[]{:T(512)S(6)} %eq.50, pred[]{:T(512)S(6)} %eq.49, bf16[64,1024]{1,0:T(8,128)(2,1)S(1)} %get-tuple-element.49, ...), kind=kLoop, calls=%fused_computation.30 | loop fusion | flops 4718592 | bytes 4194306 | tf_op jit(solution)/shard_map/broadcast_in_dim | solution.py:294
  (109 shorter events, 18.9 us)
Async XLA Ops:
  0.6 55.1 %copy-start = (bf16[1024,1024]{1,0:T(8,128)(2,1)S(1)}, bf16[1024,1024]{1,0:T(8,128)(2,1)}, u32[]{:S(2)}) copy-start(bf16[1024,1024]{1,0:T(8,128)(2,1)} %param.11) | copy-start | bytes 6291460
  0.6 6.1 %copy-start.1 = (bf16[1,256,1024]{2,1,0:T(8,128)(2,1)S(1)}, bf16[1,256,1024]{2,1,0:T(8,128)(2,1)}, u32[]{:S(2)}) copy-start(bf16[1,256,1024]{2,1,0:T(8,128)(2,1)} %param.8) | copy-start | bytes 1572868
  0.7 6.2 %copy-start.4 = (bf16[1,256,1024]{2,1,0:T(8,128)(2,1)S(1)}, bf16[1,256,1024]{2,1,0:T(8,128)(2,1)}, u32[]{:S(2)}) copy-start(bf16[1,256,1024]{2,1,0:T(8,128)(2,1)} %param.9) | copy-start | bytes 1572868
  2.9 5.1 %collective-permute-start = (bf16[256,1024]{1,0:T(8,128)(2,1)}, bf16[256,1024]{1,0:T(8,128)(2,1)}, u32[]{:S(2)}, u32[]{:S(2)}) collective-permute-start(bf16[256,1024]{1,0:T(8,128)(2,1)} %broadcast_select_fusion), channel_id=1, source_target_pairs={{0,1},{1,0},{2,3},{3,2},{4,5},{5,4},{6,7},{7,6},{8,9},{9,8},{10,11... | collective-permute-start | bytes 1572872 | tf_op jit(solution)/shard_map/ppermute | solution.py:175
  6.8 5.6 %copy-start.32 = (s32[1,3]{1,0:T(1,128)S(1)}, s32[1,3]{1,0:T(1,128)}, u32[]{:S(2)}) copy-start(s32[1,3]{1,0:T(1,128)} %param.12) | copy-start | bytes 40
  7.1 2.9 %copy-start.31 = (bf16[2,256,1024]{2,1,0:T(8,128)(2,1)}, bf16[2,256,1024]{2,1,0:T(8,128)(2,1)S(1)}, u32[]{:S(2)}) copy-start(bf16[2,256,1024]{2,1,0:T(8,128)(2,1)S(1)} %get-tuple-element.55) | copy-start | bytes 3145732
  10.0 27.7 %collective-permute-start.3 = (bf16[2,64,1024]{2,1,0:T(8,128)(2,1)}, bf16[2,64,1024]{2,1,0:T(8,128)(2,1)}, u32[]{:S(2)}, u32[]{:S(2)}) collective-permute-start(bf16[2,64,1024]{2,1,0:T(8,128)(2,1)} %get-tuple-element.44), channel_id=1, source_target_pairs={{0,6},{1,7},{2,0},{3,1},{4,2},{5,3},{6,4},{7,5},{8,14},{9,15},{10,... | collective-permute-start | bytes 786440 | tf_op jit(solution)/shard_map/ppermute | solution.py:175
  10.7 26.9 %collective-permute-start.1 = (bf16[2,64,1024]{2,1,0:T(8,128)(2,1)}, bf16[2,64,1024]{2,1,0:T(8,128)(2,1)}, u32[]{:S(2)}, u32[]{:S(2)}) collective-permute-start(bf16[2,64,1024]{2,1,0:T(8,128)(2,1)} %get-tuple-element.46), channel_id=1, source_target_pairs={{0,2},{1,3},{2,4},{3,5},{4,6},{5,7},{6,0},{7,1},{8,10},{9,11},{10,... | collective-permute-start | bytes 786440 | tf_op jit(solution)/shard_map/ppermute | solution.py:175
  11.5 26.2 %collective-permute-start.2 = (bf16[2,64,1024]{2,1,0:T(8,128)(2,1)}, bf16[2,64,1024]{2,1,0:T(8,128)(2,1)}, u32[]{:S(2)}, u32[]{:S(2)}) collective-permute-start(bf16[2,64,1024]{2,1,0:T(8,128)(2,1)} %get-tuple-element.47), channel_id=1, source_target_pairs={{0,4},{1,5},{2,6},{3,7},{4,0},{5,1},{6,2},{7,3},{8,12},{9,13},{10,... | collective-permute-start | bytes 786440 | tf_op jit(solution)/shard_map/ppermute | solution.py:175
  39.5 11.1 %all-to-all-start.1 = ((bf16[8,8,1024]{2,1,0:T(8,128)(2,1)}), bf16[8,8,1024]{2,1,0:T(8,128)(2,1)S(1)}, u32[]{:S(2)}, u32[]{:S(2)}) async-start(bf16[8,8,1024]{2,1,0:T(8,128)(2,1)} %fusion.31), calls=%async_computation.1 | async-start | bytes 262144 | tf_op jit(solution)/shard_map/all_to_all | solution.py:183
  42.9 36.3 %collective-permute-start.9 = (bf16[2,256,1024]{2,1,0:T(8,128)(2,1)}, bf16[2,256,1024]{2,1,0:T(8,128)(2,1)}, u32[]{:S(2)}, u32[]{:S(2)}) collective-permute-start(bf16[2,256,1024]{2,1,0:T(8,128)(2,1)} %copy-done.31), channel_id=1, source_target_pairs={{1,0},{2,1},{3,2},{4,3},{5,4},{6,5},{7,6},{8,7},{9,8},{10,9},{11,1... | collective-permute-start | bytes 3145736 | tf_op jit(solution)/shard_map/ppermute | solution.py:175
  45.5 35.0 %collective-permute-start.8 = (bf16[2,256,1024]{2,1,0:T(8,128)(2,1)}, bf16[2,256,1024]{2,1,0:T(8,128)(2,1)}, u32[]{:S(2)}, u32[]{:S(2)}) collective-permute-start(bf16[2,256,1024]{2,1,0:T(8,128)(2,1)} %copy-done.31), channel_id=1, source_target_pairs={{0,1},{1,2},{2,3},{3,4},{4,5},{5,6},{6,7},{7,8},{8,9},{9,10},{10,1... | collective-permute-start | bytes 3145736 | tf_op jit(solution)/shard_map/ppermute | solution.py:175
  51.3 12.2 %all-to-all-start.2 = ((bf16[8,8,1024]{2,1,0:T(8,128)(2,1)}), bf16[8,8,1024]{2,1,0:T(8,128)(2,1)S(1)}, u32[]{:S(2)}, u32[]{:S(2)}) async-start(bf16[8,8,1024]{2,1,0:T(8,128)(2,1)} %broadcast_in_dim.41), calls=%async_computation.2 | async-start | bytes 262144 | tf_op jit(solution)/shard_map/all_to_all | solution.py:183
  63.5 11.8 %collective-permute-start.6 = (bf16[64,1024]{1,0:T(8,128)(2,1)S(1)}, bf16[64,1024]{1,0:T(8,128)(2,1)S(1)}, u32[]{:S(2)}, u32[]{:S(2)}) collective-permute-start(bf16[64,1024]{1,0:T(8,128)(2,1)S(1)} %bitcast.165), channel_id=1, source_target_pairs={{0,6},{1,7},{2,0},{3,1},{4,2},{5,3},{6,4},{7,5},{8,14},{9,15},{10,... | collective-permute-start | bytes 393224 | tf_op jit(solution)/shard_map/ppermute | solution.py:175
  71.3 5.4 %collective-permute-start.5 = (bf16[64,1024]{1,0:T(8,128)(2,1)S(1)}, bf16[64,1024]{1,0:T(8,128)(2,1)S(1)}, u32[]{:S(2)}, u32[]{:S(2)}) collective-permute-start(bf16[64,1024]{1,0:T(8,128)(2,1)S(1)} %bitcast.166), channel_id=1, source_target_pairs={{0,4},{1,5},{2,6},{3,7},{4,0},{5,1},{6,2},{7,3},{8,12},{9,13},{10,... | collective-permute-start | bytes 393224 | tf_op jit(solution)/shard_map/ppermute | solution.py:175
  71.3 6.5 %collective-permute-start.4 = (bf16[64,1024]{1,0:T(8,128)(2,1)S(1)}, bf16[64,1024]{1,0:T(8,128)(2,1)}, u32[]{:S(2)}, u32[]{:S(2)}) collective-permute-start(bf16[64,1024]{1,0:T(8,128)(2,1)S(1)} %bitcast.167), channel_id=1, source_target_pairs={{0,2},{1,3},{2,4},{3,5},{4,6},{5,7},{6,0},{7,1},{8,10},{9,11},{10,... | collective-permute-start | bytes 393224 | tf_op jit(solution)/shard_map/ppermute | solution.py:175
  79.0 3.3 %copy-start.17 = (bf16[1,256,1024]{2,1,0:T(8,128)(2,1)S(1)}, bf16[1,256,1024]{2,1,0:T(8,128)(2,1)}, u32[]{:S(2)}) copy-start(bf16[1,256,1024]{2,1,0:T(8,128)(2,1)} %param.7) | copy-start | bytes 1572868
  79.0 11.6 %collective-permute-start.7 = (bf16[256,1024]{1,0:T(8,128)(2,1)S(1)}, bf16[256,1024]{1,0:T(8,128)(2,1)S(1)}, u32[]{:S(2)}, u32[]{:S(2)}) collective-permute-start(bf16[256,1024]{1,0:T(8,128)(2,1)S(1)} %pad_maximum_fusion.1.half), channel_id=1, source_target_pairs={{0,1},{1,0},{2,3},{3,2},{4,5},{5,4},{6,7},{7,6},{8,9},{9,8},{10,11... | collective-permute-start | bytes 1572872 | tf_op jit(solution)/shard_map/ppermute | solution.py:175
  80.5 10.0 %copy-start.9 = (bf16[256,1024]{1,0:T(8,128)(2,1)}, bf16[256,1024]{1,0:T(8,128)(2,1)S(1)}, u32[]{:S(2)}) copy-start(bf16[256,1024]{1,0:T(8,128)(2,1)S(1)} %get-tuple-element.40.vr) | copy-start | bytes 1572868
  80.5 10.0 %copy-start.11 = (bf16[256,1024]{1,0:T(8,128)(2,1)}, bf16[256,1024]{1,0:T(8,128)(2,1)S(1)}, u32[]{:S(2)}) copy-start(bf16[256,1024]{1,0:T(8,128)(2,1)S(1)} %get-tuple-element.41.kr) | copy-start | bytes 1572868
  82.2 8.4 %copy-start.13 = (bf16[256,1024]{1,0:T(8,128)(2,1)}, bf16[256,1024]{1,0:T(8,128)(2,1)S(1)}, u32[]{:S(2)}) copy-start(bf16[256,1024]{1,0:T(8,128)(2,1)S(1)} %get-tuple-element.42.vl) | copy-start | bytes 1572868
  82.2 8.4 %copy-start.15 = (bf16[256,1024]{1,0:T(8,128)(2,1)}, bf16[256,1024]{1,0:T(8,128)(2,1)S(1)}, u32[]{:S(2)}) copy-start(bf16[256,1024]{1,0:T(8,128)(2,1)S(1)} %get-tuple-element.43.kl) | copy-start | bytes 1572868
  82.2 8.4 %copy-start.20 = (bf16[256,1024]{1,0:T(8,128)(2,1)S(1)}, bf16[256,1024]{1,0:T(8,128)(2,1)}, u32[]{:S(2)}) copy-start(bf16[256,1024]{1,0:T(8,128)(2,1)} %convolution_convert_fusion.1.d) | copy-start | bytes 1572868
  102.6 0.8 copy-start.5
  103.4 0.8 copy-start.7
  104.2 0.8 copy-start.19
  105.0 1.0 copy-start.22
  106.0 1.0 copy-start.24
  107.0 1.0 copy-start.26
  110.0 3.7 %collective-permute-start.12 = (bf16[256,1024]{1,0:T(8,128)(2,1)}, bf16[256,1024]{1,0:T(8,128)(2,1)S(1)}, u32[]{:S(2)}, u32[]{:S(2)}) collective-permute-start(bf16[256,1024]{1,0:T(8,128)(2,1)} %copy-done.19), channel_id=1, source_target_pairs={{0,1},{1,0},{2,3},{3,2},{4,5},{5,4},{6,7},{7,6},{8,9},{9,8},{10,11... | collective-permute-start | bytes 1572872 | tf_op jit(solution)/shard_map/ppermute | solution.py:175
  112.4 2.3 %copy-start.28 = (f32[8,4,2,16,1024]{4,3,2,1,0:T(8,128)}, f32[8,4,2,16,1024]{4,3,2,1,0:T(8,128)S(1)}, u32[]{:S(2)}) copy-start(f32[8,4,2,16,1024]{4,3,2,1,0:T(8,128)S(1)} %fusion.14) | copy-start | bytes 12582916
  112.4 1.4 copy-start.6
  113.7 57.7 %collective-permute-start.20 = (bf16[8,4,16,1024]{3,2,1,0:T(8,128)(2,1)}, bf16[8,4,16,1024]{3,2,1,0:T(8,128)(2,1)}, u32[]{:S(2)}, u32[]{:S(2)}) collective-permute-start(bf16[8,4,16,1024]{3,2,1,0:T(8,128)(2,1)} %fusion.4), channel_id=1, source_target_pairs={{0,1},{1,0},{2,3},{3,2},{4,5},{5,4},{6,7},{7,6},{8,9},{9,8},{10,11... | collective-permute-start | bytes 3145736 | tf_op jit(solution)/shard_map/ppermute | solution.py:175
  116.2 6.5 %collective-permute-start.13 = (bf16[64,1024]{1,0:T(8,128)(2,1)}, bf16[64,1024]{1,0:T(8,128)(2,1)S(1)}, u32[]{:S(2)}, u32[]{:S(2)}) collective-permute-start(bf16[64,1024]{1,0:T(8,128)(2,1)} %get-tuple-element.52), channel_id=1, source_target_pairs={{0,2},{1,3},{2,4},{3,5},{4,6},{5,7},{6,0},{7,1},{8,10},{9,11},{10,... | collective-permute-start | bytes 393224 | tf_op jit(solution)/shard_map/ppermute | solution.py:175
  116.2 8.2 %collective-permute-start.15 = (bf16[64,1024]{1,0:T(8,128)(2,1)}, bf16[64,1024]{1,0:T(8,128)(2,1)S(1)}, u32[]{:S(2)}, u32[]{:S(2)}) collective-permute-start(bf16[64,1024]{1,0:T(8,128)(2,1)} %get-tuple-element.53), channel_id=1, source_target_pairs={{0,6},{1,7},{2,0},{3,1},{4,2},{5,3},{6,4},{7,5},{8,14},{9,15},{10,... | collective-permute-start | bytes 393224 | tf_op jit(solution)/shard_map/ppermute | solution.py:175
  118.9 6.1 %collective-permute-start.14 = (bf16[64,1024]{1,0:T(8,128)(2,1)S(1)}, bf16[64,1024]{1,0:T(8,128)(2,1)}, u32[]{:S(2)}, u32[]{:S(2)}) collective-permute-start(bf16[64,1024]{1,0:T(8,128)(2,1)S(1)} %get-tuple-element.54), channel_id=1, source_target_pairs={{0,4},{1,5},{2,6},{3,7},{4,0},{5,1},{6,2},{7,3},{8,12},{9,13},{10,... | collective-permute-start | bytes 393224 | tf_op jit(solution)/shard_map/ppermute | solution.py:175
  126.7 37.0 %all-to-all-start.3 = ((bf16[8,8,1024]{2,1,0:T(8,128)(2,1)}), bf16[8,8,1024]{2,1,0:T(8,128)(2,1)S(1)}, u32[]{:S(2)}, u32[]{:S(2)}) async-start(bf16[8,8,1024]{2,1,0:T(8,128)(2,1)} %fusion.30), calls=%async_computation.3 | async-start | bytes 262144 | tf_op jit(solution)/shard_map/all_to_all | solution.py:183
  130.3 1.0 copy-start.10
  131.3 1.0 copy-start.12
  132.3 1.0 copy-start.14
  133.4 1.0 copy-start.16
  134.4 1.0 copy-start.18
  135.5 1.0 copy-start.21
  136.5 1.2 copy-start.23
  137.7 1.2 copy-start.25
  139.0 1.2 copy-start.27
  156.3 1.4 copy-start.2
  157.6 55.4 %collective-permute-start.10 = (bf16[2,256,1024]{2,1,0:T(8,128)(2,1)}, bf16[2,256,1024]{2,1,0:T(8,128)(2,1)}, u32[]{:S(2)}, u32[]{:S(2)}) collective-permute-start(bf16[2,256,1024]{2,1,0:T(8,128)(2,1)} %get-tuple-element.27), channel_id=1, source_target_pairs={{1,0},{2,1},{3,2},{4,3},{5,4},{6,5},{7,6},{8,7},{9,8},{10,9},{11,1... | collective-permute-start | bytes 3145736 | tf_op jit(solution)/shard_map/ppermute | solution.py:175
  161.3 51.8 %collective-permute-start.11 = (bf16[2,256,1024]{2,1,0:T(8,128)(2,1)}, bf16[2,256,1024]{2,1,0:T(8,128)(2,1)}, u32[]{:S(2)}, u32[]{:S(2)}) collective-permute-start(bf16[2,256,1024]{2,1,0:T(8,128)(2,1)} %get-tuple-element.28), channel_id=1, source_target_pairs={{0,1},{1,2},{2,3},{3,4},{4,5},{5,6},{6,7},{7,8},{8,9},{9,10},{10,1... | collective-permute-start | bytes 3145736 | tf_op jit(solution)/shard_map/ppermute | solution.py:175
  164.4 14.7 %all-to-all-start.4 = ((bf16[8,8,1024]{2,1,0:T(8,128)(2,1)}), bf16[8,8,1024]{2,1,0:T(8,128)(2,1)S(1)}, u32[]{:S(2)}, u32[]{:S(2)}) async-start(bf16[8,8,1024]{2,1,0:T(8,128)(2,1)} %broadcast_in_dim.44), calls=%async_computation.4 | async-start | bytes 262144 | tf_op jit(solution)/shard_map/all_to_all | solution.py:183
  174.5 22.9 %copy-start.29 = (bf16[8,4,16,1024]{3,2,1,0:T(8,128)(2,1)}, bf16[8,4,16,1024]{3,2,1,0:T(8,128)(2,1)S(1)}, u32[]{:S(2)}) copy-start(bf16[8,4,16,1024]{3,2,1,0:T(8,128)(2,1)S(1)} %fusion.2) | copy-start | bytes 3145732
  179.1 12.5 %collective-permute-start.18 = (bf16[64,1024]{1,0:T(8,128)(2,1)S(1)}, bf16[64,1024]{1,0:T(8,128)(2,1)S(1)}, u32[]{:S(2)}, u32[]{:S(2)}) collective-permute-start(bf16[64,1024]{1,0:T(8,128)(2,1)S(1)} %bitcast.169), channel_id=1, source_target_pairs={{0,6},{1,7},{2,0},{3,1},{4,2},{5,3},{6,4},{7,5},{8,14},{9,15},{10,... | collective-permute-start | bytes 393224 | tf_op jit(solution)/shard_map/ppermute | solution.py:175
  188.3 5.4 %collective-permute-start.17 = (bf16[64,1024]{1,0:T(8,128)(2,1)S(1)}, bf16[64,1024]{1,0:T(8,128)(2,1)S(1)}, u32[]{:S(2)}, u32[]{:S(2)}) collective-permute-start(bf16[64,1024]{1,0:T(8,128)(2,1)S(1)} %bitcast.170), channel_id=1, source_target_pairs={{0,4},{1,5},{2,6},{3,7},{4,0},{5,1},{6,2},{7,3},{8,12},{9,13},{10,... | collective-permute-start | bytes 393224 | tf_op jit(solution)/shard_map/ppermute | solution.py:175
  188.3 7.8 %collective-permute-start.16 = (bf16[64,1024]{1,0:T(8,128)(2,1)S(1)}, bf16[64,1024]{1,0:T(8,128)(2,1)S(1)}, u32[]{:S(2)}, u32[]{:S(2)}) collective-permute-start(bf16[64,1024]{1,0:T(8,128)(2,1)S(1)} %bitcast.171), channel_id=1, source_target_pairs={{0,2},{1,3},{2,4},{3,5},{4,6},{5,7},{6,0},{7,1},{8,10},{9,11},{10,... | collective-permute-start | bytes 393224 | tf_op jit(solution)/shard_map/ppermute | solution.py:175
  191.6 10.6 %collective-permute-start.21 = (bf16[8,16,1024]{2,1,0:T(8,128)(2,1)S(1)}, bf16[8,16,1024]{2,1,0:T(8,128)(2,1)S(1)}, u32[]{:S(2)}, u32[]{:S(2)}) collective-permute-start(bf16[8,16,1024]{2,1,0:T(8,128)(2,1)S(1)} %get-tuple-element.37), channel_id=1, source_target_pairs={{0,2},{1,3},{2,4},{3,5},{4,6},{5,7},{6,0},{7,1},{8,10},{9,11},{10,... | collective-permute-start | bytes 786440 | tf_op jit(solution)/shard_map/ppermute | solution.py:175
  193.7 8.4 %collective-permute-start.23 = (bf16[8,16,1024]{2,1,0:T(8,128)(2,1)S(1)}, bf16[8,16,1024]{2,1,0:T(8,128)(2,1)S(1)}, u32[]{:S(2)}, u32[]{:S(2)}) collective-permute-start(bf16[8,16,1024]{2,1,0:T(8,128)(2,1)S(1)} %get-tuple-element.38), channel_id=1, source_target_pairs={{0,6},{1,7},{2,0},{3,1},{4,2},{5,3},{6,4},{7,5},{8,14},{9,15},{10,... | collective-permute-start | bytes 786440 | tf_op jit(solution)/shard_map/ppermute | solution.py:175
  196.0 10.2 %collective-permute-start.22 = (bf16[8,16,1024]{2,1,0:T(8,128)(2,1)S(1)}, bf16[8,16,1024]{2,1,0:T(8,128)(2,1)S(1)}, u32[]{:S(2)}, u32[]{:S(2)}) collective-permute-start(bf16[8,16,1024]{2,1,0:T(8,128)(2,1)S(1)} %get-tuple-element.39), channel_id=1, source_target_pairs={{0,4},{1,5},{2,6},{3,7},{4,0},{5,1},{6,2},{7,3},{8,12},{9,13},{10,... | collective-permute-start | bytes 786440 | tf_op jit(solution)/shard_map/ppermute | solution.py:175
  197.5 14.1 %copy-start.8 = (bf16[256,1024]{1,0:T(8,128)(2,1)S(1)}, bf16[256,1024]{1,0:T(8,128)(2,1)}, u32[]{:S(2)}) copy-start(bf16[256,1024]{1,0:T(8,128)(2,1)} %copy-done.7) | copy-start | bytes 1572868
  202.1 24.1 %collective-permute-start.19 = (bf16[256,1024]{1,0:T(8,128)(2,1)}, bf16[256,1024]{1,0:T(8,128)(2,1)}, u32[]{:S(2)}, u32[]{:S(2)}) collective-permute-start(bf16[256,1024]{1,0:T(8,128)(2,1)} %pad_maximum_fusion.3), channel_id=1, source_target_pairs={{0,1},{1,0},{2,3},{3,2},{4,5},{5,4},{6,7},{7,6},{8,9},{9,8},{10,11... | collective-permute-start | bytes 1572872 | tf_op jit(solution)/shard_map/ppermute | solution.py:175
  208.1 14.2 %all-to-all-start.5 = ((bf16[8,16,1024]{2,1,0:T(8,128)(2,1)}), bf16[8,16,1024]{2,1,0:T(8,128)(2,1)S(1)}, u32[]{:S(2)}, u32[]{:S(2)}) async-start(bf16[8,16,1024]{2,1,0:T(8,128)(2,1)} %fusion.13), calls=%async_computation.5 | async-start | bytes 524288 | tf_op jit(solution)/shard_map/all_to_all | solution.py:183
  211.6 1.6 copy-start.3
  222.3 6.9 %collective-permute-start.26 = (f32[16,1024]{1,0:T(8,128)S(1)}, f32[16,1024]{1,0:T(8,128)S(1)}, u32[]{:S(2)}, u32[]{:S(2)}) collective-permute-start(f32[16,1024]{1,0:T(8,128)S(1)} %convert_reduce_fusion), channel_id=1, source_target_pairs={{0,192},{64,0},{128,64},{192,128},{1,193},{65,1},{129,65},{193,129... | collective-permute-start | bytes 196616 | tf_op jit(solution)/shard_map/ppermute | solution.py:291
  225.2 4.7 %collective-permute-start.25 = (f32[16,1024]{1,0:T(8,128)S(1)}, f32[16,1024]{1,0:T(8,128)S(1)}, u32[]{:S(2)}, u32[]{:S(2)}) collective-permute-start(f32[16,1024]{1,0:T(8,128)S(1)} %convert_reduce_fusion), channel_id=1, source_target_pairs={{0,128},{64,192},{128,0},{192,64},{1,129},{65,193},{129,1},{193,65... | collective-permute-start | bytes 196616 | tf_op jit(solution)/shard_map/ppermute | solution.py:291
  225.5 5.0 %collective-permute-start.24 = (f32[16,1024]{1,0:T(8,128)S(1)}, f32[16,1024]{1,0:T(8,128)S(1)}, u32[]{:S(2)}, u32[]{:S(2)}) collective-permute-start(f32[16,1024]{1,0:T(8,128)S(1)} %convert_reduce_fusion), channel_id=1, source_target_pairs={{0,64},{64,128},{128,192},{192,0},{1,65},{65,129},{129,193},{193,1... | collective-permute-start | bytes 196616 | tf_op jit(solution)/shard_map/ppermute | solution.py:291
  (1 other events, 0.8 us)

commit v2 on v1

v2 whole, which is shorter than its diff:
```python
import jax
import jax.numpy as jnp
from jax import lax
from jax.experimental import pallas as pl
from jax.experimental.pallas import tpu as pltpu
from jax.sharding import PartitionSpec as P

HEAD_DIM = 64
NZ, NX, NC = 8, 4, 2
SPAN = 256
F32 = jnp.float32
BF16 = jnp.bfloat16
NEVER = -1e30


def nt(a, b):
    return lax.dot_general(a, b, (((1,), (1,)), ((), ())), preferred_element_type=F32)


def tn(a, b):
    return lax.dot_general(a, b, (((0,), (0,)), ((), ())), preferred_element_type=F32)


def nn(a, b):
    return lax.dot_general(a, b, (((1,), (0,)), ((), ())), preferred_element_type=F32)


def half_masks(shape):
    lane = lax.broadcasted_iota(jnp.int32, shape, 1)
    return [lane < HEAD_DIM, lane >= HEAD_DIM]


def local_forward(flags, q, own, left, right, m_out, l_out, o_out):
    seen = [None, flags[0] > 0, flags[1] > 0]
    for g in range(SPAN // 128):
        cols = pl.ds(g * 128, 128)
        queries = q[:, cols] * 0.125
        masks = half_masks(queries.shape)
        keys = [ref[0, :, cols] for ref in (own, left, right)]
        vals = [ref[1, :, cols] for ref in (own, left, right)]
        tops, sums, mixes = [], [], []
        for mask in masks:
            part = jnp.where(mask, queries, 0).astype(BF16)
            scores = [nt(part, k) for k in keys]
            tops_of = [jnp.max(s, axis=1, keepdims=True) for s in scores]
            top = tops_of[0]
            for t, f in zip(tops_of[1:], seen[1:]):
                top = jnp.maximum(top, jnp.where(f, t, NEVER))
            shifts = [top if f is None else jnp.where(f, top, -NEVER) for f in seen]
            weights = [jnp.exp(s - t) for s, t in zip(scores, shifts)]
            sums.append(jnp.sum(weights[0] + weights[1] + weights[2], axis=1, keepdims=True))
            tops.append(top)
            mixes.append(sum(nn(w.astype(BF16), v) for w, v in zip(weights, vals)))
        m_out[:, cols] = jnp.where(masks[0], tops[0], tops[1])
        l_out[:, cols] = jnp.where(masks[0], sums[0], sums[1])
        o_out[:, cols] = jnp.where(masks[0], mixes[0], mixes[1])


def hub_block(
    flags, q, d, half, rest, m_in, l_in, o_in, grad,
    attn_out, lse_out, cen_out, dq_out, mine_out, other_out, kept_out, sent_out,
):
    first = flags[2] == 0
    seen = flags[3] > 0
    for g in range(SPAN // 128):
        cols = pl.ds(g * 128, 128)
        queries = q[:, cols] * 0.125
        grads = d[:, cols]
        masks = half_masks(queries.shape)
        a, b = half[:, cols], rest[:, cols]
        key = jnp.where(first, a, b)
        val = jnp.where(first, b, a)
        m_loc, l_loc, o_loc = m_in[:, cols], l_in[:, cols], o_in[:, cols]
        lses, cens, mixes, dqs = [], [], [], []
        dk = dv = 0.0
        for h, mask in enumerate(masks):
            part = jnp.where(mask, queries, 0).astype(BF16)
            gpart = jnp.where(mask, grads, 0).astype(BF16)
            at = slice(h * HEAD_DIM, h * HEAD_DIM + 1)
            scores = nt(part, key)
            old = m_loc[:, at]
            top = jnp.max(scores, axis=1, keepdims=True)
            top = jnp.maximum(old, jnp.where(seen, top, NEVER))
            weights = jnp.exp(scores - jnp.where(seen, top, -NEVER))
            fade = jnp.exp(old - top)
            total = l_loc[:, at] * fade + jnp.sum(weights, axis=1, keepdims=True)
            inv = 1.0 / total
            coarse = weights.astype(BF16)
            mix = (o_loc * fade + nn(coarse, val)) * inv
            cen = jnp.sum(mix * gpart.astype(F32), axis=1, keepdims=True)
            dscore = (weights * (nt(gpart, val) - cen)).astype(BF16)
            dqs.append(nn(dscore, key) * inv)
            dk += tn(dscore, (part.astype(F32) * inv).astype(BF16))
            dv += tn(coarse, (gpart.astype(F32) * inv).astype(BF16))
            lses.append(top + jnp.log(total))
            cens.append(cen)
            mixes.append(mix)
        attn = jnp.where(masks[0], mixes[0], mixes[1]).astype(BF16)
        attn_out[:, cols] = attn
        weight = tn(attn, grad[...])
        slab = weight.shape[0] // (NX * NC)
        weight = weight.reshape(NX, NC, slab, weight.shape[1])
        for j in range(NX):
            slot = (j - flags[4] + NX) % NX
            kept_out[slot, g] = jnp.where(first, weight[j, 0], weight[j, 1])
            sent_out[slot, g] = jnp.where(first, weight[j, 1], weight[j, 0]).astype(BF16)
        lse_out[:, cols] = jnp.where(masks[0], lses[0], lses[1])
        cen_out[:, cols] = jnp.where(masks[0], cens[0], cens[1])
        dq_out[:, cols] = jnp.where(masks[0], dqs[0], dqs[1])
        mine_out[:, cols] = jnp.where(first, dk, dv).astype(BF16)
        other_out[:, cols] = jnp.where(first, dv, dk).astype(BF16)


def local_backward(flags, q, d, own, left, right, lse_in, cen_in, dq_in, dq_out, own_out, left_out, right_out):
    seen = [None, flags[0] > 0, flags[1] > 0]
    for g in range(SPAN // 128):
        cols = pl.ds(g * 128, 128)
        queries = q[:, cols] * 0.125
        grads = d[:, cols]
        masks = half_masks(queries.shape)
        keys = [ref[0, :, cols] for ref in (own, left, right)]
        vals = [ref[1, :, cols] for ref in (own, left, right)]
        lse, cens = lse_in[:, cols], cen_in[:, cols]
        parts = [jnp.where(m, queries, 0).astype(BF16) for m in masks]
        gparts = [jnp.where(m, grads, 0).astype(BF16) for m in masks]
        dq = [0.0, 0.0]
        for key, val, flag, out in zip(keys, vals, seen, (own_out, left_out, right_out)):
            dk = dv = 0.0
            for h in range(2):
                at = slice(h * HEAD_DIM, h * HEAD_DIM + 1)
                shift = lse[:, at]
                if flag is not None:
                    shift = jnp.where(flag, shift, -NEVER)
                probs = jnp.exp(nt(parts[h], key) - shift)
                dscore = (probs * (nt(gparts[h], val) - cens[:, at])).astype(BF16)
                dq[h] += nn(dscore, key)
                dk += tn(dscore, parts[h])
                dv += tn(probs.astype(BF16), gparts[h])
            out[0, :, cols] = dk.astype(out.dtype)
            out[1, :, cols] = dv.astype(out.dtype)
        total = jnp.where(masks[0], dq[0], dq[1]) + dq_in[:, cols]
        dq_out[:, cols] = (total * 0.125).astype(BF16)


def prepare(spot, listed, counts, key, value, ids_out, flags_out, pair, *pieces):
    region = spot[0]
    left = right = far = jnp.int32(0)
    hub = jnp.int32(-1)
    for j in range(1, listed.shape[1]):
        entry = listed[0, j]
        used = j < counts[0]
        on_left, on_right = entry == region - 1, entry == region + 1
        beside = on_left | on_right
        left = jnp.where(used & on_left, 1, left)
        right = jnp.where(used & on_right, 1, right)
        far = jnp.where(used & jnp.logical_not(beside), 1, far)
        hub = jnp.where(used & jnp.logical_not(beside), entry, hub)
    x = region // NC % NX
    flags_out[0] = left
    flags_out[1] = right
    flags_out[2] = region % NC
    flags_out[3] = far
    flags_out[4] = x
    flags_out[5] = region
    flags_out[6] = 0
    flags_out[7] = 0
    ids_out[...] = jnp.full(ids_out.shape, hub, jnp.int32)
    pair[0] = key[...]
    pair[1] = value[...]
    quarter = pieces[0].shape[1]
    for k, out in enumerate(pieces):
        rows = pl.ds(pl.multiple_of((x + k) % NX * quarter, quarter), quarter)
        out[0] = key[rows, :]
        out[1] = value[rows, :]


def add_pieces(mine, theirs, *pieces):
    for out, k in zip(pieces, range(NX)):
        out[...] = (mine[k].astype(F32) + theirs[k].astype(F32)).astype(BF16)


def simple(body, ins, outs, name, scalars=0):
    smem = pl.BlockSpec(memory_space=pltpu.SMEM)
    vmem = pl.BlockSpec(memory_space=pltpu.VMEM)
    return pl.pallas_call(
        body,
        in_specs=[smem] * scalars + [vmem] * (len(ins) - scalars),
        out_specs=[smem if s == (8,) else vmem for s, _ in outs],
        out_shape=[jax.ShapeDtypeStruct(s, t) for s, t in outs],
        compiler_params=pltpu.CompilerParams(vmem_limit_bytes=32 * 1024 * 1024),
        name=name,
    )(*ins)


def local_backward_into(flags, *refs):
    local_backward(flags, *refs[:8], *refs[9:])


def choose(flags, ids, own, one, two, three, mine_out, other_out, flags_out):
    hub = jnp.max(ids[...])
    c, x = flags[2], flags[4]
    hub_z, hub_x, hub_c = hub // (NX * NC), hub // NC % NX, hub % NC
    for i in range(5):
        flags_out[i] = flags[i]
    flags_out[5] = (hub == flags[5]).astype(jnp.int32)
    flags_out[6] = hub_z
    flags_out[7] = (hub_c == c).astype(jnp.int32)
    for k, ref in enumerate((own, one, two, three)):

        @pl.when((x - hub_x + NX) % NX == k)
        def _():
            mine_out[...] = ref[c]
            other_out[...] = ref[1 - c]


def combine(flags, *refs):
    owns, lefts, rights = refs[0:2], refs[2:4], refs[4:6]
    far_half, far_rest, key_out, value_out = refs[6:]
    first = flags[2] == 0
    at_hub = flags[5] > 0
    tall = key_out.shape[0]
    quarter = far_half.shape[0] // NX
    for j in range(tall // quarter):
        spot = pl.program_id(0) * (tall // quarter) + j
        begin = pl.multiple_of((flags[4] - spot + NX) % NX * quarter, quarter)
        rows = pl.ds(j * quarter, quarter)
        at = 0
        for own, left, right in zip(owns, lefts, rights):
            cols = pl.ds(at, own.shape[-1])
            at += own.shape[-1]
            total = own[:, rows] + left[:, rows].astype(F32) + right[:, rows].astype(F32)
            half = far_half[pl.ds(begin, quarter), cols].astype(F32)
            rest = far_rest[pl.ds(begin, quarter), cols].astype(F32)
            far_key = jnp.where(first, half, rest)
            far_value = jnp.where(first, rest, half)
            key_out[rows, cols] = (total[0] + jnp.where(at_hub, far_key, 0.0)).astype(BF16)
            value_out[rows, cols] = (total[1] + jnp.where(at_hub, far_value, 0.0)).astype(BF16)


def across(shape, start=0):
    lead = (0,) * (len(shape) - 1)
    return pl.BlockSpec(tuple(shape[:-1]) + (SPAN,), lambda i, flags: lead + (i + start,))


def call(body, flags, ins, outs, steps, flops, name, aliases={}):
    shapes = [jax.ShapeDtypeStruct(s, t) for s, t, _ in outs]
    arrays = [a for a, _ in ins]
    moved = sum(a.size * a.dtype.itemsize for a in arrays + shapes)
    return pl.pallas_call(
        body,
        grid_spec=pltpu.PrefetchScalarGridSpec(
            num_scalar_prefetch=1,
            grid=(steps,),
            in_specs=[p or across(a.shape) for a, p in ins],
            out_specs=[p or across(s) for s, _, p in outs],
        ),
        out_shape=shapes,
        compiler_params=pltpu.CompilerParams(vmem_limit_bytes=56 * 1024 * 1024),
        cost_estimate=pl.CostEstimate(flops=flops, bytes_accessed=moved, transcendentals=0),
        input_output_aliases=aliases,
        name=name,
    )(flags, *arrays)


def place(z, x, c):
    return (z % NZ) * NX * NC + (x % NX) * NC + c % NC


def spots():
    return [(z, x, c) for z in range(NZ) for x in range(NX) for c in range(NC)]


def hop(dx=0, dc=0):
    return [(place(z, x, c), place(z, x + dx, c + dc)) for z, x, c in spots()]


Z_GROUPS = [[place(z, x, c) for z in range(NZ)] for x in range(NX) for c in range(NC)]


def send(value, pairs):
    return lax.ppermute(value, "region", pairs)


def pick(value, index):
    return lax.dynamic_index_in_dim(value, index, 0, keepdims=False)


def swap_z(value):
    return lax.all_to_all(value, "region", 0, 0, axis_index_groups=Z_GROUPS, tiled=True)


def gather_z(value):
    out = swap_z(jnp.broadcast_to(value[None], (NZ,) + value.shape))
    return out.reshape((-1,) + value.shape[1:])


def gather_x(value):
    return jnp.concatenate([value] + [send(value, hop(dx=k)) for k in range(1, NX)])


def sum_x(pieces):
    got = [pieces[0]] + [send(pieces[k], hop(dx=k)) for k in range(1, NX)]
    return sum(g.astype(F32) for g in got)


def shifted(value, step):
    last = NZ * NX * NC
    return send(value, [(i, i + step) for i in range(last) if 0 <= i + step < last])


def on_device(query, key_in, value, d_out, out_weight, attended, counts):
    region = lax.axis_index("region")
    x, c = (region // NC) % NX, region % NC
    first = c == 0
    query, key, value, grad_out = query[0], key_in[0], value[0], d_out[0]
    rows, width = query.shape
    quarter, eighth = rows // NX, rows // (NX * NZ)
    spots_count = NZ * NX * NC
    ids, flags, pair, *pieces = simple(
        prepare,
        [jnp.reshape(region, (1,)), attended, counts, key, value],
        [((spots_count, 1, 128), jnp.int32), ((8,), jnp.int32), ((2, rows, width), BF16)]
        + [((2, quarter, width), BF16)] * NX,
        "prepare",
        3,
    )
    arrived = [pieces[0]] + [send(pieces[k], hop(dx=k)) for k in range(1, NX)]
    ids = lax.all_to_all(ids, "region", 0, 0, tiled=True)
    mine, other, flags = simple(
        choose,
        [flags, ids, *arrived],
        [((quarter, width), BF16)] * 2 + [((8,), jnp.int32)],
        "choose",
        1,
    )
    part = jnp.where(flags[7] > 0, mine, send(other, hop(dc=1)))
    part, pair = lax.optimization_barrier((part, pair))
    near = [pair, shifted(pair, 1), shifted(pair, -1)]
    share = pick(swap_z(part.reshape(NZ, eighth, width)), flags[6])
    share, near = lax.optimization_barrier((share, near))

    flat, double = (rows, width), (2, rows, width)
    stats = call(
        local_forward,
        flags,
        [(a, None) for a in (query, *near)],
        [(flat, F32, None)] * 3,
        width // SPAN,
        int(5e9),
        "local_forward",
    )
    d_attn = lax.dot_general(
        grad_out, out_weight, (((1,), (1,)), ((), ())), preferred_element_type=F32
    ).astype(BF16)
    spread, stats, d_attn = lax.optimization_barrier((gather_z(share), stats, d_attn))
    half = gather_x(spread)
    rest = send(half, hop(dc=1))

    slab = width // (NZ * NX * NC)
    by_spot = (NX, NZ, slab, width)
    spot_block = pl.BlockSpec((NX, SPAN // 128, slab, width), lambda i, flags: (0, i, 0, 0))
    whole = pl.BlockSpec(flat, lambda i, flags: (0, 0))
    attn, lse, cen, dq_far, far_mine, far_other, kept, sent = call(
        hub_block,
        flags,
        [(a, None) for a in (query, d_attn, half, rest, *stats)] + [(grad_out, whole)],
        [(flat, t, None) for t in (BF16, F32, F32, F32, BF16, BF16)]
        + [(by_spot, F32, spot_block), (by_spot, BF16, spot_block)],
        width // SPAN,
        int(9e9),
        "hub_block",
    )

    stacked = (NX, quarter, width)
    pieces = simple(
        add_pieces,
        [far_mine.reshape(stacked), send(far_other, hop(dc=1)).reshape(stacked)],
        [((quarter, width), BF16)] * NX,
        "add_pieces",
    )
    pieces = [pieces[-k % NX] for k in range(NX)]
    turned = send(sent, hop(dc=1))
    pieces, kept, attn = lax.optimization_barrier((pieces, kept, attn))
    slabs = simple(add_pieces, [kept, turned], [((NZ, slab, width), BF16)] * NX, "add_slabs")
    layer = nn(attn, out_weight).astype(BF16)
    pieces = [pieces[0]] + [send(pieces[k], hop(dx=k)) for k in range(1, NX)]
    pieces, slabs, layer, lse = lax.optimization_barrier((pieces, slabs, layer, lse))
    summed = sum(p.astype(F32) for p in pieces).astype(BF16)

    def backward(lse, d_query, begin, steps):
        inputs = (query, d_attn, *near, lse, cen, dq_far)
        ins = [(a, across(a.shape, begin)) for a in inputs]
        wide = (2, rows, steps * SPAN)
        body, aliases = local_backward, {}
        if d_query is not None:
            body, aliases = local_backward_into, {1 + len(ins): 0}
            ins = ins + [(d_query, pl.BlockSpec(memory_space=pl.ANY))]
        return call(
            body,
            flags,
            ins,
            [(flat, BF16, across(flat, begin))]
            + [(wide, F32, None), (wide, BF16, None), (wide, BF16, None)],
            steps,
            int(2e9) * steps,
            "local_backward",
            aliases,
        )

    d_query, *first_part = backward(lse, None, 0, 2)
    slabs = [slabs[0]] + [send(slabs[k], hop(dx=k)) for k in range(1, NX)]
    summed, first_part, lse = lax.optimization_barrier(
        (swap_z(summed.reshape(NZ, eighth, width)), first_part, lse)
    )
    total = jnp.sum(summed.astype(F32), axis=0).astype(BF16)
    weight = sum(p.astype(F32) for p in slabs).astype(BF16)
    sides = [shifted(first_part[1], -1), shifted(first_part[2], 1)]
    d_query, *second_part = backward(lse, d_query, 2, 2)
    both = jnp.concatenate([jnp.broadcast_to(total[None], (NZ,) + total.shape), weight], axis=1)
    both, second_part, sides = lax.optimization_barrier((swap_z(both), second_part, sides))
    far_half = gather_x(both[:, :eighth].reshape(quarter, width))
    weight, far_half = lax.optimization_barrier((both[:, eighth:], far_half))
    far_rest = send(far_half, hop(dc=1))
    weight = jnp.sum(weight.astype(F32), axis=0)
    parts = [first_part, second_part]
    rights = [sides[0], shifted(second_part[1], -1)]
    lefts = [sides[1], shifted(second_part[2], 1)]
    dp = lax.axis_size("dp")
    shares = [
        lax.ppermute(weight, "dp", [(i, (i + k) % dp) for i in range(dp)]) for k in range(1, dp)
    ]

    tall = rows // 2

    def pair_block(a):
        return pl.BlockSpec((2, tall, a.shape[-1]), lambda i, flags: (0, i, 0))

    d_key, d_value = call(
        combine,
        flags,
        [(a, pair_block(a)) for a in (*[p[0] for p in parts], *lefts, *rights)]
        + [(a, whole) for a in (far_half, far_rest)],
        [(flat, BF16, pl.BlockSpec((tall, width), lambda i, flags: (i, 0)))] * 2,
        2,
        int(1e6),
        "combine",
    )
    d_key, shares = lax.optimization_barrier((d_key, shares))
    d_weight = weight + sum(shares)
    return layer[None], d_query[None], d_key[None], d_value[None], d_weight


def solution(mesh):
    rows = P("dp", "region", None)
    return jax.shard_map(
        on_device,
        mesh=mesh,
        in_specs=(rows, rows, rows, rows, P(), P("region", None), P("region")),
        out_specs=(rows, rows, rows, rows, P("region", None)),
        check_vma=False,
    )
```

time: 234 us -> 195 us (0.83)
  the two profiles are of different devices: /device:TPU:1 before, /device:TPU:40 now
where the time goes in v2:
time: 195 us; the launch traced here: 194 us
  starting transfers between devices  68.4 us (35%)
  Pallas kernels  52 us (27%)
  waiting for transfers between devices  34.6 us (18%)
  blocking collectives  17.6 us (9%)
  local copies, waits for them, and re-layouts  7.49 us (4%)
  matrix products  5.12 us (3%)
  between operations  4.37 us (2%)
  other arithmetic  4.14 us (2%)
    pallas_call x5, Pallas kernels, call(): pl.pallas_call(body, grid_spec=pltpu.PrefetchScalarGridSpec(num_scalar_pr...  49.1 us
    ppermute x26, starting transfers between devices, send(): return lax.ppermute(value, 'region', pairs)  38 us
    ppermute x26, waiting for transfers between devices, send(): return lax.ppermute(value, 'region', pairs)  28.4 us
    all_to_all x4, starting transfers between devices, swap_z(): lax.all_to_all(value, 'region', 0, 0, axis_index_groups=Z_GROUPS, tiled=T...  25.4 us
    all_to_all x1, blocking collectives, on_device(): ids = lax.all_to_all(ids, 'region', 0, 0, tiled=True)  17.6 us
    all_to_all x4, waiting for transfers between devices, swap_z(): lax.all_to_all(value, 'region', 0, 0, axis_index_groups=Z_GROUPS, tiled=T...  6.2 us
    unnamed x35, local copies, waits for them, and re-layouts  6.18 us
    ppermute x3, starting transfers between devices, on_device(): lax.ppermute(weight, 'dp', [(i, (i + k) % dp) for i in range(dp)])  5.01 us
  transfers between devices with their start and end apart: 33, of which 13 were waited for; matrix products, arithmetic and copies ran while one was open for 3% of the time, Pallas kernels for 18%

profile of v2, /device:TPU:40, one launch (start us, length us, event | category | flops | bytes accessed | tf_op | source)
XLA Modules:
  0.0 193.7 jit_solution(8943547564231744627)
XLA Ops:
  1.5 1.0 copy-done.2
  2.5 1.0 copy-done.3
  3.5 0.7 copy-done.6
  4.2 1.2 prepare.1
  5.4 1.6 collective-permute-start
  6.9 2.7 %collective-permute-start.1 = (bf16[2,64,1024]{2,1,0:T(8,128)(2,1)S(1)}, bf16[2,64,1024]{2,1,0:T(8,128)(2,1)S(1)}, u32[]{:S(2)}, u32[]{:S(2)}) collective-permute-start(bf16[2,64,1024]{2,1,0:T(8,128)(2,1)S(1)} %get-tuple-element.92), channel_id=1, source_target_pairs={{0,4},{1,5},{2,6},{3,7},{4,0},{5,1},{6,2},{7,3},{8,12},{9,13},{10,... | collective-permute-start | bytes 786440 | tf_op jit(solution)/shard_map/ppermute | solution.py:281
  9.7 1.4 collective-permute-start.2
  11.1 17.6 %all_to_all.25.ids = s32[64,1,128]{2,1,0:T(1,128)S(1)} all-to-all(s32[64,1,128]{2,1,0:T(1,128)S(1)} %get-tuple-element.89), channel_id=1, replica_groups=mesh['dp'=4,'region'=64] {'region'}, dimensions={0} | all-to-all | bytes 65536 | tf_op jit(solution)/shard_map/all_to_all | solution.py:328
  28.7 1.4 choose.1
  30.2 0.6 fusion.2
  31.6 0.7 broadcast_select_fusion
  32.2 3.8 %collective-permute-start.5 = (bf16[2,256,1024]{2,1,0:T(8,128)(2,1)S(1)}, bf16[2,256,1024]{2,1,0:T(8,128)(2,1)}, u32[]{:S(2)}, u32[]{:S(2)}) collective-permute-start(bf16[2,256,1024]{2,1,0:T(8,128)(2,1)S(1)} %get-tuple-element.101.own.refs_2_), channel_id=1, source_target_pairs={{1,0},{2,1},{3,2},{4,3},{5,4},{6,5},{7,6},{8,7},{9,8},{10,9},{11,1... | collective-permute-start | bytes 3145736 | tf_op jit(solution)/shard_map/ppermute | solution.py:281
  36.1 1.9 collective-permute-start.4
  38.0 4.8 %all-to-all-start.1 = ((bf16[8,8,1024]{2,1,0:T(8,128)(2,1)}), bf16[8,8,1024]{2,1,0:T(8,128)(2,1)S(1)}, u32[]{:S(2)}, u32[]{:S(2)}) async-start(bf16[8,8,1024]{2,1,0:T(8,128)(2,1)} %bitcast.5), calls=%async_computation.1 | async-start | bytes 262144 | tf_op jit(solution)/shard_map/all_to_all | solution.py:289
  42.8 2.6 %convolution_convert_fusion.1.d.refs_1_ = bf16[256,1024]{1,0:T(8,128)(2,1)} fusion(bf16[1024,1024]{1,0:T(8,128)(2,1)S(1)} %copy-done, bf16[1,256,1024]{2,1,0:T(8,128)(2,1)} %param.10), kind=kOutput, calls=%fused_computation.1 | convolution fusion | flops 537133056 | bytes 3145728 | tf_op jit(solution)/shard_map/dot_general | solution.py:352
  47.4 6.2 %all-to-all-done.1 = bf16[8,8,1024]{2,1,0:T(8,128)(2,1)S(1)} async-done(((bf16[8,8,1024]{2,1,0:T(8,128)(2,1)}), bf16[8,8,1024]{2,1,0:T(8,128)(2,1)S(1)}, u32[]{:S(2)}, u32[]{:S(2)}) %all-to-all-start.1) | async-done | bytes 131104 | tf_op jit(solution)/shard_map/all_to_all | solution.py:289
  53.6 2.7 %collective-permute-done.4.left.refs_3_ = bf16[2,256,1024]{2,1,0:T(8,128)(2,1)} collective-permute-done((bf16[2,256,1024]{2,1,0:T(8,128)(2,1)S(1)}, bf16[2,256,1024]{2,1,0:T(8,128)(2,1)}, u32[]{:S(2)}, u32[]{:S(2)}) %collective-permute-start.4) | collective-permute-done | bytes 1048608 | tf_op jit(solution)/shard_map/ppermute | solution.py:281
  56.3 0.7 broadcast_in_dim.24
  56.9 6.1 %all-to-all-start.2 = ((bf16[8,8,1024]{2,1,0:T(8,128)(2,1)}), bf16[8,8,1024]{2,1,0:T(8,128)(2,1)S(1)}, u32[]{:S(2)}, u32[]{:S(2)}) async-start(bf16[8,8,1024]{2,1,0:T(8,128)(2,1)} %broadcast_in_dim.24), calls=%async_computation.2 | async-start | bytes 262144 | tf_op jit(solution)/shard_map/all_to_all | solution.py:289
  63.0 9.8 %local_forward.1 = (f32[256,1024]{1,0:T(8,128)}, f32[256,1024]{1,0:T(8,128)}, f32[256,1024]{1,0:T(8,128)}) custom-call(s32[8]{0:T(128)} %copy-done.5, bf16[256,1024]{1,0:T(8,128)(2,1)} %bitcast.35, bf16[2,256,1024]{2,1,0:T(8,128)(2,1)} %copy-done.7, bf16[2,256,1024]{2,1,0:T(8,128)(2,1)} %collective-permute-done.4.left.refs_3_, ...), custom_call_target="tpu_custom_call" | custom-call | flops 5000000000 | bytes 6815744 | tf_op jit(solution)/shard_map/local_forward/pallas_call | solution.py:249
  72.9 3.2 %collective-permute-start.8 = (bf16[64,1024]{1,0:T(8,128)(2,1)S(1)}, bf16[64,1024]{1,0:T(8,128)(2,1)S(1)}, u32[]{:S(2)}, u32[]{:S(2)}) collective-permute-start(bf16[64,1024]{1,0:T(8,128)(2,1)S(1)} %bitcast.31), channel_id=1, source_target_pairs={{0,6},{1,7},{2,0},{3,1},{4,2},{5,3},{6,4},{7,5},{8,14},{9,15},{10,... | collective-permute-start | bytes 393224 | tf_op jit(solution)/shard_map/ppermute | solution.py:281
  76.2 4.3 %collective-permute-done.6 = bf16[64,1024]{1,0:T(8,128)(2,1)S(1)} collective-permute-done((bf16[64,1024]{1,0:T(8,128)(2,1)S(1)}, bf16[64,1024]{1,0:T(8,128)(2,1)S(1)}, u32[]{:S(2)}, u32[]{:S(2)}) %collective-permute-start.6) | collective-permute-done | bytes 131104 | tf_op jit(solution)/shard_map/ppermute | solution.py:281
  80.5 2.1 %collective-permute-done.7 = bf16[64,1024]{1,0:T(8,128)(2,1)S(1)} collective-permute-done((bf16[64,1024]{1,0:T(8,128)(2,1)S(1)}, bf16[64,1024]{1,0:T(8,128)(2,1)S(1)}, u32[]{:S(2)}, u32[]{:S(2)}) %collective-permute-start.7) | collective-permute-done | bytes 131104 | tf_op jit(solution)/shard_map/ppermute | solution.py:281
  82.7 0.3 collective-permute-start.9
  83.0 1.9 collective-permute-done.9.rest
  84.9 0.8 copy-done.15
  85.7 15.4 %hub_block.1 = (bf16[256,1024]{1,0:T(8,128)(2,1)}, f32[256,1024]{1,0:T(8,128)}, f32[256,1024]{1,0:T(8,128)}, f32[256,1024]{1,0:T(8,128)}, bf16[256,1024]{1,0:T(8...) custom-call(s32[8]{0:T(128)} %copy-done.5, ...), custom_call_target="tpu_custom_call" | custom-call | flops 8999999488 | bytes 13631488 | tf_op jit(solution)/shard_map/hub_block/pallas_call | solution.py:249
  101.0 0.2 collective-permute-start.14
  101.2 0.4 collective-permute-start.10
  101.6 3.1 %collective-permute-done.10 = bf16[256,1024]{1,0:T(8,128)(2,1)S(1)} collective-permute-done((bf16[256,1024]{1,0:T(8,128)(2,1)}, bf16[256,1024]{1,0:T(8,128)(2,1)S(1)}, u32[]{:S(2)}, u32[]{:S(2)}) %collective-permute-start.10) | collective-permute-done | bytes 524320 | tf_op jit(solution)/shard_map/ppermute | solution.py:281
  104.7 1.0 copy-done.4
  105.9 0.8 collective-permute-start.11
  106.7 2.8 %collective-permute-start.12 = (bf16[64,1024]{1,0:T(8,128)(2,1)S(1)}, bf16[64,1024]{1,0:T(8,128)(2,1)S(1)}, u32[]{:S(2)}, u32[]{:S(2)}) collective-permute-start(bf16[64,1024]{1,0:T(8,128)(2,1)S(1)} %get-tuple-element.122), channel_id=1, source_target_pairs={{0,4},{1,5},{2,6},{3,7},{4,0},{5,1},{6,2},{7,3},{8,12},{9,13},{10,... | collective-permute-start | bytes 393224 | tf_op jit(solution)/shard_map/ppermute | solution.py:281
  109.5 2.5 %convolution_convert_fusion = bf16[256,1024]{1,0:T(8,128)(2,1)} fusion(bf16[256,1024]{1,0:T(8,128)(2,1)} %get-tuple-element.130, bf16[1024,1024]{1,0:T(8,128)(2,1)S(1)} %copy-done), kind=kOutput, calls=%fused_computation | convolution fusion | flops 537133056 | bytes 3145728 | tf_op jit(solution)/shard_map/dot_general | solution.py:25
  112.0 0.2 add_slabs.1
  112.2 1.0 collective-permute-done.11
  113.2 2.6 %collective-permute-done.12 = bf16[64,1024]{1,0:T(8,128)(2,1)S(1)} collective-permute-done((bf16[64,1024]{1,0:T(8,128)(2,1)S(1)}, bf16[64,1024]{1,0:T(8,128)(2,1)S(1)}, u32[]{:S(2)}, u32[]{:S(2)}) %collective-permute-start.12) | collective-permute-done | bytes 131104 | tf_op jit(solution)/shard_map/ppermute | solution.py:281
  115.8 0.3 collective-permute-done.13
  116.2 0.7 fusion
  116.9 7.2 %all-to-all-start.3 = ((bf16[8,8,1024]{2,1,0:T(8,128)(2,1)}), bf16[8,8,1024]{2,1,0:T(8,128)(2,1)S(1)}, u32[]{:S(2)}, u32[]{:S(2)}) async-start(bf16[8,8,1024]{2,1,0:T(8,128)(2,1)} %fusion), calls=%async_computation.3 | async-start | bytes 262144 | tf_op jit(solution)/shard_map/all_to_all | solution.py:289
  124.1 0.4 collective-permute-start.15
  124.6 3.6 %collective-permute-start.16 = (bf16[8,16,1024]{2,1,0:T(8,128)(2,1)S(1)}, bf16[8,16,1024]{2,1,0:T(8,128)(2,1)}, u32[]{:S(2)}, u32[]{:S(2)}) collective-permute-start(bf16[8,16,1024]{2,1,0:T(8,128)(2,1)S(1)} %get-tuple-element.150), channel_id=1, source_target_pairs={{0,4},{1,5},{2,6},{3,7},{4,0},{5,1},{6,2},{7,3},{8,12},{9,13},{10,... | collective-permute-start | bytes 786440 | tf_op jit(solution)/shard_map/ppermute | solution.py:281
  128.2 9.8 %local_backward.2 = (bf16[256,1024]{1,0:T(8,128)(2,1)}, f32[2,256,512]{2,1,0:T(8,128)}, bf16[2,256,512]{2,1,0:T(8,128)(2,1)}, bf16[2,256,512]{2,1,0:T(8,128)(2,1)}) custom-call(s32[8]{0:T(128)} %copy-done.5, bf16[256,1024]{1,0:T(8,128)(2,1)} %bitcast.37, bf16[256,1024]{1,0:T(8,128)(2,1)} %convolution_convert_fusion.1.d.refs_1_, ...), custom_call_target="tpu_custom_call" | custom-call | flops 4000000000 | bytes 9961472 | tf_op jit(solution)/shard_map/local_backward/pallas_call | solution.py:249
  138.1 1.4 collective-permute-done.16
  139.5 1.2 add_convert_fusion
  140.7 0.8 pad_maximum_fusion.1
  141.5 7.2 %all-to-all-start.4 = ((bf16[8,24,1024]{2,1,0:T(8,128)(2,1)}), bf16[8,24,1024]{2,1,0:T(8,128)(2,1)S(1)}, u32[]{:S(2)}, u32[]{:S(2)}) async-start(bf16[8,24,1024]{2,1,0:T(8,128)(2,1)} %pad_maximum_fusion.1), calls=%async_computation.4 | async-start | bytes 786432 | tf_op jit(solution)/shard_map/all_to_all | solution.py:289
  148.7 2.7 %collective-permute-start.18 = (bf16[2,256,512]{2,1,0:T(8,128)(2,1)}, bf16[2,256,512]{2,1,0:T(8,128)(2,1)S(1)}, u32[]{:S(2)}, u32[]{:S(2)}) collective-permute-start(bf16[2,256,512]{2,1,0:T(8,128)(2,1)} %get-tuple-element.155), channel_id=1, source_target_pairs={{1,0},{2,1},{3,2},{4,3},{5,4},{6,5},{7,6},{8,7},{9,8},{10,9},{11,1... | collective-permute-start | bytes 1572872 | tf_op jit(solution)/shard_map/ppermute | solution.py:281
  151.5 1.9 collective-permute-start.19
  153.4 9.9 %local_backward.3 = (bf16[256,1024]{1,0:T(8,128)(2,1)}, f32[2,256,512]{2,1,0:T(8,128)}, bf16[2,256,512]{2,1,0:T(8,128)(2,1)}, bf16[2,256,512]{2,1,0:T(8,128)(2,1)}) custom-call(s32[8]{0:T(128)} %copy-done.5, bf16[256,1024]{1,0:T(8,128)(2,1)} %bitcast.38, bf16[256,1024]{1,0:T(8,128)(2,1)} %convolution_convert_fusion.1.d.refs_1_, ...), custom_call_target="tpu_custom_call", output_to_operand_aliasing={{0}: (9, {})} | custom-call | flops 4000000000 | bytes 10485760 | tf_op jit(solution)/shard_map/local_backward/pallas_call | solution.py:249
  163.3 2.1 %collective-permute-done.19.refs_2_ = bf16[2,256,512]{2,1,0:T(8,128)(2,1)S(1)} collective-permute-done((bf16[2,256,512]{2,1,0:T(8,128)(2,1)}, bf16[2,256,512]{2,1,0:T(8,128)(2,1)S(1)}, u32[]{:S(2)}, u32[]{:S(2)}) %collective-permute-start.19) | collective-permute-done | bytes 524320 | tf_op jit(solution)/shard_map/ppermute | solution.py:281
  165.6 0.2 collective-permute-start.23
  165.8 1.8 collective-permute-start.22
  167.6 2.7 %collective-permute-start.20 = (bf16[2,256,512]{2,1,0:T(8,128)(2,1)}, bf16[2,256,512]{2,1,0:T(8,128)(2,1)S(1)}, u32[]{:S(2)}, u32[]{:S(2)}) collective-permute-start(bf16[2,256,512]{2,1,0:T(8,128)(2,1)} %get-tuple-element.159), channel_id=1, source_target_pairs={{0,1},{1,2},{2,3},{3,4},{4,5},{5,6},{6,7},{7,8},{8,9},{9,10},{10,1... | collective-permute-start | bytes 1572872 | tf_op jit(solution)/shard_map/ppermute | solution.py:281
  170.3 5.0 %collective-permute-start.21 = (bf16[2,256,512]{2,1,0:T(8,128)(2,1)}, bf16[2,256,512]{2,1,0:T(8,128)(2,1)S(1)}, u32[]{:S(2)}, u32[]{:S(2)}) collective-permute-start(bf16[2,256,512]{2,1,0:T(8,128)(2,1)} %get-tuple-element.161), channel_id=1, source_target_pairs={{1,0},{2,1},{3,2},{4,3},{5,4},{6,5},{7,6},{8,7},{9,8},{10,9},{11,1... | collective-permute-start | bytes 1572872 | tf_op jit(solution)/shard_map/ppermute | solution.py:281
  175.3 6.6 %collective-permute-done.22 = bf16[64,1024]{1,0:T(8,128)(2,1)S(1)} collective-permute-done((bf16[64,1024]{1,0:T(8,128)(2,1)S(1)}, bf16[64,1024]{1,0:T(8,128)(2,1)S(1)}, u32[]{:S(2)}, u32[]{:S(2)}) %collective-permute-start.22) | collective-permute-done | bytes 131104 | tf_op jit(solution)/shard_map/ppermute | solution.py:281
  182.0 0.2 collective-permute-start.25
  182.2 0.5 collective-permute-start.28
  182.8 2.6 %collective-permute-start.27 = (f32[16,1024]{1,0:T(8,128)S(1)}, f32[16,1024]{1,0:T(8,128)S(1)}, u32[]{:S(2)}, u32[]{:S(2)}) collective-permute-start(f32[16,1024]{1,0:T(8,128)S(1)} %convert_reduce_fusion), channel_id=1, source_target_pairs={{0,128},{64,192},{128,0},{192,64},{1,129},{65,193},{129,1},{193,65... | collective-permute-start | bytes 196616 | tf_op jit(solution)/shard_map/ppermute | solution.py:430
  185.4 1.9 collective-permute-start.26
  187.3 0.8 copy-done.12
  188.0 0.8 copy-done.13
  188.8 4.2 %combine.1 = (bf16[256,1024]{1,0:T(8,128)(2,1)}, bf16[256,1024]{1,0:T(8,128)(2,1)}) custom-call(s32[8]{0:T(128)} %copy-done.5, f32[2,256,512]{2,1,0:T(8,128)} %get-tuple-element.146.refs_0_, f32[2,256,512]{2,1,0:T(8,128)} %get-tuple-element.157.refs_1_, bf16[2,256,512]{2,1,0:T(8,128)(2,1)} %copy-done.10, bf16[2,256,512]{2,1,0:T(8,128)(2,1)} %copy-done.11, ...), custom_call_target="tpu_custom_call" | custom-call | flops 1000000 | bytes 6291456 | tf_op jit(solution)/shard_map/combine/pallas_call | solution.py:249
  193.1 0.6 add_add_fusion
  (64 shorter events, 0.8 us)
Async XLA Ops:
  0.6 42.2 %copy-start = (bf16[1024,1024]{1,0:T(8,128)(2,1)S(1)}, bf16[1024,1024]{1,0:T(8,128)(2,1)}, u32[]{:S(2)}) copy-start(bf16[1024,1024]{1,0:T(8,128)(2,1)} %param.11) | copy-start | bytes 6291460
  1.4 1.0 copy-start.2
  2.5 1.0 copy-start.3
  3.5 0.7 copy-start.6
  5.4 40.1 %copy-start.7 = (bf16[2,256,1024]{2,1,0:T(8,128)(2,1)}, bf16[2,256,1024]{2,1,0:T(8,128)(2,1)S(1)}, u32[]{:S(2)}) copy-start(bf16[2,256,1024]{2,1,0:T(8,128)(2,1)S(1)} %get-tuple-element.101.own.refs_2_) | copy-start | bytes 3145732
  5.4 23.3 %collective-permute-start = (bf16[2,64,1024]{2,1,0:T(8,128)(2,1)S(1)}, bf16[2,64,1024]{2,1,0:T(8,128)(2,1)S(1)}, u32[]{:S(2)}, u32[]{:S(2)}) collective-permute-start(bf16[2,64,1024]{2,1,0:T(8,128)(2,1)S(1)} %get-tuple-element.91), channel_id=1, source_target_pairs={{0,2},{1,3},{2,4},{3,5},{4,6},{5,7},{6,0},{7,1},{8,10},{9,11},{10,... | collective-permute-start | bytes 786440 | tf_op jit(solution)/shard_map/ppermute | solution.py:281
  6.9 21.7 %collective-permute-start.1 = (bf16[2,64,1024]{2,1,0:T(8,128)(2,1)S(1)}, bf16[2,64,1024]{2,1,0:T(8,128)(2,1)S(1)}, u32[]{:S(2)}, u32[]{:S(2)}) collective-permute-start(bf16[2,64,1024]{2,1,0:T(8,128)(2,1)S(1)} %get-tuple-element.92), channel_id=1, source_target_pairs={{0,4},{1,5},{2,6},{3,7},{4,0},{5,1},{6,2},{7,3},{8,12},{9,13},{10,... | collective-permute-start | bytes 786440 | tf_op jit(solution)/shard_map/ppermute | solution.py:281
  9.7 19.0 %collective-permute-start.2 = (bf16[2,64,1024]{2,1,0:T(8,128)(2,1)S(1)}, bf16[2,64,1024]{2,1,0:T(8,128)(2,1)S(1)}, u32[]{:S(2)}, u32[]{:S(2)}) collective-permute-start(bf16[2,64,1024]{2,1,0:T(8,128)(2,1)S(1)} %get-tuple-element.93), channel_id=1, source_target_pairs={{0,6},{1,7},{2,0},{3,1},{4,2},{5,3},{6,4},{7,5},{8,14},{9,15},{10,... | collective-permute-start | bytes 786440 | tf_op jit(solution)/shard_map/ppermute | solution.py:281
  30.1 26.8 %copy-start.5 = (s32[8]{0:T(128)}, s32[8]{0:T(128)S(1)}, u32[]{:S(2)}) copy-start(s32[8]{0:T(128)S(1)} %get-tuple-element.94.flags) | copy-start | bytes 100
  30.1 1.4 collective-permute-start.3
  32.2 21.3 %collective-permute-start.5 = (bf16[2,256,1024]{2,1,0:T(8,128)(2,1)S(1)}, bf16[2,256,1024]{2,1,0:T(8,128)(2,1)}, u32[]{:S(2)}, u32[]{:S(2)}) collective-permute-start(bf16[2,256,1024]{2,1,0:T(8,128)(2,1)S(1)} %get-tuple-element.101.own.refs_2_), channel_id=1, source_target_pairs={{1,0},{2,1},{3,2},{4,3},{5,4},{6,5},{7,6},{8,7},{9,8},{10,9},{11,1... | collective-permute-start | bytes 3145736 | tf_op jit(solution)/shard_map/ppermute | solution.py:281
  36.1 20.2 %collective-permute-start.4 = (bf16[2,256,1024]{2,1,0:T(8,128)(2,1)S(1)}, bf16[2,256,1024]{2,1,0:T(8,128)(2,1)}, u32[]{:S(2)}, u32[]{:S(2)}) collective-permute-start(bf16[2,256,1024]{2,1,0:T(8,128)(2,1)S(1)} %get-tuple-element.101.own.refs_2_), channel_id=1, source_target_pairs={{0,1},{1,2},{2,3},{3,4},{4,5},{5,6},{6,7},{7,8},{8,9},{9,10},{10,1... | collective-permute-start | bytes 3145736 | tf_op jit(solution)/shard_map/ppermute | solution.py:281
  38.0 15.5 %all-to-all-start.1 = ((bf16[8,8,1024]{2,1,0:T(8,128)(2,1)}), bf16[8,8,1024]{2,1,0:T(8,128)(2,1)S(1)}, u32[]{:S(2)}, u32[]{:S(2)}) async-start(bf16[8,8,1024]{2,1,0:T(8,128)(2,1)} %bitcast.5), calls=%async_computation.1 | async-start | bytes 262144 | tf_op jit(solution)/shard_map/all_to_all | solution.py:289
  56.9 15.9 %all-to-all-start.2 = ((bf16[8,8,1024]{2,1,0:T(8,128)(2,1)}), bf16[8,8,1024]{2,1,0:T(8,128)(2,1)S(1)}, u32[]{:S(2)}, u32[]{:S(2)}) async-start(bf16[8,8,1024]{2,1,0:T(8,128)(2,1)} %broadcast_in_dim.24), calls=%async_computation.2 | async-start | bytes 262144 | tf_op jit(solution)/shard_map/all_to_all | solution.py:289
  72.8 7.7 %collective-permute-start.6 = (bf16[64,1024]{1,0:T(8,128)(2,1)S(1)}, bf16[64,1024]{1,0:T(8,128)(2,1)S(1)}, u32[]{:S(2)}, u32[]{:S(2)}) collective-permute-start(bf16[64,1024]{1,0:T(8,128)(2,1)S(1)} %bitcast.30), channel_id=1, source_target_pairs={{0,2},{1,3},{2,4},{3,5},{4,6},{5,7},{6,0},{7,1},{8,10},{9,11},{10,... | collective-permute-start | bytes 393224 | tf_op jit(solution)/shard_map/ppermute | solution.py:281
  72.9 9.7 %collective-permute-start.8 = (bf16[64,1024]{1,0:T(8,128)(2,1)S(1)}, bf16[64,1024]{1,0:T(8,128)(2,1)S(1)}, u32[]{:S(2)}, u32[]{:S(2)}) collective-permute-start(bf16[64,1024]{1,0:T(8,128)(2,1)S(1)} %bitcast.31), channel_id=1, source_target_pairs={{0,6},{1,7},{2,0},{3,1},{4,2},{5,3},{6,4},{7,5},{8,14},{9,15},{10,... | collective-permute-start | bytes 393224 | tf_op jit(solution)/shard_map/ppermute | solution.py:281
  76.2 6.5 %collective-permute-start.7 = (bf16[64,1024]{1,0:T(8,128)(2,1)S(1)}, bf16[64,1024]{1,0:T(8,128)(2,1)S(1)}, u32[]{:S(2)}, u32[]{:S(2)}) collective-permute-start(bf16[64,1024]{1,0:T(8,128)(2,1)S(1)} %bitcast.32), channel_id=1, source_target_pairs={{0,4},{1,5},{2,6},{3,7},{4,0},{5,1},{6,2},{7,3},{8,12},{9,13},{10,... | collective-permute-start | bytes 393224 | tf_op jit(solution)/shard_map/ppermute | solution.py:281
  82.7 2.2 %copy-start.14 = (bf16[256,1024]{1,0:T(8,128)(2,1)}, bf16[256,1024]{1,0:T(8,128)(2,1)S(1)}, u32[]{:S(2)}) copy-start(bf16[256,1024]{1,0:T(8,128)(2,1)S(1)} %constant_dynamic-update-slice_fusion.half) | copy-start | bytes 1572868
  82.7 2.2 %collective-permute-start.9 = (bf16[256,1024]{1,0:T(8,128)(2,1)S(1)}, bf16[256,1024]{1,0:T(8,128)(2,1)S(1)}, u32[]{:S(2)}, u32[]{:S(2)}) collective-permute-start(bf16[256,1024]{1,0:T(8,128)(2,1)S(1)} %constant_dynamic-update-slice_fusion.half), channel_id=1, source_target_pairs={{0,1},{1,0},{2,3},{3,2},{4,5},{5,4},{6,7},{7,6},{8,9},{9,8},{10,11... | collective-permute-start | bytes 1572872 | tf_op jit(solution)/shard_map/ppermute | solution.py:281
  84.9 0.8 copy-start.15
  101.0 11.0 %collective-permute-start.14 = (bf16[4,8,16,1024]{3,2,1,0:T(8,128)(2,1)}, bf16[4,8,16,1024]{3,2,1,0:T(8,128)(2,1)S(1)}, u32[]{:S(2)}, u32[]{:S(2)}) collective-permute-start(bf16[4,8,16,1024]{3,2,1,0:T(8,128)(2,1)} %get-tuple-element.125), channel_id=1, source_target_pairs={{0,1},{1,0},{2,3},{3,2},{4,5},{5,4},{6,7},{7,6},{8,9},{9,8},{10,11... | collective-permute-start | bytes 3145736 | tf_op jit(solution)/shard_map/ppermute | solution.py:281
  101.2 3.5 %collective-permute-start.10 = (bf16[256,1024]{1,0:T(8,128)(2,1)}, bf16[256,1024]{1,0:T(8,128)(2,1)S(1)}, u32[]{:S(2)}, u32[]{:S(2)}) collective-permute-start(bf16[256,1024]{1,0:T(8,128)(2,1)} %get-tuple-element.113), channel_id=1, source_target_pairs={{0,1},{1,0},{2,3},{3,2},{4,5},{5,4},{6,7},{7,6},{8,9},{9,8},{10,11... | collective-permute-start | bytes 1572872 | tf_op jit(solution)/shard_map/ppermute | solution.py:281
  104.7 1.0 copy-start.4
  105.8 6.3 %copy-start.1 = (f32[4,8,16,1024]{3,2,1,0:T(8,128)S(1)}, f32[4,8,16,1024]{3,2,1,0:T(8,128)}, u32[]{:S(2)}) copy-start(f32[4,8,16,1024]{3,2,1,0:T(8,128)} %get-tuple-element.124.mine) | copy-start | bytes 6291460
  105.9 7.3 %collective-permute-start.11 = (bf16[64,1024]{1,0:T(8,128)(2,1)S(1)}, bf16[64,1024]{1,0:T(8,128)(2,1)S(1)}, u32[]{:S(2)}, u32[]{:S(2)}) collective-permute-start(bf16[64,1024]{1,0:T(8,128)(2,1)S(1)} %get-tuple-element.121), channel_id=1, source_target_pairs={{0,2},{1,3},{2,4},{3,5},{4,6},{5,7},{6,0},{7,1},{8,10},{9,11},{10,... | collective-permute-start | bytes 393224 | tf_op jit(solution)/shard_map/ppermute | solution.py:281
  106.7 9.2 %collective-permute-start.12 = (bf16[64,1024]{1,0:T(8,128)(2,1)S(1)}, bf16[64,1024]{1,0:T(8,128)(2,1)S(1)}, u32[]{:S(2)}, u32[]{:S(2)}) collective-permute-start(bf16[64,1024]{1,0:T(8,128)(2,1)S(1)} %get-tuple-element.122), channel_id=1, source_target_pairs={{0,4},{1,5},{2,6},{3,7},{4,0},{5,1},{6,2},{7,3},{8,12},{9,13},{10,... | collective-permute-start | bytes 393224 | tf_op jit(solution)/shard_map/ppermute | solution.py:281
  109.5 6.7 %collective-permute-start.13 = (bf16[64,1024]{1,0:T(8,128)(2,1)S(1)}, bf16[64,1024]{1,0:T(8,128)(2,1)S(1)}, u32[]{:S(2)}, u32[]{:S(2)}) collective-permute-start(bf16[64,1024]{1,0:T(8,128)(2,1)S(1)} %get-tuple-element.123), channel_id=1, source_target_pairs={{0,6},{1,7},{2,0},{3,1},{4,2},{5,3},{6,4},{7,5},{8,14},{9,15},{10,... | collective-permute-start | bytes 393224 | tf_op jit(solution)/shard_map/ppermute | solution.py:281
  116.9 21.1 %all-to-all-start.3 = ((bf16[8,8,1024]{2,1,0:T(8,128)(2,1)}), bf16[8,8,1024]{2,1,0:T(8,128)(2,1)S(1)}, u32[]{:S(2)}, u32[]{:S(2)}) async-start(bf16[8,8,1024]{2,1,0:T(8,128)(2,1)} %fusion), calls=%async_computation.3 | async-start | bytes 262144 | tf_op jit(solution)/shard_map/all_to_all | solution.py:289
  124.1 14.0 %collective-permute-start.15 = (bf16[8,16,1024]{2,1,0:T(8,128)(2,1)S(1)}, bf16[8,16,1024]{2,1,0:T(8,128)(2,1)S(1)}, u32[]{:S(2)}, u32[]{:S(2)}) collective-permute-start(bf16[8,16,1024]{2,1,0:T(8,128)(2,1)S(1)} %get-tuple-element.149), channel_id=1, source_target_pairs={{0,2},{1,3},{2,4},{3,5},{4,6},{5,7},{6,0},{7,1},{8,10},{9,11},{10,... | collective-permute-start | bytes 786440 | tf_op jit(solution)/shard_map/ppermute | solution.py:281
  124.6 15.0 %collective-permute-start.16 = (bf16[8,16,1024]{2,1,0:T(8,128)(2,1)S(1)}, bf16[8,16,1024]{2,1,0:T(8,128)(2,1)}, u32[]{:S(2)}, u32[]{:S(2)}) collective-permute-start(bf16[8,16,1024]{2,1,0:T(8,128)(2,1)S(1)} %get-tuple-element.150), channel_id=1, source_target_pairs={{0,4},{1,5},{2,6},{3,7},{4,0},{5,1},{6,2},{7,3},{8,12},{9,13},{10,... | collective-permute-start | bytes 786440 | tf_op jit(solution)/shard_map/ppermute | solution.py:281
  128.2 11.3 %collective-permute-start.17 = (bf16[8,16,1024]{2,1,0:T(8,128)(2,1)S(1)}, bf16[8,16,1024]{2,1,0:T(8,128)(2,1)}, u32[]{:S(2)}, u32[]{:S(2)}) collective-permute-start(bf16[8,16,1024]{2,1,0:T(8,128)(2,1)S(1)} %get-tuple-element.151), channel_id=1, source_target_pairs={{0,6},{1,7},{2,0},{3,1},{4,2},{5,3},{6,4},{7,5},{8,14},{9,15},{10,... | collective-permute-start | bytes 786440 | tf_op jit(solution)/shard_map/ppermute | solution.py:281
  141.5 23.9 %all-to-all-start.4 = ((bf16[8,24,1024]{2,1,0:T(8,128)(2,1)}), bf16[8,24,1024]{2,1,0:T(8,128)(2,1)S(1)}, u32[]{:S(2)}, u32[]{:S(2)}) async-start(bf16[8,24,1024]{2,1,0:T(8,128)(2,1)} %pad_maximum_fusion.1), calls=%async_computation.4 | async-start | bytes 786432 | tf_op jit(solution)/shard_map/all_to_all | solution.py:289
  148.7 14.6 %collective-permute-start.18 = (bf16[2,256,512]{2,1,0:T(8,128)(2,1)}, bf16[2,256,512]{2,1,0:T(8,128)(2,1)S(1)}, u32[]{:S(2)}, u32[]{:S(2)}) collective-permute-start(bf16[2,256,512]{2,1,0:T(8,128)(2,1)} %get-tuple-element.155), channel_id=1, source_target_pairs={{1,0},{2,1},{3,2},{4,3},{5,4},{6,5},{7,6},{8,7},{9,8},{10,9},{11,1... | collective-permute-start | bytes 1572872 | tf_op jit(solution)/shard_map/ppermute | solution.py:281
  151.5 14.0 %collective-permute-start.19 = (bf16[2,256,512]{2,1,0:T(8,128)(2,1)}, bf16[2,256,512]{2,1,0:T(8,128)(2,1)S(1)}, u32[]{:S(2)}, u32[]{:S(2)}) collective-permute-start(bf16[2,256,512]{2,1,0:T(8,128)(2,1)} %get-tuple-element.156), channel_id=1, source_target_pairs={{0,1},{1,2},{2,3},{3,4},{4,5},{5,6},{6,7},{7,8},{8,9},{9,10},{10,1... | collective-permute-start | bytes 1572872 | tf_op jit(solution)/shard_map/ppermute | solution.py:281
  163.3 23.9 %copy-start.9 = (bf16[2,256,512]{2,1,0:T(8,128)(2,1)}, bf16[2,256,512]{2,1,0:T(8,128)(2,1)S(1)}, u32[]{:S(2)}) copy-start(bf16[2,256,512]{2,1,0:T(8,128)(2,1)S(1)} %collective-permute-done.18.refs_4_) | copy-start | bytes 1572868
  165.5 21.8 %copy-start.10 = (bf16[2,256,512]{2,1,0:T(8,128)(2,1)}, bf16[2,256,512]{2,1,0:T(8,128)(2,1)S(1)}, u32[]{:S(2)}) copy-start(bf16[2,256,512]{2,1,0:T(8,128)(2,1)S(1)} %collective-permute-done.19.refs_2_) | copy-start | bytes 1572868
  165.5 9.8 %collective-permute-start.24 = (bf16[64,1024]{1,0:T(8,128)(2,1)S(1)}, bf16[64,1024]{1,0:T(8,128)(2,1)S(1)}, u32[]{:S(2)}, u32[]{:S(2)}) collective-permute-start(bf16[64,1024]{1,0:T(8,128)(2,1)S(1)} %slice_bitcast_fusion), channel_id=1, source_target_pairs={{0,6},{1,7},{2,0},{3,1},{4,2},{5,3},{6,4},{7,5},{8,14},{9,15},{10,... | collective-permute-start | bytes 393224 | tf_op jit(solution)/shard_map/ppermute | solution.py:281
  165.6 9.7 %collective-permute-start.23 = (bf16[64,1024]{1,0:T(8,128)(2,1)S(1)}, bf16[64,1024]{1,0:T(8,128)(2,1)S(1)}, u32[]{:S(2)}, u32[]{:S(2)}) collective-permute-start(bf16[64,1024]{1,0:T(8,128)(2,1)S(1)} %slice_bitcast_fusion), channel_id=1, source_target_pairs={{0,4},{1,5},{2,6},{3,7},{4,0},{5,1},{6,2},{7,3},{8,12},{9,13},{10,... | collective-permute-start | bytes 393224 | tf_op jit(solution)/shard_map/ppermute | solution.py:281
  165.8 16.2 %collective-permute-start.22 = (bf16[64,1024]{1,0:T(8,128)(2,1)S(1)}, bf16[64,1024]{1,0:T(8,128)(2,1)S(1)}, u32[]{:S(2)}, u32[]{:S(2)}) collective-permute-start(bf16[64,1024]{1,0:T(8,128)(2,1)S(1)} %slice_bitcast_fusion), channel_id=1, source_target_pairs={{0,2},{1,3},{2,4},{3,5},{4,6},{5,7},{6,0},{7,1},{8,10},{9,11},{10,... | collective-permute-start | bytes 393224 | tf_op jit(solution)/shard_map/ppermute | solution.py:281
  167.6 17.7 %collective-permute-start.20 = (bf16[2,256,512]{2,1,0:T(8,128)(2,1)}, bf16[2,256,512]{2,1,0:T(8,128)(2,1)S(1)}, u32[]{:S(2)}, u32[]{:S(2)}) collective-permute-start(bf16[2,256,512]{2,1,0:T(8,128)(2,1)} %get-tuple-element.159), channel_id=1, source_target_pairs={{0,1},{1,2},{2,3},{3,4},{4,5},{5,6},{6,7},{7,8},{8,9},{9,10},{10,1... | collective-permute-start | bytes 1572872 | tf_op jit(solution)/shard_map/ppermute | solution.py:281
  170.3 16.9 %collective-permute-start.21 = (bf16[2,256,512]{2,1,0:T(8,128)(2,1)}, bf16[2,256,512]{2,1,0:T(8,128)(2,1)S(1)}, u32[]{:S(2)}, u32[]{:S(2)}) collective-permute-start(bf16[2,256,512]{2,1,0:T(8,128)(2,1)} %get-tuple-element.161), channel_id=1, source_target_pairs={{1,0},{2,1},{3,2},{4,3},{5,4},{6,5},{7,6},{8,7},{9,8},{10,9},{11,1... | collective-permute-start | bytes 1572872 | tf_op jit(solution)/shard_map/ppermute | solution.py:281
  182.0 5.3 %copy-start.8 = (bf16[256,1024]{1,0:T(8,128)(2,1)}, bf16[256,1024]{1,0:T(8,128)(2,1)S(1)}, u32[]{:S(2)}) copy-start(bf16[256,1024]{1,0:T(8,128)(2,1)S(1)} %pad_maximum_fusion.refs_6_) | copy-start | bytes 1572868
  182.0 5.2 %collective-permute-start.25 = (bf16[256,1024]{1,0:T(8,128)(2,1)S(1)}, bf16[256,1024]{1,0:T(8,128)(2,1)S(1)}, u32[]{:S(2)}, u32[]{:S(2)}) collective-permute-start(bf16[256,1024]{1,0:T(8,128)(2,1)S(1)} %pad_maximum_fusion.refs_6_), channel_id=1, source_target_pairs={{0,1},{1,0},{2,3},{3,2},{4,5},{5,4},{6,7},{7,6},{8,9},{9,8},{10,11... | collective-permute-start | bytes 1572872 | tf_op jit(solution)/shard_map/ppermute | solution.py:281
  182.2 10.9 %collective-permute-start.28 = (f32[16,1024]{1,0:T(8,128)S(1)}, f32[16,1024]{1,0:T(8,128)S(1)}, u32[]{:S(2)}, u32[]{:S(2)}) collective-permute-start(f32[16,1024]{1,0:T(8,128)S(1)} %convert_reduce_fusion), channel_id=1, source_target_pairs={{0,192},{64,0},{128,64},{192,128},{1,193},{65,1},{129,65},{193,129... | collective-permute-start | bytes 196616 | tf_op jit(solution)/shard_map/ppermute | solution.py:430
  182.8 10.3 %collective-permute-start.27 = (f32[16,1024]{1,0:T(8,128)S(1)}, f32[16,1024]{1,0:T(8,128)S(1)}, u32[]{:S(2)}, u32[]{:S(2)}) collective-permute-start(f32[16,1024]{1,0:T(8,128)S(1)} %convert_reduce_fusion), channel_id=1, source_target_pairs={{0,128},{64,192},{128,0},{192,64},{1,129},{65,193},{129,1},{193,65... | collective-permute-start | bytes 196616 | tf_op jit(solution)/shard_map/ppermute | solution.py:430
  185.4 1.9 copy-start.11
  185.4 7.7 %collective-permute-start.26 = (f32[16,1024]{1,0:T(8,128)S(1)}, f32[16,1024]{1,0:T(8,128)S(1)}, u32[]{:S(2)}, u32[]{:S(2)}) collective-permute-start(f32[16,1024]{1,0:T(8,128)S(1)} %convert_reduce_fusion), channel_id=1, source_target_pairs={{0,64},{64,128},{128,192},{192,0},{1,65},{65,129},{129,193},{193,1... | collective-permute-start | bytes 196616 | tf_op jit(solution)/shard_map/ppermute | solution.py:430
  187.2 0.8 copy-start.12
  188.0 0.8 copy-start.13

commit v3 on v2

--- a/solution.py
+++ b/solution.py
@@ -30,14 +30,14 @@
     return [lane < HEAD_DIM, lane >= HEAD_DIM]
 
 
-def local_forward(flags, q, own, left, right, m_out, l_out, o_out):
+def local_forward(flags, q, own, core, chip, m_out, l_out, o_out):
     seen = [None, flags[0] > 0, flags[1] > 0]
     for g in range(SPAN // 128):
         cols = pl.ds(g * 128, 128)
         queries = q[:, cols] * 0.125
         masks = half_masks(queries.shape)
-        keys = [ref[0, :, cols] for ref in (own, left, right)]
-        vals = [ref[1, :, cols] for ref in (own, left, right)]
+        keys = [ref[0, :, cols] for ref in (own, core, chip)]
+        vals = [ref[1, :, cols] for ref in (own, core, chip)]
         tops, sums, mixes = [], [], []
         for mask in masks:
             part = jnp.where(mask, queries, 0).astype(BF16)
@@ -111,20 +111,22 @@
         other_out[:, cols] = jnp.where(first, dv, dk).astype(BF16)
 
 
-def local_backward(flags, q, d, own, left, right, lse_in, cen_in, dq_in, dq_out, own_out, left_out, right_out):
+def local_backward(
+    flags, q, d, own, core, chip, lse_in, cen_in, dq_in, dq_out, own_out, core_out, chip_out
+):
     seen = [None, flags[0] > 0, flags[1] > 0]
     for g in range(SPAN // 128):
         cols = pl.ds(g * 128, 128)
         queries = q[:, cols] * 0.125
         grads = d[:, cols]
         masks = half_masks(queries.shape)
-        keys = [ref[0, :, cols] for ref in (own, left, right)]
-        vals = [ref[1, :, cols] for ref in (own, left, right)]
+        keys = [ref[0, :, cols] for ref in (own, core, chip)]
+        vals = [ref[1, :, cols] for ref in (own, core, chip)]
         lse, cens = lse_in[:, cols], cen_in[:, cols]
         parts = [jnp.where(m, queries, 0).astype(BF16) for m in masks]
         gparts = [jnp.where(m, grads, 0).astype(BF16) for m in masks]
         dq = [0.0, 0.0]
-        for key, val, flag, out in zip(keys, vals, seen, (own_out, left_out, right_out)):
+        for key, val, flag, out in zip(keys, vals, seen, (own_out, core_out, chip_out)):
             dk = dv = 0.0
             for h in range(2):
                 at = slice(h * HEAD_DIM, h * HEAD_DIM + 1)
@@ -156,8 +158,9 @@
         far = jnp.where(used & jnp.logical_not(beside), 1, far)
         hub = jnp.where(used & jnp.logical_not(beside), entry, hub)
     x = region // NC % NX
-    flags_out[0] = left
-    flags_out[1] = right
+    lower = region % NC == 0
+    flags_out[0] = jnp.where(lower, right, left)
+    flags_out[1] = jnp.where(lower, left, right)
     flags_out[2] = region % NC
     flags_out[3] = far
     flags_out[4] = x
@@ -174,9 +177,15 @@
         out[1] = value[rows, :]
 
 
-def add_pieces(mine, theirs, *pieces):
-    for out, k in zip(pieces, range(NX)):
-        out[...] = (mine[k].astype(F32) + theirs[k].astype(F32)).astype(BF16)
+def add_pieces(flags, mine, theirs, kept, turned, *pieces):
+    quarter = mine.shape[1]
+    for k, out in enumerate(pieces):
+        spot = (flags[4] + k) % NX
+        far = mine[spot].astype(F32) + theirs[spot].astype(F32)
+        out[pl.ds(0, quarter), :] = far.astype(BF16)
+        slab = kept[k] + turned[k].astype(F32)
+        slab = slab.reshape(-1, slab.shape[-1]).astype(BF16)
+        out[pl.ds(quarter, slab.shape[0]), :] = slab
 
 
 def simple(body, ins, outs, name, scalars=0):
@@ -193,7 +202,7 @@
 
 
 def local_backward_into(flags, *refs):
-    local_backward(flags, *refs[:8], *refs[9:])
+    local_backward(flags, *refs[:8], *refs[12:])
 
 
 def choose(flags, ids, own, one, two, three, mine_out, other_out, flags_out):
@@ -213,28 +222,18 @@
             other_out[...] = ref[1 - c]
 
 
-def combine(flags, *refs):
-    owns, lefts, rights = refs[0:2], refs[2:4], refs[4:6]
-    far_half, far_rest, key_out, value_out = refs[6:]
+def combine(flags, own, from_core, from_chip, far_half, far_rest, key_out, value_out):
     first = flags[2] == 0
     at_hub = flags[5] > 0
-    tall = key_out.shape[0]
-    quarter = far_half.shape[0] // NX
-    for j in range(tall // quarter):
-        spot = pl.program_id(0) * (tall // quarter) + j
-        begin = pl.multiple_of((flags[4] - spot + NX) % NX * quarter, quarter)
-        rows = pl.ds(j * quarter, quarter)
-        at = 0
-        for own, left, right in zip(owns, lefts, rights):
-            cols = pl.ds(at, own.shape[-1])
-            at += own.shape[-1]
-            total = own[:, rows] + left[:, rows].astype(F32) + right[:, rows].astype(F32)
-            half = far_half[pl.ds(begin, quarter), cols].astype(F32)
-            rest = far_rest[pl.ds(begin, quarter), cols].astype(F32)
-            far_key = jnp.where(first, half, rest)
-            far_value = jnp.where(first, rest, half)
-            key_out[rows, cols] = (total[0] + jnp.where(at_hub, far_key, 0.0)).astype(BF16)
-            value_out[rows, cols] = (total[1] + jnp.where(at_hub, far_value, 0.0)).astype(BF16)
+    tall = 64
+    for begin in range(0, key_out.shape[0], tall):
+        rows = pl.ds(begin, tall)
+        total = own[:, rows] + from_core[:, rows].astype(F32) + from_chip[:, rows].astype(F32)
+        half, rest = far_half[rows, :].astype(F32), far_rest[rows, :].astype(F32)
+        far_key = jnp.where(first, half, rest)
+        far_value = jnp.where(first, rest, half)
+        key_out[rows, :] = (total[0] + jnp.where(at_hub, far_key, 0.0)).astype(BF16)
+        value_out[rows, :] = (total[1] + jnp.where(at_hub, far_value, 0.0)).astype(BF16)
 
 
 def across(shape, start=0):
@@ -289,23 +288,24 @@
     return lax.all_to_all(value, "region", 0, 0, axis_index_groups=Z_GROUPS, tiled=True)
 
 
-def gather_z(value):
-    out = swap_z(jnp.broadcast_to(value[None], (NZ,) + value.shape))
+PLANE_GROUPS = [[place(z, x, c) for x in range(NX) for z in range(NZ)] for c in range(NC)]
+
+
+def gather_plane(value):
+    count = NZ * NX
+    out = lax.all_to_all(
+        jnp.broadcast_to(value[None], (count,) + value.shape),
+        "region",
+        0,
+        0,
+        axis_index_groups=PLANE_GROUPS,
+        tiled=True,
+    )
     return out.reshape((-1,) + value.shape[1:])
 
 
-def gather_x(value):
-    return jnp.concatenate([value] + [send(value, hop(dx=k)) for k in range(1, NX)])
-
-
-def sum_x(pieces):
-    got = [pieces[0]] + [send(pieces[k], hop(dx=k)) for k in range(1, NX)]
-    return sum(g.astype(F32) for g in got)
-
-
-def shifted(value, step):
-    last = NZ * NX * NC
-    return send(value, [(i, i + step) for i in range(last) if 0 <= i + step < last])
+CORE = hop(dc=1)
+CHIP = [p for r in range(1, NZ * NX * NC - 1, NC) for p in ((r, r + 1), (r + 1, r))]
 
 
 def on_device(query, key_in, value, d_out, out_weight, attended, counts):
@@ -335,7 +335,7 @@
     )
     part = jnp.where(flags[7] > 0, mine, send(other, hop(dc=1)))
     part, pair = lax.optimization_barrier((part, pair))
-    near = [pair, shifted(pair, 1), shifted(pair, -1)]
+    near = [pair, send(pair, CORE), send(pair, CHIP)]
     share = pick(swap_z(part.reshape(NZ, eighth, width)), flags[6])
     share, near = lax.optimization_barrier((share, near))
 
@@ -352,8 +352,7 @@
     d_attn = lax.dot_general(
         grad_out, out_weight, (((1,), (1,)), ((), ())), preferred_element_type=F32
     ).astype(BF16)
-    spread, stats, d_attn = lax.optimization_barrier((gather_z(share), stats, d_attn))
-    half = gather_x(spread)
+    half, stats, d_attn = lax.optimization_barrier((gather_plane(share), stats, d_attn))
     rest = send(half, hop(dc=1))
 
     slab = width // (NZ * NX * NC)
@@ -371,82 +370,66 @@
         "hub_block",
     )
 
+    received = send(far_other, CORE)
+    turned = send(sent, CORE)
+    layer = nn(attn, out_weight).astype(BF16)
+    received, turned, layer = lax.optimization_barrier((received, turned, layer))
     stacked = (NX, quarter, width)
     pieces = simple(
         add_pieces,
-        [far_mine.reshape(stacked), send(far_other, hop(dc=1)).reshape(stacked)],
-        [((quarter, width), BF16)] * NX,
+        [flags, far_mine.reshape(stacked), received.reshape(stacked), kept, turned],
+        [((quarter + NZ * slab, width), BF16)] * NX,
         "add_pieces",
-    )
-    pieces = [pieces[-k % NX] for k in range(NX)]
-    turned = send(sent, hop(dc=1))
-    pieces, kept, attn = lax.optimization_barrier((pieces, kept, attn))
-    slabs = simple(add_pieces, [kept, turned], [((NZ, slab, width), BF16)] * NX, "add_slabs")
-    layer = nn(attn, out_weight).astype(BF16)
+        1,
+    )
+    pieces, lse = lax.optimization_barrier((pieces, lse))
     pieces = [pieces[0]] + [send(pieces[k], hop(dx=k)) for k in range(1, NX)]
-    pieces, slabs, layer, lse = lax.optimization_barrier((pieces, slabs, layer, lse))
+
+    steps = width // SPAN // 2
+    double = (2, rows, width)
+
+    def backward(lse, done, begin):
+        ins = [(a, across(a.shape, begin)) for a in (query, d_attn, *near, lse, cen, dq_far)]
+        outs = [(flat, BF16), (double, F32), (double, BF16), (double, BF16)]
+        return call(
+            local_backward_into if done else local_backward,
+            flags,
+            ins + [(a, pl.BlockSpec(memory_space=pl.ANY)) for a in done],
+            [(s, t, across(s, begin)) for s, t in outs],
+            steps,
+            int(4e9),
+            "local_backward",
+            {1 + len(ins) + i: i for i in range(len(done))},
+        )
+
+    grads = backward(lse, [], 0)
+    pieces, grads, lse = lax.optimization_barrier((pieces, grads, lse))
     summed = sum(p.astype(F32) for p in pieces).astype(BF16)
-
-    def backward(lse, d_query, begin, steps):
-        inputs = (query, d_attn, *near, lse, cen, dq_far)
-        ins = [(a, across(a.shape, begin)) for a in inputs]
-        wide = (2, rows, steps * SPAN)
-        body, aliases = local_backward, {}
-        if d_query is not None:
-            body, aliases = local_backward_into, {1 + len(ins): 0}
-            ins = ins + [(d_query, pl.BlockSpec(memory_space=pl.ANY))]
-        return call(
-            body,
-            flags,
-            ins,
-            [(flat, BF16, across(flat, begin))]
-            + [(wide, F32, None), (wide, BF16, None), (wide, BF16, None)],
-            steps,
-            int(2e9) * steps,
-            "local_backward",
-            aliases,
-        )
-
-    d_query, *first_part = backward(lse, None, 0, 2)
-    slabs = [slabs[0]] + [send(slabs[k], hop(dx=k)) for k in range(1, NX)]
-    summed, first_part, lse = lax.optimization_barrier(
-        (swap_z(summed.reshape(NZ, eighth, width)), first_part, lse)
-    )
-    total = jnp.sum(summed.astype(F32), axis=0).astype(BF16)
-    weight = sum(p.astype(F32) for p in slabs).astype(BF16)
-    sides = [shifted(first_part[1], -1), shifted(first_part[2], 1)]
-    d_query, *second_part = backward(lse, d_query, 2, 2)
-    both = jnp.concatenate([jnp.broadcast_to(total[None], (NZ,) + total.shape), weight], axis=1)
-    both, second_part, sides = lax.optimization_barrier((swap_z(both), second_part, sides))
-    far_half = gather_x(both[:, :eighth].reshape(quarter, width))
-    weight, far_half = lax.optimization_barrier((both[:, eighth:], far_half))
-    far_rest = send(far_half, hop(dc=1))
-    weight = jnp.sum(weight.astype(F32), axis=0)
-    parts = [first_part, second_part]
-    rights = [sides[0], shifted(second_part[1], -1)]
-    lefts = [sides[1], shifted(second_part[2], 1)]
+    both = [summed[:quarter].reshape(NZ, eighth, width), summed[quarter:].reshape(NZ, slab, width)]
+    both = swap_z(jnp.concatenate(both, axis=1))
+    grads = backward(lse, grads, steps)
+    both, grads = lax.optimization_barrier((both, grads))
+    d_query, own, to_core, to_chip = grads
+    total = jnp.sum(both[:, :eighth].astype(F32), axis=0).astype(BF16)
+    weight = jnp.sum(both[:, eighth:].astype(F32), axis=0)
+
+    far_half = gather_plane(total)
+    from_chip = send(to_chip, CHIP)
+    from_core = send(to_core, CORE)
     dp = lax.axis_size("dp")
     shares = [
         lax.ppermute(weight, "dp", [(i, (i + k) % dp) for i in range(dp)]) for k in range(1, dp)
     ]
-
-    tall = rows // 2
-
-    def pair_block(a):
-        return pl.BlockSpec((2, tall, a.shape[-1]), lambda i, flags: (0, i, 0))
-
-    d_key, d_value = call(
+    far_half, shares, from_chip = lax.optimization_barrier((far_half, shares, from_chip))
+    d_weight = weight + sum(shares)
+    far_rest = send(far_half, CORE)
+    d_key, d_value = simple(
         combine,
-        flags,
-        [(a, pair_block(a)) for a in (*[p[0] for p in parts], *lefts, *rights)]
-        + [(a, whole) for a in (far_half, far_rest)],
-        [(flat, BF16, pl.BlockSpec((tall, width), lambda i, flags: (i, 0)))] * 2,
-        2,
-        int(1e6),
+        [flags, own, from_core, from_chip, far_half, far_rest],
+        [(flat, BF16)] * 2,
         "combine",
-    )
-    d_key, shares = lax.optimization_barrier((d_key, shares))
-    d_weight = weight + sum(shares)
+        1,
+    )
     return layer[None], d_query[None], d_key[None], d_value[None], d_weight
 
 

time: 195 us -> 182 us (0.933)
  the two profiles are of different devices: /device:TPU:40 before, /device:TPU:1 now
where the time goes in v3:
time: 182 us; the launch traced here: 181 us
  Pallas kernels  52 us (29%)
  starting transfers between devices  50.9 us (28%)
  waiting for transfers between devices  39.9 us (22%)
  blocking collectives  19.7 us (11%)
  local copies, waits for them, and re-layouts  7.47 us (4%)
  between operations  4.25 us (2%)
  matrix products  4.18 us (2%)
  other arithmetic  2.42 us (1%)
    pallas_call x4, Pallas kernels, call(): pl.pallas_call(body, grid_spec=pltpu.PrefetchScalarGridSpec(num_scalar_pr...  45 us
    ppermute x15, starting transfers between devices, send(): return lax.ppermute(value, 'region', pairs)  23 us
    all_to_all x1, blocking collectives, on_device(): ids = lax.all_to_all(ids, 'region', 0, 0, tiled=True)  19.7 us
    all_to_all x2, waiting for transfers between devices, gather_plane(): lax.all_to_all(jnp.broadcast_to(value[None], (count,) + value.shape), 're...  16.6 us
    all_to_all x2, starting transfers between devices, gather_plane(): lax.all_to_all(jnp.broadcast_to(value[None], (count,) + value.shape), 're...  15.2 us
    ppermute x15, waiting for transfers between devices, send(): return lax.ppermute(value, 'region', pairs)  12.5 us
    all_to_all x2, waiting for transfers between devices, swap_z(): lax.all_to_all(value, 'region', 0, 0, axis_index_groups=Z_GROUPS, tiled=T...  8.42 us
    all_to_all x2, starting transfers between devices, swap_z(): lax.all_to_all(value, 'region', 0, 0, axis_index_groups=Z_GROUPS, tiled=T...  7.63 us
  transfers between devices with their start and end apart: 22, of which 12 were waited for; matrix products, arithmetic and copies ran while one was open for 3% of the time, Pallas kernels for 16%

profile of v3, /device:TPU:1, one launch (start us, length us, event | category | flops | bytes accessed | tf_op | source)
XLA Modules:
  0.0 180.9 jit_solution(1320759488028153465)
XLA Ops:
  0.6 0.0 copy-start
  1.5 1.0 copy-done.4
  2.5 1.0 copy-done.5
  3.5 0.7 copy-done.9
  4.2 1.7 prepare.1
  5.9 2.1 %collective-permute-start = (bf16[2,64,1024]{2,1,0:T(8,128)(2,1)S(1)}, bf16[2,64,1024]{2,1,0:T(8,128)(2,1)S(1)}, u32[]{:S(2)}, u32[]{:S(2)}) collective-permute-start(bf16[2,64,1024]{2,1,0:T(8,128)(2,1)S(1)} %get-tuple-element.81), channel_id=1, source_target_pairs={{0,2},{1,3},{2,4},{3,5},{4,6},{5,7},{6,0},{7,1},{8,10},{9,11},{10,... | collective-permute-start | bytes 786440 | tf_op jit(solution)/shard_map/ppermute | solution.py:280
  8.0 2.5 %collective-permute-start.1 = (bf16[2,64,1024]{2,1,0:T(8,128)(2,1)S(1)}, bf16[2,64,1024]{2,1,0:T(8,128)(2,1)S(1)}, u32[]{:S(2)}, u32[]{:S(2)}) collective-permute-start(bf16[2,64,1024]{2,1,0:T(8,128)(2,1)S(1)} %get-tuple-element.82), channel_id=1, source_target_pairs={{0,4},{1,5},{2,6},{3,7},{4,0},{5,1},{6,2},{7,3},{8,12},{9,13},{10,... | collective-permute-start | bytes 786440 | tf_op jit(solution)/shard_map/ppermute | solution.py:280
  10.5 1.2 collective-permute-start.2
  11.6 19.7 %all_to_all.25.ids = s32[64,1,128]{2,1,0:T(1,128)S(1)} all-to-all(s32[64,1,128]{2,1,0:T(1,128)S(1)} %get-tuple-element.79), channel_id=1, replica_groups=mesh['dp'=4,'region'=64] {'region'}, dimensions={0} | all-to-all | bytes 65536 | tf_op jit(solution)/shard_map/all_to_all | solution.py:328
  31.3 0.0 collective-permute-done.one
  31.4 0.0 collective-permute-done.1.two
  31.4 0.0 collective-permute-done.2.three
  31.4 1.4 choose.1
  32.8 0.8 collective-permute-start.3
  33.6 0.6 fusion.1
  34.8 0.0 collective-permute-done.3
  34.8 0.7 broadcast_select_fusion
  35.5 0.1 collective-permute-start.4
  35.6 2.5 %collective-permute-start.5 = (bf16[2,256,1024]{2,1,0:T(8,128)(2,1)}, bf16[2,256,1024]{2,1,0:T(8,128)(2,1)}, u32[]{:S(2)}, u32[]{:S(2)}) collective-permute-start(bf16[2,256,1024]{2,1,0:T(8,128)(2,1)} %get-tuple-element.91.own.refs_2_), channel_id=1, source_target_pairs={{1,2},{2,1},{3,4},{4,3},{5,6},{6,5},{7,8},{8,7},{9,10},{10,9},{11,... | collective-permute-start | bytes 3145736 | tf_op jit(solution)/shard_map/ppermute | solution.py:280
  38.1 3.4 %all-to-all-start.1 = ((bf16[8,8,1024]{2,1,0:T(8,128)(2,1)}), bf16[8,8,1024]{2,1,0:T(8,128)(2,1)S(1)}, u32[]{:S(2)}, u32[]{:S(2)}) async-start(bf16[8,8,1024]{2,1,0:T(8,128)(2,1)} %bitcast.5), calls=%async_computation.1 | async-start | bytes 262144 | tf_op jit(solution)/shard_map/all_to_all | solution.py:288
  43.4 5.9 %all-to-all-done.1 = bf16[8,8,1024]{2,1,0:T(8,128)(2,1)S(1)} async-done(((bf16[8,8,1024]{2,1,0:T(8,128)(2,1)}), bf16[8,8,1024]{2,1,0:T(8,128)(2,1)S(1)}, u32[]{:S(2)}, u32[]{:S(2)}) %all-to-all-start.1) | async-done | bytes 131104 | tf_op jit(solution)/shard_map/all_to_all | solution.py:288
  49.3 2.7 %collective-permute-done.5.chip.refs_4_ = bf16[2,256,1024]{2,1,0:T(8,128)(2,1)} collective-permute-done((bf16[2,256,1024]{2,1,0:T(8,128)(2,1)}, bf16[2,256,1024]{2,1,0:T(8,128)(2,1)}, u32[]{:S(2)}, u32[]{:S(2)}) %collective-permute-start.5) | collective-permute-done | bytes 1048608 | tf_op jit(solution)/shard_map/ppermute | solution.py:280
  52.0 0.9 broadcast_in_dim.24
  52.9 10.2 %all-to-all-start.2 = ((bf16[32,8,1024]{2,1,0:T(8,128)(2,1)}), bf16[32,8,1024]{2,1,0:T(8,128)(2,1)S(1)}, u32[]{:S(2)}, u32[]{:S(2)}) async-start(bf16[32,8,1024]{2,1,0:T(8,128)(2,1)} %broadcast_in_dim.24), calls=%async_computation.2 | async-start | bytes 1048576 | tf_op jit(solution)/shard_map/all_to_all | solution.py:296
  63.1 1.6 convolution_convert_fusion.1.d.refs_1_
  64.7 9.8 %local_forward.1 = (f32[256,1024]{1,0:T(8,128)}, f32[256,1024]{1,0:T(8,128)}, f32[256,1024]{1,0:T(8,128)}) custom-call(s32[8]{0:T(128)} %copy-done.6, bf16[256,1024]{1,0:T(8,128)(2,1)} %bitcast.36, bf16[2,256,1024]{2,1,0:T(8,128)(2,1)} %get-tuple-element.91.own.refs_2_, bf16[2,256,1024]{2,1,0:T(8,128)(2,1)} %collective-permute-done.4.core.refs_3_, ...), custom_call_target="tpu_custom_call" | custom-call | flops 5000000000 | bytes 6815744 | tf_op jit(solution)/shard_map/local_forward/pallas_call | solution.py:248
  74.5 5.4 %all-to-all-done.2 = bf16[32,8,1024]{2,1,0:T(8,128)(2,1)S(1)} async-done(((bf16[32,8,1024]{2,1,0:T(8,128)(2,1)}), bf16[32,8,1024]{2,1,0:T(8,128)(2,1)S(1)}, u32[]{:S(2)}, u32[]{:S(2)}) %all-to-all-start.2) | async-done | bytes 524320 | tf_op jit(solution)/shard_map/all_to_all | solution.py:296
  79.9 0.6 collective-permute-start.6
  80.5 1.5 collective-permute-done.6.rest
  82.1 0.8 copy-done.12
  82.9 15.4 %hub_block.1 = (bf16[256,1024]{1,0:T(8,128)(2,1)}, f32[256,1024]{1,0:T(8,128)}, f32[256,1024]{1,0:T(8,128)}, f32[256,1024]{1,0:T(8,128)}, bf16[256,1024]{1,0:T(8...) custom-call(s32[8]{0:T(128)} %copy-done.6, ...), custom_call_target="tpu_custom_call" | custom-call | flops 8999999488 | bytes 13631488 | tf_op jit(solution)/shard_map/hub_block/pallas_call | solution.py:248
  98.3 0.5 collective-permute-start.8
  98.8 0.3 collective-permute-start.7
  99.0 2.6 %convolution_convert_fusion = bf16[256,1024]{1,0:T(8,128)(2,1)} fusion(bf16[256,1024]{1,0:T(8,128)(2,1)} %get-tuple-element.104, bf16[1024,1024]{1,0:T(8,128)(2,1)S(1)} %copy-done), kind=kOutput, calls=%fused_computation | convolution fusion | flops 537133056 | bytes 3145728 | tf_op jit(solution)/shard_map/dot_general | solution.py:25
  101.6 0.4 collective-permute-done.7
  102.0 0.8 add_pieces.1
  102.9 0.1 collective-permute-start.9
  103.0 1.9 %collective-permute-start.10 = (bf16[192,1024]{1,0:T(8,128)(2,1)S(1)}, bf16[192,1024]{1,0:T(8,128)(2,1)S(1)}, u32[]{:S(2)}, u32[]{:S(2)}) collective-permute-start(bf16[192,1024]{1,0:T(8,128)(2,1)S(1)} %get-tuple-element.117), channel_id=1, source_target_pairs={{0,4},{1,5},{2,6},{3,7},{4,0},{5,1},{6,2},{7,3},{8,12},{9,13},{10,... | collective-permute-start | bytes 1179656 | tf_op jit(solution)/shard_map/ppermute | solution.py:280
  104.9 1.4 collective-permute-start.11
  106.3 9.9 %local_backward.2 = (bf16[256,1024]{1,0:T(8,128)(2,1)}, f32[2,256,1024]{2,1,0:T(8,128)}, bf16[2,256,1024]{2,1,0:T(8,128)(2,1)}, bf16[2,256,1024]{2,1,0:T(8,128)(2,1)}) custom-call(s32[8]{0:T(128)} %copy-done.6, bf16[256,1024]{1,0:T(8,128)(2,1)} %bitcast.38, bf16[256,1024]{1,0:T(8,128)(2,1)} %convolution_convert_fusion.1.d.refs_1_, ...), custom_call_target="tpu_custom_call" | custom-call | flops 4000000000 | bytes 12058624 | tf_op jit(solution)/shard_map/local_backward/pallas_call | solution.py:248
  116.2 6.0 %collective-permute-done.10 = bf16[192,1024]{1,0:T(8,128)(2,1)S(1)} collective-permute-done((bf16[192,1024]{1,0:T(8,128)(2,1)S(1)}, bf16[192,1024]{1,0:T(8,128)(2,1)S(1)}, u32[]{:S(2)}, u32[]{:S(2)}) %collective-permute-start.10) | collective-permute-done | bytes 393248 | tf_op jit(solution)/shard_map/ppermute | solution.py:280
  122.2 1.0 collective-permute-done.11
  123.2 0.3 add_convert_fusion
  123.5 0.8 pad_maximum_fusion
  124.3 4.2 %all-to-all-start.3 = ((bf16[8,24,1024]{2,1,0:T(8,128)(2,1)}), bf16[8,24,1024]{2,1,0:T(8,128)(2,1)S(1)}, u32[]{:S(2)}, u32[]{:S(2)}) async-start(bf16[8,24,1024]{2,1,0:T(8,128)(2,1)} %pad_maximum_fusion), calls=%async_computation.3 | async-start | bytes 786432 | tf_op jit(solution)/shard_map/all_to_all | solution.py:288
  128.5 9.9 %local_backward.3 = (bf16[256,1024]{1,0:T(8,128)(2,1)}, f32[2,256,1024]{2,1,0:T(8,128)}, bf16[2,256,1024]{2,1,0:T(8,128)(2,1)}, bf16[2,256,1024]{2,1,0:T(8,128)(2,1)}) custom-call(s32[8]{0:T(128)} %copy-done.6, bf16[256,1024]{1,0:T(8,128)(2,1)} %bitcast.39, ...), custom_call_target="tpu_custom_call", output_to_operand_aliasing={{0}: (9, {}), {1}: (10, {}), {2}: (11, {}), {3}: (12, {})} | custom-call | flops 4000000000 | bytes 16777216 | tf_op jit(solution)/shard_map/local_backward/pallas_call | solution.py:248
  138.4 2.5 %all-to-all-done.3 = bf16[8,24,1024]{2,1,0:T(8,128)(2,1)S(1)} async-done(((bf16[8,24,1024]{2,1,0:T(8,128)(2,1)}), bf16[8,24,1024]{2,1,0:T(8,128)(2,1)S(1)}, u32[]{:S(2)}, u32[]{:S(2)}) %all-to-all-start.3) | async-done | bytes 393248 | tf_op jit(solution)/shard_map/all_to_all | solution.py:288
  140.9 6.7 %collective-permute-start.16 = (bf16[2,256,1024]{2,1,0:T(8,128)(2,1)}, bf16[2,256,1024]{2,1,0:T(8,128)(2,1)}, u32[]{:S(2)}, u32[]{:S(2)}) collective-permute-start(bf16[2,256,1024]{2,1,0:T(8,128)(2,1)} %get-tuple-element.143), channel_id=1, source_target_pairs={{1,2},{2,1},{3,4},{4,3},{5,6},{6,5},{7,8},{8,7},{9,10},{10,9},{11,... | collective-permute-start | bytes 3145736 | tf_op jit(solution)/shard_map/ppermute | solution.py:280
  147.7 0.9 broadcast_in_dim.27
  148.5 5.0 %all-to-all-start.4 = ((bf16[32,8,1024]{2,1,0:T(8,128)(2,1)}), bf16[32,8,1024]{2,1,0:T(8,128)(2,1)S(1)}, u32[]{:S(2)}, u32[]{:S(2)}) async-start(bf16[32,8,1024]{2,1,0:T(8,128)(2,1)} %broadcast_in_dim.27), calls=%async_computation.4 | async-start | bytes 1048576 | tf_op jit(solution)/shard_map/all_to_all | solution.py:296
  153.5 0.1 collective-permute-start.12
  153.7 1.4 collective-permute-start.13
  155.0 2.6 %collective-permute-start.14 = (f32[16,1024]{1,0:T(8,128)S(1)}, f32[16,1024]{1,0:T(8,128)S(1)}, u32[]{:S(2)}, u32[]{:S(2)}) collective-permute-start(f32[16,1024]{1,0:T(8,128)S(1)} %convert_reduce_fusion), channel_id=1, source_target_pairs={{0,128},{64,192},{128,0},{192,64},{1,129},{65,193},{129,1},{193,65... | collective-permute-start | bytes 196616 | tf_op jit(solution)/shard_map/ppermute | solution.py:421
  157.6 1.1 collective-permute-start.15
  158.7 2.0 %collective-permute-done.14 = f32[16,1024]{1,0:T(8,128)S(1)} collective-permute-done((f32[16,1024]{1,0:T(8,128)S(1)}, f32[16,1024]{1,0:T(8,128)S(1)}, u32[]{:S(2)}, u32[]{:S(2)}) %collective-permute-start.14) | collective-permute-done | bytes 65568 | tf_op jit(solution)/shard_map/ppermute | solution.py:421
  160.8 0.3 collective-permute-done.15
  161.1 11.2 %all-to-all-done.4 = bf16[32,8,1024]{2,1,0:T(8,128)(2,1)S(1)} async-done(((bf16[32,8,1024]{2,1,0:T(8,128)(2,1)}), bf16[32,8,1024]{2,1,0:T(8,128)(2,1)S(1)}, u32[]{:S(2)}, u32[]{:S(2)}) %all-to-all-start.4) | async-done | bytes 524320 | tf_op jit(solution)/shard_map/all_to_all | solution.py:296
  172.3 0.0 collective-permute-done.16.from_chip
  172.3 2.3 %collective-permute-start.17 = (bf16[256,1024]{1,0:T(8,128)(2,1)S(1)}, bf16[256,1024]{1,0:T(8,128)(2,1)S(1)}, u32[]{:S(2)}, u32[]{:S(2)}) collective-permute-start(bf16[256,1024]{1,0:T(8,128)(2,1)S(1)} %bitcast.26), channel_id=1, source_target_pairs={{0,1},{1,0},{2,3},{3,2},{4,5},{5,4},{6,7},{7,6},{8,9},{9,8},{10,11... | collective-permute-start | bytes 1572872 | tf_op jit(solution)/shard_map/ppermute | solution.py:280
  174.6 0.6 add_add_fusion
  175.3 0.0 collective-permute-done.12.from_core
  175.3 0.9 collective-permute-done.17.far_rest
  176.2 1.6 copy-done.1
  177.8 3.1 %combine.1 = (bf16[256,1024]{1,0:T(8,128)(2,1)}, bf16[256,1024]{1,0:T(8,128)(2,1)}) custom-call(s32[8]{0:T(128)S(1)} %copy-done.8, f32[2,256,1024]{2,1,0:T(8,128)S(1)} %copy-done.1, bf16[2,256,1024]{2,1,0:T(8,128)(2,1)} %collective-permute-done.12.from_core, bf16[2,256,1024]{2,1,0:T(8,128)(2,1)} %collective-permute-done.16.from_chip, ...), custom_call_target="tpu_custom_call" | custom-call | tf_op jit(solution)/shard_map/combine/pallas_call | solution.py:194
  (29 shorter events, 0.1 us)
Async XLA Ops:
  0.6 62.4 %copy-start = (bf16[1024,1024]{1,0:T(8,128)(2,1)S(1)}, bf16[1024,1024]{1,0:T(8,128)(2,1)}, u32[]{:S(2)}) copy-start(bf16[1024,1024]{1,0:T(8,128)(2,1)} %param.11) | copy-start | bytes 6291460
  1.4 1.0 copy-start.4
  2.5 1.0 copy-start.5
  3.5 0.7 copy-start.9
  4.2 58.9 %copy-start.11 = (bf16[1,256,1024]{2,1,0:T(8,128)(2,1)S(1)}, bf16[1,256,1024]{2,1,0:T(8,128)(2,1)}, u32[]{:S(2)}) copy-start(bf16[1,256,1024]{2,1,0:T(8,128)(2,1)} %param.10) | copy-start | bytes 1572868
  5.9 25.5 %collective-permute-start = (bf16[2,64,1024]{2,1,0:T(8,128)(2,1)S(1)}, bf16[2,64,1024]{2,1,0:T(8,128)(2,1)S(1)}, u32[]{:S(2)}, u32[]{:S(2)}) collective-permute-start(bf16[2,64,1024]{2,1,0:T(8,128)(2,1)S(1)} %get-tuple-element.81), channel_id=1, source_target_pairs={{0,2},{1,3},{2,4},{3,5},{4,6},{5,7},{6,0},{7,1},{8,10},{9,11},{10,... | collective-permute-start | bytes 786440 | tf_op jit(solution)/shard_map/ppermute | solution.py:280
  8.0 23.3 %collective-permute-start.1 = (bf16[2,64,1024]{2,1,0:T(8,128)(2,1)S(1)}, bf16[2,64,1024]{2,1,0:T(8,128)(2,1)S(1)}, u32[]{:S(2)}, u32[]{:S(2)}) collective-permute-start(bf16[2,64,1024]{2,1,0:T(8,128)(2,1)S(1)} %get-tuple-element.82), channel_id=1, source_target_pairs={{0,4},{1,5},{2,6},{3,7},{4,0},{5,1},{6,2},{7,3},{8,12},{9,13},{10,... | collective-permute-start | bytes 786440 | tf_op jit(solution)/shard_map/ppermute | solution.py:280
  10.5 20.9 %collective-permute-start.2 = (bf16[2,64,1024]{2,1,0:T(8,128)(2,1)S(1)}, bf16[2,64,1024]{2,1,0:T(8,128)(2,1)S(1)}, u32[]{:S(2)}, u32[]{:S(2)}) collective-permute-start(bf16[2,64,1024]{2,1,0:T(8,128)(2,1)S(1)} %get-tuple-element.83), channel_id=1, source_target_pairs={{0,6},{1,7},{2,0},{3,1},{4,2},{5,3},{6,4},{7,5},{8,14},{9,15},{10,... | collective-permute-start | bytes 786440 | tf_op jit(solution)/shard_map/ppermute | solution.py:280
  32.8 31.9 %copy-start.6 = (s32[8]{0:T(128)}, s32[8]{0:T(128)S(1)}, u32[]{:S(2)}) copy-start(s32[8]{0:T(128)S(1)} %get-tuple-element.84.flags) | copy-start | bytes 100
  32.8 2.0 %collective-permute-start.3 = (bf16[64,1024]{1,0:T(8,128)(2,1)S(1)}, bf16[64,1024]{1,0:T(8,128)(2,1)S(1)}, u32[]{:S(2)}, u32[]{:S(2)}) collective-permute-start(bf16[64,1024]{1,0:T(8,128)(2,1)S(1)} %get-tuple-element.86), channel_id=1, source_target_pairs={{0,1},{1,0},{2,3},{3,2},{4,5},{5,4},{6,7},{7,6},{8,9},{9,8},{10,11... | collective-permute-start | bytes 393224 | tf_op jit(solution)/shard_map/ppermute | solution.py:280
  35.5 13.8 %collective-permute-start.4 = (bf16[2,256,1024]{2,1,0:T(8,128)(2,1)}, bf16[2,256,1024]{2,1,0:T(8,128)(2,1)}, u32[]{:S(2)}, u32[]{:S(2)}) collective-permute-start(bf16[2,256,1024]{2,1,0:T(8,128)(2,1)} %get-tuple-element.91.own.refs_2_), channel_id=1, source_target_pairs={{0,1},{1,0},{2,3},{3,2},{4,5},{5,4},{6,7},{7,6},{8,9},{9,8},{10,11... | collective-permute-start | bytes 3145736 | tf_op jit(solution)/shard_map/ppermute | solution.py:280
  35.6 16.4 %collective-permute-start.5 = (bf16[2,256,1024]{2,1,0:T(8,128)(2,1)}, bf16[2,256,1024]{2,1,0:T(8,128)(2,1)}, u32[]{:S(2)}, u32[]{:S(2)}) collective-permute-start(bf16[2,256,1024]{2,1,0:T(8,128)(2,1)} %get-tuple-element.91.own.refs_2_), channel_id=1, source_target_pairs={{1,2},{2,1},{3,4},{4,3},{5,6},{6,5},{7,8},{8,7},{9,10},{10,9},{11,... | collective-permute-start | bytes 3145736 | tf_op jit(solution)/shard_map/ppermute | solution.py:280
  38.1 11.3 %all-to-all-start.1 = ((bf16[8,8,1024]{2,1,0:T(8,128)(2,1)}), bf16[8,8,1024]{2,1,0:T(8,128)(2,1)S(1)}, u32[]{:S(2)}, u32[]{:S(2)}) async-start(bf16[8,8,1024]{2,1,0:T(8,128)(2,1)} %bitcast.5), calls=%async_computation.1 | async-start | bytes 262144 | tf_op jit(solution)/shard_map/all_to_all | solution.py:288
  52.9 27.1 %all-to-all-start.2 = ((bf16[32,8,1024]{2,1,0:T(8,128)(2,1)}), bf16[32,8,1024]{2,1,0:T(8,128)(2,1)S(1)}, u32[]{:S(2)}, u32[]{:S(2)}) async-start(bf16[32,8,1024]{2,1,0:T(8,128)(2,1)} %broadcast_in_dim.24), calls=%async_computation.2 | async-start | bytes 1048576 | tf_op jit(solution)/shard_map/all_to_all | solution.py:296
  79.9 2.2 %copy-start.10 = (bf16[32,8,1024]{2,1,0:T(8,128)(2,1)}, bf16[32,8,1024]{2,1,0:T(8,128)(2,1)S(1)}, u32[]{:S(2)}) copy-start(bf16[32,8,1024]{2,1,0:T(8,128)(2,1)S(1)} %all-to-all-done.2) | copy-start | bytes 1572868
  79.9 2.1 %collective-permute-start.6 = (bf16[256,1024]{1,0:T(8,128)(2,1)S(1)}, bf16[256,1024]{1,0:T(8,128)(2,1)S(1)}, u32[]{:S(2)}, u32[]{:S(2)}) collective-permute-start(bf16[256,1024]{1,0:T(8,128)(2,1)S(1)} %bitcast.33), channel_id=1, source_target_pairs={{0,1},{1,0},{2,3},{3,2},{4,5},{5,4},{6,7},{7,6},{8,9},{9,8},{10,11... | collective-permute-start | bytes 1572872 | tf_op jit(solution)/shard_map/ppermute | solution.py:280
  82.1 0.8 copy-start.12
  98.3 3.7 %copy-start.2 = (f32[4,8,16,1024]{3,2,1,0:T(8,128)S(1)}, f32[4,8,16,1024]{3,2,1,0:T(8,128)}, u32[]{:S(2)}) copy-start(f32[4,8,16,1024]{3,2,1,0:T(8,128)} %get-tuple-element.108.kept) | copy-start | bytes 6291460
  98.3 3.7 %copy-start.3 = (bf16[256,1024]{1,0:T(8,128)(2,1)S(1)}, bf16[256,1024]{1,0:T(8,128)(2,1)}, u32[]{:S(2)}) copy-start(bf16[256,1024]{1,0:T(8,128)(2,1)} %get-tuple-element.106) | copy-start | bytes 1572868
  98.3 3.7 %copy-start.7 = (s32[8]{0:T(128)S(1)}, s32[8]{0:T(128)}, u32[]{:S(2)}) copy-start(s32[8]{0:T(128)} %copy-done.6) | copy-start | bytes 100
  98.3 3.7 %collective-permute-start.8 = (bf16[4,8,16,1024]{3,2,1,0:T(8,128)(2,1)}, bf16[4,8,16,1024]{3,2,1,0:T(8,128)(2,1)S(1)}, u32[]{:S(2)}, u32[]{:S(2)}) collective-permute-start(bf16[4,8,16,1024]{3,2,1,0:T(8,128)(2,1)} %get-tuple-element.103), channel_id=1, source_target_pairs={{0,1},{1,0},{2,3},{3,2},{4,5},{5,4},{6,7},{7,6},{8,9},{9,8},{10,11... | collective-permute-start | bytes 3145736 | tf_op jit(solution)/shard_map/ppermute | solution.py:280
  98.8 3.2 %collective-permute-start.7 = (bf16[256,1024]{1,0:T(8,128)(2,1)}, bf16[256,1024]{1,0:T(8,128)(2,1)S(1)}, u32[]{:S(2)}, u32[]{:S(2)}) collective-permute-start(bf16[256,1024]{1,0:T(8,128)(2,1)} %get-tuple-element.102), channel_id=1, source_target_pairs={{0,1},{1,0},{2,3},{3,2},{4,5},{5,4},{6,7},{7,6},{8,9},{9,8},{10,11... | collective-permute-start | bytes 1572872 | tf_op jit(solution)/shard_map/ppermute | solution.py:280
  102.9 13.3 %collective-permute-start.9 = (bf16[192,1024]{1,0:T(8,128)(2,1)S(1)}, bf16[192,1024]{1,0:T(8,128)(2,1)S(1)}, u32[]{:S(2)}, u32[]{:S(2)}) collective-permute-start(bf16[192,1024]{1,0:T(8,128)(2,1)S(1)} %get-tuple-element.116), channel_id=1, source_target_pairs={{0,2},{1,3},{2,4},{3,5},{4,6},{5,7},{6,0},{7,1},{8,10},{9,11},{10,... | collective-permute-start | bytes 1179656 | tf_op jit(solution)/shard_map/ppermute | solution.py:280
  103.0 19.2 %collective-permute-start.10 = (bf16[192,1024]{1,0:T(8,128)(2,1)S(1)}, bf16[192,1024]{1,0:T(8,128)(2,1)S(1)}, u32[]{:S(2)}, u32[]{:S(2)}) collective-permute-start(bf16[192,1024]{1,0:T(8,128)(2,1)S(1)} %get-tuple-element.117), channel_id=1, source_target_pairs={{0,4},{1,5},{2,6},{3,7},{4,0},{5,1},{6,2},{7,3},{8,12},{9,13},{10,... | collective-permute-start | bytes 1179656 | tf_op jit(solution)/shard_map/ppermute | solution.py:280
  104.9 18.3 %collective-permute-start.11 = (bf16[192,1024]{1,0:T(8,128)(2,1)S(1)}, bf16[192,1024]{1,0:T(8,128)(2,1)S(1)}, u32[]{:S(2)}, u32[]{:S(2)}) collective-permute-start(bf16[192,1024]{1,0:T(8,128)(2,1)S(1)} %get-tuple-element.118), channel_id=1, source_target_pairs={{0,6},{1,7},{2,0},{3,1},{4,2},{5,3},{6,4},{7,5},{8,14},{9,15},{10,... | collective-permute-start | bytes 1179656 | tf_op jit(solution)/shard_map/ppermute | solution.py:280
  124.3 16.6 %all-to-all-start.3 = ((bf16[8,24,1024]{2,1,0:T(8,128)(2,1)}), bf16[8,24,1024]{2,1,0:T(8,128)(2,1)S(1)}, u32[]{:S(2)}, u32[]{:S(2)}) async-start(bf16[8,24,1024]{2,1,0:T(8,128)(2,1)} %pad_maximum_fusion), calls=%async_computation.3 | async-start | bytes 786432 | tf_op jit(solution)/shard_map/all_to_all | solution.py:288
  138.4 37.7 %copy-start.8 = (s32[8]{0:T(128)S(1)}, s32[8]{0:T(128)}, u32[]{:S(2)}) copy-start(s32[8]{0:T(128)} %copy-done.6) | copy-start | bytes 100
  140.9 31.4 %collective-permute-start.16 = (bf16[2,256,1024]{2,1,0:T(8,128)(2,1)}, bf16[2,256,1024]{2,1,0:T(8,128)(2,1)}, u32[]{:S(2)}, u32[]{:S(2)}) collective-permute-start(bf16[2,256,1024]{2,1,0:T(8,128)(2,1)} %get-tuple-element.143), channel_id=1, source_target_pairs={{1,2},{2,1},{3,4},{4,3},{5,6},{6,5},{7,8},{8,7},{9,10},{10,9},{11,... | collective-permute-start | bytes 3145736 | tf_op jit(solution)/shard_map/ppermute | solution.py:280
  148.5 23.7 %all-to-all-start.4 = ((bf16[32,8,1024]{2,1,0:T(8,128)(2,1)}), bf16[32,8,1024]{2,1,0:T(8,128)(2,1)S(1)}, u32[]{:S(2)}, u32[]{:S(2)}) async-start(bf16[32,8,1024]{2,1,0:T(8,128)(2,1)} %broadcast_in_dim.27), calls=%async_computation.4 | async-start | bytes 1048576 | tf_op jit(solution)/shard_map/all_to_all | solution.py:296
  153.5 21.8 %collective-permute-start.12 = (bf16[2,256,1024]{2,1,0:T(8,128)(2,1)}, bf16[2,256,1024]{2,1,0:T(8,128)(2,1)}, u32[]{:S(2)}, u32[]{:S(2)}) collective-permute-start(bf16[2,256,1024]{2,1,0:T(8,128)(2,1)} %get-tuple-element.141), channel_id=1, source_target_pairs={{0,1},{1,0},{2,3},{3,2},{4,5},{5,4},{6,7},{7,6},{8,9},{9,8},{10,11... | collective-permute-start | bytes 3145736 | tf_op jit(solution)/shard_map/ppermute | solution.py:280
  153.7 5.1 %collective-permute-start.13 = (f32[16,1024]{1,0:T(8,128)S(1)}, f32[16,1024]{1,0:T(8,128)S(1)}, u32[]{:S(2)}, u32[]{:S(2)}) collective-permute-start(f32[16,1024]{1,0:T(8,128)S(1)} %convert_reduce_fusion), channel_id=1, source_target_pairs={{0,64},{64,128},{128,192},{192,0},{1,65},{65,129},{129,193},{193,1... | collective-permute-start | bytes 196616 | tf_op jit(solution)/shard_map/ppermute | solution.py:421
  155.0 5.7 %collective-permute-start.14 = (f32[16,1024]{1,0:T(8,128)S(1)}, f32[16,1024]{1,0:T(8,128)S(1)}, u32[]{:S(2)}, u32[]{:S(2)}) collective-permute-start(f32[16,1024]{1,0:T(8,128)S(1)} %convert_reduce_fusion), channel_id=1, source_target_pairs={{0,128},{64,192},{128,0},{192,64},{1,129},{65,193},{129,1},{193,65... | collective-permute-start | bytes 196616 | tf_op jit(solution)/shard_map/ppermute | solution.py:421
  157.6 3.4 %collective-permute-start.15 = (f32[16,1024]{1,0:T(8,128)S(1)}, f32[16,1024]{1,0:T(8,128)S(1)}, u32[]{:S(2)}, u32[]{:S(2)}) collective-permute-start(f32[16,1024]{1,0:T(8,128)S(1)} %convert_reduce_fusion), channel_id=1, source_target_pairs={{0,192},{64,0},{128,64},{192,128},{1,193},{65,1},{129,65},{193,129... | collective-permute-start | bytes 196616 | tf_op jit(solution)/shard_map/ppermute | solution.py:421
  172.3 3.9 %collective-permute-start.17 = (bf16[256,1024]{1,0:T(8,128)(2,1)S(1)}, bf16[256,1024]{1,0:T(8,128)(2,1)S(1)}, u32[]{:S(2)}, u32[]{:S(2)}) collective-permute-start(bf16[256,1024]{1,0:T(8,128)(2,1)S(1)} %bitcast.26), channel_id=1, source_target_pairs={{0,1},{1,0},{2,3},{3,2},{4,5},{5,4},{6,7},{7,6},{8,9},{9,8},{10,11... | collective-permute-start | bytes 1572872 | tf_op jit(solution)/shard_map/ppermute | solution.py:280
  176.2 1.6 copy-start.1

commit v4 on v3

--- a/solution.py
+++ b/solution.py
@@ -222,18 +222,19 @@
             other_out[...] = ref[1 - c]
 
 
-def combine(flags, own, from_core, from_chip, far_half, far_rest, key_out, value_out):
+def combine(flags, base, far_half, far_rest, key_out, value_out):
     first = flags[2] == 0
     at_hub = flags[5] > 0
     tall = 64
     for begin in range(0, key_out.shape[0], tall):
         rows = pl.ds(begin, tall)
-        total = own[:, rows] + from_core[:, rows].astype(F32) + from_chip[:, rows].astype(F32)
-        half, rest = far_half[rows, :].astype(F32), far_rest[rows, :].astype(F32)
-        far_key = jnp.where(first, half, rest)
-        far_value = jnp.where(first, rest, half)
-        key_out[rows, :] = (total[0] + jnp.where(at_hub, far_key, 0.0)).astype(BF16)
-        value_out[rows, :] = (total[1] + jnp.where(at_hub, far_value, 0.0)).astype(BF16)
+        half, rest = far_half[rows, :], far_rest[rows, :]
+        far_key = jnp.where(first, half, rest).astype(F32)
+        far_value = jnp.where(first, rest, half).astype(F32)
+        far_key = jnp.where(at_hub, far_key, 0.0)
+        far_value = jnp.where(at_hub, far_value, 0.0)
+        key_out[rows, :] = (base[0, rows].astype(F32) + far_key).astype(BF16)
+        value_out[rows, :] = (base[1, rows].astype(F32) + far_value).astype(BF16)
 
 
 def across(shape, start=0):
@@ -385,10 +386,10 @@
     pieces, lse = lax.optimization_barrier((pieces, lse))
     pieces = [pieces[0]] + [send(pieces[k], hop(dx=k)) for k in range(1, NX)]
 
-    steps = width // SPAN // 2
+    blocks = width // SPAN
     double = (2, rows, width)
 
-    def backward(lse, done, begin):
+    def backward(lse, done, begin, steps):
         ins = [(a, across(a.shape, begin)) for a in (query, d_attn, *near, lse, cen, dq_far)]
         outs = [(flat, BF16), (double, F32), (double, BF16), (double, BF16)]
         return call(
@@ -397,35 +398,36 @@
             ins + [(a, pl.BlockSpec(memory_space=pl.ANY)) for a in done],
             [(s, t, across(s, begin)) for s, t in outs],
             steps,
-            int(4e9),
+            int(2e9) * steps,
             "local_backward",
             {1 + len(ins) + i: i for i in range(len(done))},
         )
 
-    grads = backward(lse, [], 0)
+    grads = backward(lse, [], 0, blocks - 1)
     pieces, grads, lse = lax.optimization_barrier((pieces, grads, lse))
     summed = sum(p.astype(F32) for p in pieces).astype(BF16)
     both = [summed[:quarter].reshape(NZ, eighth, width), summed[quarter:].reshape(NZ, slab, width)]
     both = swap_z(jnp.concatenate(both, axis=1))
-    grads = backward(lse, grads, steps)
-    both, grads = lax.optimization_barrier((both, grads))
+    grads = backward(lse, grads, blocks - 1, 1)
     d_query, own, to_core, to_chip = grads
+    from_chip = send(to_chip, CHIP)
+    from_core = send(to_core, CORE)
+    both, own = lax.optimization_barrier((both, own))
     total = jnp.sum(both[:, :eighth].astype(F32), axis=0).astype(BF16)
     weight = jnp.sum(both[:, eighth:].astype(F32), axis=0)
 
     far_half = gather_plane(total)
-    from_chip = send(to_chip, CHIP)
-    from_core = send(to_core, CORE)
     dp = lax.axis_size("dp")
     shares = [
         lax.ppermute(weight, "dp", [(i, (i + k) % dp) for i in range(dp)]) for k in range(1, dp)
     ]
-    far_half, shares, from_chip = lax.optimization_barrier((far_half, shares, from_chip))
+    base = (own + from_core.astype(F32) + from_chip.astype(F32)).astype(BF16)
+    far_half, shares, base = lax.optimization_barrier((far_half, shares, base))
     d_weight = weight + sum(shares)
     far_rest = send(far_half, CORE)
     d_key, d_value = simple(
         combine,
-        [flags, own, from_core, from_chip, far_half, far_rest],
+        [flags, base, far_half, far_rest],
         [(flat, BF16)] * 2,
         "combine",
         1,

time: 182 us -> 174 us (0.956)
  starting transfers between devices: 50.9 us -> 45.9 us
  waiting for transfers between devices: 39.9 us -> 36.2 us
  other arithmetic: 2.42 us -> 5.11 us
    ppermute x15, starting transfers between devices: 23 us -> 18.2 us  [send(): return lax.ppermute(value, 'region', pairs)]
    all_to_all x2, waiting for transfers between devices: 8.42 us -> 12 us  [swap_z(): lax.all_to_all(value, 'region', 0, 0, axis_index_groups=Z_GROUPS, tiled=T...]
    all_to_all x2, waiting for transfers between devices: 16.6 us -> 13.6 us  [gather_plane(): lax.all_to_all(jnp.broadcast_to(value[None], (count,) + value.shape), 're...]
    convert_element_type x0 -> x1, other arithmetic: none -> 2.69 us  [on_device(): base = (own + from_core.astype(F32) + from_chip.astype(F32)).astype(BF16)]
    ppermute x3, waiting for transfers between devices: 2.34 us -> 0.01 us  [on_device(): lax.ppermute(weight, 'dp', [(i, (i + k) % dp) for i in range(dp)])]
    ppermute x15, waiting for transfers between devices: 12.5 us -> 10.6 us  [send(): return lax.ppermute(value, 'region', pairs)]
    unnamed x26 -> x22, local copies, waits for them, and re-layouts: 5.15 us -> 3.56 us
  transfers between devices with their start and end apart: 22 -> 22, of which waited for: 12 -> 10; matrix products, arithmetic and copies ran while one was open for 3% -> 6% of each run, Pallas kernels for 16% -> 17%
where the time goes in v4:
time: 174 us; the launch traced here: 173 us
  Pallas kernels  50.7 us (29%)
  starting transfers between devices  45.9 us (26%)
  waiting for transfers between devices  36.2 us (21%)
  blocking collectives  19.7 us (11%)
  local copies, waits for them, and re-layouts  5.88 us (3%)
  matrix products  5.17 us (3%)
  other arithmetic  5.11 us (3%)
  between operations  4.27 us (2%)
    pallas_call x4, Pallas kernels, call(): pl.pallas_call(body, grid_spec=pltpu.PrefetchScalarGridSpec(num_scalar_pr...  44.9 us
    all_to_all x1, blocking collectives, on_device(): ids = lax.all_to_all(ids, 'region', 0, 0, tiled=True)  19.7 us
    ppermute x15, starting transfers between devices, send(): return lax.ppermute(value, 'region', pairs)  18.2 us
    all_to_all x2, starting transfers between devices, gather_plane(): lax.all_to_all(jnp.broadcast_to(value[None], (count,) + value.shape), 're...  14.9 us
    all_to_all x2, waiting for transfers between devices, gather_plane(): lax.all_to_all(jnp.broadcast_to(value[None], (count,) + value.shape), 're...  13.6 us
    all_to_all x2, waiting for transfers between devices, swap_z(): lax.all_to_all(value, 'region', 0, 0, axis_index_groups=Z_GROUPS, tiled=T...  12 us
    ppermute x15, waiting for transfers between devices, send(): return lax.ppermute(value, 'region', pairs)  10.6 us
    all_to_all x2, starting transfers between devices, swap_z(): lax.all_to_all(value, 'region', 0, 0, axis_index_groups=Z_GROUPS, tiled=T...  7.63 us
  transfers between devices with their start and end apart: 22, of which 10 were waited for; matrix products, arithmetic and copies ran while one was open for 6% of the time, Pallas kernels for 17%

profile of v4, /device:TPU:1, one launch (start us, length us, event | category | flops | bytes accessed | tf_op | source)
XLA Modules:
  0.0 172.9 jit_solution(719852243718952077)
XLA Ops:
  0.6 0.0 copy-start
  1.5 1.0 copy-done.4
  2.5 1.0 copy-done.5
  3.5 0.7 copy-done.9
  4.2 1.2 prepare.1
  5.4 2.1 %collective-permute-start = (bf16[2,64,1024]{2,1,0:T(8,128)(2,1)S(1)}, bf16[2,64,1024]{2,1,0:T(8,128)(2,1)S(1)}, u32[]{:S(2)}, u32[]{:S(2)}) collective-permute-start(bf16[2,64,1024]{2,1,0:T(8,128)(2,1)S(1)} %get-tuple-element.78), channel_id=1, source_target_pairs={{0,2},{1,3},{2,4},{3,5},{4,6},{5,7},{6,0},{7,1},{8,10},{9,11},{10,... | collective-permute-start | bytes 786440 | tf_op jit(solution)/shard_map/ppermute | solution.py:281
  7.5 2.5 %collective-permute-start.1 = (bf16[2,64,1024]{2,1,0:T(8,128)(2,1)S(1)}, bf16[2,64,1024]{2,1,0:T(8,128)(2,1)S(1)}, u32[]{:S(2)}, u32[]{:S(2)}) collective-permute-start(bf16[2,64,1024]{2,1,0:T(8,128)(2,1)S(1)} %get-tuple-element.79), channel_id=1, source_target_pairs={{0,4},{1,5},{2,6},{3,7},{4,0},{5,1},{6,2},{7,3},{8,12},{9,13},{10,... | collective-permute-start | bytes 786440 | tf_op jit(solution)/shard_map/ppermute | solution.py:281
  9.9 1.2 collective-permute-start.2
  11.1 19.7 %all_to_all.25.ids = s32[64,1,128]{2,1,0:T(1,128)S(1)} all-to-all(s32[64,1,128]{2,1,0:T(1,128)S(1)} %get-tuple-element.76), channel_id=1, replica_groups=mesh['dp'=4,'region'=64] {'region'}, dimensions={0} | all-to-all | bytes 65536 | tf_op jit(solution)/shard_map/all_to_all | solution.py:329
  30.8 0.0 collective-permute-done.one
  30.8 0.0 collective-permute-done.1.two
  30.8 0.0 collective-permute-done.2.three
  30.8 1.4 choose.1
  32.3 0.8 collective-permute-start.3
  33.0 0.6 fusion.1
  34.3 0.0 collective-permute-done.3
  34.3 0.7 broadcast_select_fusion
  35.0 0.1 collective-permute-start.4
  35.1 2.5 %collective-permute-start.5 = (bf16[2,256,1024]{2,1,0:T(8,128)(2,1)S(1)}, bf16[2,256,1024]{2,1,0:T(8,128)(2,1)}, u32[]{:S(2)}, u32[]{:S(2)}) collective-permute-start(bf16[2,256,1024]{2,1,0:T(8,128)(2,1)S(1)} %get-tuple-element.88.own.refs_2_), channel_id=1, source_target_pairs={{1,2},{2,1},{3,4},{4,3},{5,6},{6,5},{7,8},{8,7},{9,10},{10,9},{11,... | collective-permute-start | bytes 3145736 | tf_op jit(solution)/shard_map/ppermute | solution.py:281
  37.6 3.4 %all-to-all-start.1 = ((bf16[8,8,1024]{2,1,0:T(8,128)(2,1)}), bf16[8,8,1024]{2,1,0:T(8,128)(2,1)S(1)}, u32[]{:S(2)}, u32[]{:S(2)}) async-start(bf16[8,8,1024]{2,1,0:T(8,128)(2,1)} %bitcast.5), calls=%async_computation.1 | async-start | bytes 262144 | tf_op jit(solution)/shard_map/all_to_all | solution.py:289
  42.9 5.9 %all-to-all-done.1 = bf16[8,8,1024]{2,1,0:T(8,128)(2,1)S(1)} async-done(((bf16[8,8,1024]{2,1,0:T(8,128)(2,1)}), bf16[8,8,1024]{2,1,0:T(8,128)(2,1)S(1)}, u32[]{:S(2)}, u32[]{:S(2)}) %all-to-all-start.1) | async-done | bytes 131104 | tf_op jit(solution)/shard_map/all_to_all | solution.py:289
  48.8 0.0 collective-permute-done.4.core.refs_3_
  48.8 2.5 %collective-permute-done.5.chip.refs_4_ = bf16[2,256,1024]{2,1,0:T(8,128)(2,1)} collective-permute-done((bf16[2,256,1024]{2,1,0:T(8,128)(2,1)S(1)}, bf16[2,256,1024]{2,1,0:T(8,128)(2,1)}, u32[]{:S(2)}, u32[]{:S(2)}) %collective-permute-start.5) | collective-permute-done | bytes 1048608 | tf_op jit(solution)/shard_map/ppermute | solution.py:281
  51.3 0.9 broadcast_in_dim.24
  52.1 10.3 %all-to-all-start.2 = ((bf16[32,8,1024]{2,1,0:T(8,128)(2,1)}), bf16[32,8,1024]{2,1,0:T(8,128)(2,1)}, u32[]{:S(2)}, u32[]{:S(2)}) async-start(bf16[32,8,1024]{2,1,0:T(8,128)(2,1)} %broadcast_in_dim.24), calls=%async_computation.2 | async-start | bytes 1048576 | tf_op jit(solution)/shard_map/all_to_all | solution.py:297
  62.5 2.6 %convolution_convert_fusion.1.d.refs_1_ = bf16[256,1024]{1,0:T(8,128)(2,1)} fusion(bf16[1024,1024]{1,0:T(8,128)(2,1)S(1)} %copy-done, bf16[1,256,1024]{2,1,0:T(8,128)(2,1)} %param.10), kind=kOutput, calls=%fused_computation.2 | convolution fusion | flops 537133056 | bytes 3145728 | tf_op jit(solution)/shard_map/dot_general | solution.py:353
  65.1 9.8 %local_forward.1 = (f32[256,1024]{1,0:T(8,128)}, f32[256,1024]{1,0:T(8,128)}, f32[256,1024]{1,0:T(8,128)}) custom-call(s32[8]{0:T(128)} %copy-done.6, bf16[256,1024]{1,0:T(8,128)(2,1)} %bitcast.31, bf16[2,256,1024]{2,1,0:T(8,128)(2,1)} %copy-done.2, bf16[2,256,1024]{2,1,0:T(8,128)(2,1)} %collective-permute-done.4.core.refs_3_, ...), custom_call_target="tpu_custom_call" | custom-call | flops 5000000000 | bytes 6815744 | tf_op jit(solution)/shard_map/local_forward/pallas_call | solution.py:249
  74.9 4.4 %all-to-all-done.2 = bf16[32,8,1024]{2,1,0:T(8,128)(2,1)} async-done(((bf16[32,8,1024]{2,1,0:T(8,128)(2,1)}), bf16[32,8,1024]{2,1,0:T(8,128)(2,1)}, u32[]{:S(2)}, u32[]{:S(2)}) %all-to-all-start.2) | async-done | bytes 524320 | tf_op jit(solution)/shard_map/all_to_all | solution.py:297
  79.3 0.6 collective-permute-start.6
  79.9 1.7 %collective-permute-done.6.rest = bf16[256,1024]{1,0:T(8,128)(2,1)S(1)} collective-permute-done((bf16[256,1024]{1,0:T(8,128)(2,1)}, bf16[256,1024]{1,0:T(8,128)(2,1)S(1)}, u32[]{:S(2)}, u32[]{:S(2)}) %collective-permute-start.6) | collective-permute-done | bytes 524320 | tf_op jit(solution)/shard_map/ppermute | solution.py:281
  81.7 0.8 copy-done.10
  82.5 15.4 %hub_block.1 = (bf16[256,1024]{1,0:T(8,128)(2,1)}, f32[256,1024]{1,0:T(8,128)}, f32[256,1024]{1,0:T(8,128)}, f32[256,1024]{1,0:T(8,128)}, bf16[256,1024]{1,0:T(8...) custom-call(s32[8]{0:T(128)} %copy-done.6, ...), custom_call_target="tpu_custom_call" | custom-call | flops 8999999488 | bytes 13631488 | tf_op jit(solution)/shard_map/hub_block/pallas_call | solution.py:249
  97.9 0.5 collective-permute-start.8
  98.3 0.3 collective-permute-start.7
  98.6 2.6 %convolution_convert_fusion = bf16[256,1024]{1,0:T(8,128)(2,1)} fusion(bf16[256,1024]{1,0:T(8,128)(2,1)} %get-tuple-element.101, bf16[1024,1024]{1,0:T(8,128)(2,1)S(1)} %copy-done), kind=kOutput, calls=%fused_computation.1 | convolution fusion | flops 537133056 | bytes 3145728 | tf_op jit(solution)/shard_map/dot_general | solution.py:25
  101.2 0.4 collective-permute-done.7
  101.6 0.8 add_pieces.1
  102.5 1.4 collective-permute-start.10
  103.8 1.1 collective-permute-start.11
  104.9 0.3 collective-permute-start.9
  105.3 13.4 %local_backward.2 = (bf16[256,1024]{1,0:T(8,128)(2,1)}, f32[2,256,1024]{2,1,0:T(8,128)}, bf16[2,256,1024]{2,1,0:T(8,128)(2,1)}, bf16[2,256,1024]{2,1,0:T(8,128)(2,1)}) custom-call(s32[8]{0:T(128)} %copy-done.6, bf16[256,1024]{1,0:T(8,128)(2,1)} %bitcast.33, bf16[256,1024]{1,0:T(8,128)(2,1)} %convolution_convert_fusion.1.d.refs_1_, ...), custom_call_target="tpu_custom_call" | custom-call | flops 6000000000 | bytes 12058624 | tf_op jit(solution)/shard_map/local_backward/pallas_call | solution.py:249
  118.7 0.0 collective-permute-done.10
  118.7 2.5 %collective-permute-done.11 = bf16[192,1024]{1,0:T(8,128)(2,1)S(1)} collective-permute-done((bf16[192,1024]{1,0:T(8,128)(2,1)S(1)}, bf16[192,1024]{1,0:T(8,128)(2,1)S(1)}, u32[]{:S(2)}, u32[]{:S(2)}) %collective-permute-start.11) | collective-permute-done | bytes 393248 | tf_op jit(solution)/shard_map/ppermute | solution.py:281
  121.2 2.3 %collective-permute-done.9 = bf16[192,1024]{1,0:T(8,128)(2,1)S(1)} collective-permute-done((bf16[192,1024]{1,0:T(8,128)(2,1)S(1)}, bf16[192,1024]{1,0:T(8,128)(2,1)S(1)}, u32[]{:S(2)}, u32[]{:S(2)}) %collective-permute-start.9) | collective-permute-done | bytes 393248 | tf_op jit(solution)/shard_map/ppermute | solution.py:281
  123.5 0.3 add_convert_fusion.1
  123.8 0.8 pad_maximum_fusion
  124.6 4.2 %all-to-all-start.3 = ((bf16[8,24,1024]{2,1,0:T(8,128)(2,1)}), bf16[8,24,1024]{2,1,0:T(8,128)(2,1)S(1)}, u32[]{:S(2)}, u32[]{:S(2)}) async-start(bf16[8,24,1024]{2,1,0:T(8,128)(2,1)} %pad_maximum_fusion), calls=%async_computation.3 | async-start | bytes 786432 | tf_op jit(solution)/shard_map/all_to_all | solution.py:289
  128.8 6.3 %local_backward.3 = (bf16[256,1024]{1,0:T(8,128)(2,1)}, f32[2,256,1024]{2,1,0:T(8,128)}, bf16[2,256,1024]{2,1,0:T(8,128)(2,1)}, bf16[2,256,1024]{2,1,0:T(8,128)(2,1)}) custom-call(s32[8]{0:T(128)} %copy-done.6, bf16[256,1024]{1,0:T(8,128)(2,1)} %bitcast.34, ...), custom_call_target="tpu_custom_call", output_to_operand_aliasing={{0}: (9, {}), {1}: (10, {}), {2}: (11, {}), {3}: (12, {})} | custom-call | flops 2000000000 | bytes 16777216 | tf_op jit(solution)/shard_map/local_backward/pallas_call | solution.py:249
  135.2 0.8 collective-permute-start.15
  136.0 1.9 %collective-permute-start.16 = (bf16[2,256,1024]{2,1,0:T(8,128)(2,1)}, bf16[2,256,1024]{2,1,0:T(8,128)(2,1)}, u32[]{:S(2)}, u32[]{:S(2)}) collective-permute-start(bf16[2,256,1024]{2,1,0:T(8,128)(2,1)} %get-tuple-element.137), channel_id=1, source_target_pairs={{1,2},{2,1},{3,4},{4,3},{5,6},{6,5},{7,8},{8,7},{9,10},{10,9},{11,... | collective-permute-start | bytes 3145736 | tf_op jit(solution)/shard_map/ppermute | solution.py:281
  137.9 6.0 %all-to-all-done.3 = bf16[8,24,1024]{2,1,0:T(8,128)(2,1)S(1)} async-done(((bf16[8,24,1024]{2,1,0:T(8,128)(2,1)}), bf16[8,24,1024]{2,1,0:T(8,128)(2,1)S(1)}, u32[]{:S(2)}, u32[]{:S(2)}) %all-to-all-start.3) | async-done | bytes 393248 | tf_op jit(solution)/shard_map/all_to_all | solution.py:289
  143.9 0.9 broadcast_in_dim.27
  144.8 4.6 %all-to-all-start.4 = ((bf16[32,8,1024]{2,1,0:T(8,128)(2,1)}), bf16[32,8,1024]{2,1,0:T(8,128)(2,1)}, u32[]{:S(2)}, u32[]{:S(2)}) async-start(bf16[32,8,1024]{2,1,0:T(8,128)(2,1)} %broadcast_in_dim.27), calls=%async_computation.4 | async-start | bytes 1048576 | tf_op jit(solution)/shard_map/all_to_all | solution.py:297
  149.5 1.4 collective-permute-start.12
  150.9 2.6 %collective-permute-start.13 = (f32[16,1024]{1,0:T(8,128)S(1)}, f32[16,1024]{1,0:T(8,128)S(1)}, u32[]{:S(2)}, u32[]{:S(2)}) collective-permute-start(f32[16,1024]{1,0:T(8,128)S(1)} %convert_reduce_fusion), channel_id=1, source_target_pairs={{0,128},{64,192},{128,0},{192,64},{1,129},{65,193},{129,1},{193,65... | collective-permute-start | bytes 196616 | tf_op jit(solution)/shard_map/ppermute | solution.py:422
  153.5 1.1 collective-permute-start.14
  154.5 0.0 collective-permute-done.15
  154.5 0.0 collective-permute-done.16
  154.5 2.7 %add_convert_fusion.base = bf16[2,256,1024]{2,1,0:T(8,128)(2,1)S(1)} fusion(bf16[2,256,1024]{2,1,0:T(8,128)(2,1)} %collective-permute-done.16, f32[2,256,1024]{2,1,0:T(8,128)} %get-tuple-element.135, bf16[2,256,1024]{2,1,0:T(8,128)(2,1)} %collective-permute-done.15), kind=kLoop, calls=%fused_computation | loop fusion | flops 2621440 | bytes 5242880 | tf_op jit(solution)/shard_map/convert_element_type | solution.py:424
  157.3 9.2 %all-to-all-done.4 = bf16[32,8,1024]{2,1,0:T(8,128)(2,1)} async-done(((bf16[32,8,1024]{2,1,0:T(8,128)(2,1)}), bf16[32,8,1024]{2,1,0:T(8,128)(2,1)}, u32[]{:S(2)}, u32[]{:S(2)}) %all-to-all-start.4) | async-done | bytes 524320 | tf_op jit(solution)/shard_map/all_to_all | solution.py:297
  166.5 2.3 %collective-permute-start.17 = (bf16[256,1024]{1,0:T(8,128)(2,1)}, bf16[256,1024]{1,0:T(8,128)(2,1)S(1)}, u32[]{:S(2)}, u32[]{:S(2)}) collective-permute-start(bf16[256,1024]{1,0:T(8,128)(2,1)} %bitcast.16.far_half), channel_id=1, source_target_pairs={{0,1},{1,0},{2,3},{3,2},{4,5},{5,4},{6,7},{7,6},{8,9},{9,8},{10,11... | collective-permute-start | bytes 1572872 | tf_op jit(solution)/shard_map/ppermute | solution.py:281
  168.8 0.6 add_add_fusion
  169.5 1.1 collective-permute-done.17.far_rest
  170.6 2.3 %combine.1 = (bf16[256,1024]{1,0:T(8,128)(2,1)}, bf16[256,1024]{1,0:T(8,128)(2,1)}) custom-call(s32[8]{0:T(128)S(1)} %copy-done.8, bf16[2,256,1024]{2,1,0:T(8,128)(2,1)S(1)} %add_convert_fusion.base, bf16[256,1024]{1,0:T(8,128)(2,1)} %bitcast.16.far_half, bf16[256,1024]{1,0:T(8,128)(2,1)S(1)} %collective-permute-done.17.far_rest), custom_call_target="tpu_custom_call" | custom-call | tf_op jit(solution)/shard_map/combine/pallas_call | solution.py:194
  (26 shorter events, 0.1 us)
Async XLA Ops:
  0.6 61.8 %copy-start = (bf16[1024,1024]{1,0:T(8,128)(2,1)S(1)}, bf16[1024,1024]{1,0:T(8,128)(2,1)}, u32[]{:S(2)}) copy-start(bf16[1024,1024]{1,0:T(8,128)(2,1)} %param.11) | copy-start | bytes 6291460
  1.4 1.0 copy-start.4
  2.5 1.0 copy-start.5
  3.5 0.7 copy-start.9
  5.4 59.7 %copy-start.2 = (bf16[2,256,1024]{2,1,0:T(8,128)(2,1)}, bf16[2,256,1024]{2,1,0:T(8,128)(2,1)S(1)}, u32[]{:S(2)}) copy-start(bf16[2,256,1024]{2,1,0:T(8,128)(2,1)S(1)} %get-tuple-element.88.own.refs_2_) | copy-start | bytes 3145732
  5.4 25.5 %collective-permute-start = (bf16[2,64,1024]{2,1,0:T(8,128)(2,1)S(1)}, bf16[2,64,1024]{2,1,0:T(8,128)(2,1)S(1)}, u32[]{:S(2)}, u32[]{:S(2)}) collective-permute-start(bf16[2,64,1024]{2,1,0:T(8,128)(2,1)S(1)} %get-tuple-element.78), channel_id=1, source_target_pairs={{0,2},{1,3},{2,4},{3,5},{4,6},{5,7},{6,0},{7,1},{8,10},{9,11},{10,... | collective-permute-start | bytes 786440 | tf_op jit(solution)/shard_map/ppermute | solution.py:281
  7.5 23.3 %collective-permute-start.1 = (bf16[2,64,1024]{2,1,0:T(8,128)(2,1)S(1)}, bf16[2,64,1024]{2,1,0:T(8,128)(2,1)S(1)}, u32[]{:S(2)}, u32[]{:S(2)}) collective-permute-start(bf16[2,64,1024]{2,1,0:T(8,128)(2,1)S(1)} %get-tuple-element.79), channel_id=1, source_target_pairs={{0,4},{1,5},{2,6},{3,7},{4,0},{5,1},{6,2},{7,3},{8,12},{9,13},{10,... | collective-permute-start | bytes 786440 | tf_op jit(solution)/shard_map/ppermute | solution.py:281
  9.9 20.9 %collective-permute-start.2 = (bf16[2,64,1024]{2,1,0:T(8,128)(2,1)S(1)}, bf16[2,64,1024]{2,1,0:T(8,128)(2,1)S(1)}, u32[]{:S(2)}, u32[]{:S(2)}) collective-permute-start(bf16[2,64,1024]{2,1,0:T(8,128)(2,1)S(1)} %get-tuple-element.80), channel_id=1, source_target_pairs={{0,6},{1,7},{2,0},{3,1},{4,2},{5,3},{6,4},{7,5},{8,14},{9,15},{10,... | collective-permute-start | bytes 786440 | tf_op jit(solution)/shard_map/ppermute | solution.py:281
  32.3 32.8 %copy-start.6 = (s32[8]{0:T(128)}, s32[8]{0:T(128)S(1)}, u32[]{:S(2)}) copy-start(s32[8]{0:T(128)S(1)} %get-tuple-element.81.flags) | copy-start | bytes 100
  32.3 2.0 %collective-permute-start.3 = (bf16[64,1024]{1,0:T(8,128)(2,1)S(1)}, bf16[64,1024]{1,0:T(8,128)(2,1)S(1)}, u32[]{:S(2)}, u32[]{:S(2)}) collective-permute-start(bf16[64,1024]{1,0:T(8,128)(2,1)S(1)} %get-tuple-element.83), channel_id=1, source_target_pairs={{0,1},{1,0},{2,3},{3,2},{4,5},{5,4},{6,7},{7,6},{8,9},{9,8},{10,11... | collective-permute-start | bytes 393224 | tf_op jit(solution)/shard_map/ppermute | solution.py:281
  35.0 13.8 %collective-permute-start.4 = (bf16[2,256,1024]{2,1,0:T(8,128)(2,1)S(1)}, bf16[2,256,1024]{2,1,0:T(8,128)(2,1)}, u32[]{:S(2)}, u32[]{:S(2)}) collective-permute-start(bf16[2,256,1024]{2,1,0:T(8,128)(2,1)S(1)} %get-tuple-element.88.own.refs_2_), channel_id=1, source_target_pairs={{0,1},{1,0},{2,3},{3,2},{4,5},{5,4},{6,7},{7,6},{8,9},{9,8},{10,11... | collective-permute-start | bytes 3145736 | tf_op jit(solution)/shard_map/ppermute | solution.py:281
  35.1 16.2 %collective-permute-start.5 = (bf16[2,256,1024]{2,1,0:T(8,128)(2,1)S(1)}, bf16[2,256,1024]{2,1,0:T(8,128)(2,1)}, u32[]{:S(2)}, u32[]{:S(2)}) collective-permute-start(bf16[2,256,1024]{2,1,0:T(8,128)(2,1)S(1)} %get-tuple-element.88.own.refs_2_), channel_id=1, source_target_pairs={{1,2},{2,1},{3,4},{4,3},{5,6},{6,5},{7,8},{8,7},{9,10},{10,9},{11,... | collective-permute-start | bytes 3145736 | tf_op jit(solution)/shard_map/ppermute | solution.py:281
  37.6 11.3 %all-to-all-start.1 = ((bf16[8,8,1024]{2,1,0:T(8,128)(2,1)}), bf16[8,8,1024]{2,1,0:T(8,128)(2,1)S(1)}, u32[]{:S(2)}, u32[]{:S(2)}) async-start(bf16[8,8,1024]{2,1,0:T(8,128)(2,1)} %bitcast.5), calls=%async_computation.1 | async-start | bytes 262144 | tf_op jit(solution)/shard_map/all_to_all | solution.py:289
  52.1 27.2 %all-to-all-start.2 = ((bf16[32,8,1024]{2,1,0:T(8,128)(2,1)}), bf16[32,8,1024]{2,1,0:T(8,128)(2,1)}, u32[]{:S(2)}, u32[]{:S(2)}) async-start(bf16[32,8,1024]{2,1,0:T(8,128)(2,1)} %broadcast_in_dim.24), calls=%async_computation.2 | async-start | bytes 1048576 | tf_op jit(solution)/shard_map/all_to_all | solution.py:297
  79.3 2.4 %collective-permute-start.6 = (bf16[256,1024]{1,0:T(8,128)(2,1)}, bf16[256,1024]{1,0:T(8,128)(2,1)S(1)}, u32[]{:S(2)}, u32[]{:S(2)}) collective-permute-start(bf16[256,1024]{1,0:T(8,128)(2,1)} %bitcast.8.half), channel_id=1, source_target_pairs={{0,1},{1,0},{2,3},{3,2},{4,5},{5,4},{6,7},{7,6},{8,9},{9,8},{10,11... | collective-permute-start | bytes 1572872 | tf_op jit(solution)/shard_map/ppermute | solution.py:281
  81.7 0.8 copy-start.10
  97.8 3.7 %copy-start.1 = (f32[4,8,16,1024]{3,2,1,0:T(8,128)S(1)}, f32[4,8,16,1024]{3,2,1,0:T(8,128)}, u32[]{:S(2)}) copy-start(f32[4,8,16,1024]{3,2,1,0:T(8,128)} %get-tuple-element.105.kept) | copy-start | bytes 6291460
  97.9 3.7 %copy-start.3 = (bf16[256,1024]{1,0:T(8,128)(2,1)S(1)}, bf16[256,1024]{1,0:T(8,128)(2,1)}, u32[]{:S(2)}) copy-start(bf16[256,1024]{1,0:T(8,128)(2,1)} %get-tuple-element.103) | copy-start | bytes 1572868
  97.9 3.7 %copy-start.7 = (s32[8]{0:T(128)S(1)}, s32[8]{0:T(128)}, u32[]{:S(2)}) copy-start(s32[8]{0:T(128)} %copy-done.6) | copy-start | bytes 100
  97.9 3.7 %collective-permute-start.8 = (bf16[4,8,16,1024]{3,2,1,0:T(8,128)(2,1)}, bf16[4,8,16,1024]{3,2,1,0:T(8,128)(2,1)S(1)}, u32[]{:S(2)}, u32[]{:S(2)}) collective-permute-start(bf16[4,8,16,1024]{3,2,1,0:T(8,128)(2,1)} %get-tuple-element.100), channel_id=1, source_target_pairs={{0,1},{1,0},{2,3},{3,2},{4,5},{5,4},{6,7},{7,6},{8,9},{9,8},{10,11... | collective-permute-start | bytes 3145736 | tf_op jit(solution)/shard_map/ppermute | solution.py:281
  98.3 3.2 %collective-permute-start.7 = (bf16[256,1024]{1,0:T(8,128)(2,1)}, bf16[256,1024]{1,0:T(8,128)(2,1)S(1)}, u32[]{:S(2)}, u32[]{:S(2)}) collective-permute-start(bf16[256,1024]{1,0:T(8,128)(2,1)} %get-tuple-element.99), channel_id=1, source_target_pairs={{0,1},{1,0},{2,3},{3,2},{4,5},{5,4},{6,7},{7,6},{8,9},{9,8},{10,11... | collective-permute-start | bytes 1572872 | tf_op jit(solution)/shard_map/ppermute | solution.py:281
  102.5 16.2 %collective-permute-start.10 = (bf16[192,1024]{1,0:T(8,128)(2,1)S(1)}, bf16[192,1024]{1,0:T(8,128)(2,1)S(1)}, u32[]{:S(2)}, u32[]{:S(2)}) collective-permute-start(bf16[192,1024]{1,0:T(8,128)(2,1)S(1)} %get-tuple-element.114), channel_id=1, source_target_pairs={{0,4},{1,5},{2,6},{3,7},{4,0},{5,1},{6,2},{7,3},{8,12},{9,13},{10,... | collective-permute-start | bytes 1179656 | tf_op jit(solution)/shard_map/ppermute | solution.py:281
  103.8 17.4 %collective-permute-start.11 = (bf16[192,1024]{1,0:T(8,128)(2,1)S(1)}, bf16[192,1024]{1,0:T(8,128)(2,1)S(1)}, u32[]{:S(2)}, u32[]{:S(2)}) collective-permute-start(bf16[192,1024]{1,0:T(8,128)(2,1)S(1)} %get-tuple-element.115), channel_id=1, source_target_pairs={{0,6},{1,7},{2,0},{3,1},{4,2},{5,3},{6,4},{7,5},{8,14},{9,15},{10,... | collective-permute-start | bytes 1179656 | tf_op jit(solution)/shard_map/ppermute | solution.py:281
  104.9 18.6 %collective-permute-start.9 = (bf16[192,1024]{1,0:T(8,128)(2,1)S(1)}, bf16[192,1024]{1,0:T(8,128)(2,1)S(1)}, u32[]{:S(2)}, u32[]{:S(2)}) collective-permute-start(bf16[192,1024]{1,0:T(8,128)(2,1)S(1)} %get-tuple-element.113), channel_id=1, source_target_pairs={{0,2},{1,3},{2,4},{3,5},{4,6},{5,7},{6,0},{7,1},{8,10},{9,11},{10,... | collective-permute-start | bytes 1179656 | tf_op jit(solution)/shard_map/ppermute | solution.py:281
  124.6 19.3 %all-to-all-start.3 = ((bf16[8,24,1024]{2,1,0:T(8,128)(2,1)}), bf16[8,24,1024]{2,1,0:T(8,128)(2,1)S(1)}, u32[]{:S(2)}, u32[]{:S(2)}) async-start(bf16[8,24,1024]{2,1,0:T(8,128)(2,1)} %pad_maximum_fusion), calls=%async_computation.3 | async-start | bytes 786432 | tf_op jit(solution)/shard_map/all_to_all | solution.py:289
  135.2 19.3 %collective-permute-start.15 = (bf16[2,256,1024]{2,1,0:T(8,128)(2,1)}, bf16[2,256,1024]{2,1,0:T(8,128)(2,1)}, u32[]{:S(2)}, u32[]{:S(2)}) collective-permute-start(bf16[2,256,1024]{2,1,0:T(8,128)(2,1)} %get-tuple-element.136), channel_id=1, source_target_pairs={{0,1},{1,0},{2,3},{3,2},{4,5},{5,4},{6,7},{7,6},{8,9},{9,8},{10,11... | collective-permute-start | bytes 3145736 | tf_op jit(solution)/shard_map/ppermute | solution.py:281
  136.0 18.6 %collective-permute-start.16 = (bf16[2,256,1024]{2,1,0:T(8,128)(2,1)}, bf16[2,256,1024]{2,1,0:T(8,128)(2,1)}, u32[]{:S(2)}, u32[]{:S(2)}) collective-permute-start(bf16[2,256,1024]{2,1,0:T(8,128)(2,1)} %get-tuple-element.137), channel_id=1, source_target_pairs={{1,2},{2,1},{3,4},{4,3},{5,6},{6,5},{7,8},{8,7},{9,10},{10,9},{11,... | collective-permute-start | bytes 3145736 | tf_op jit(solution)/shard_map/ppermute | solution.py:281
  144.8 21.7 %all-to-all-start.4 = ((bf16[32,8,1024]{2,1,0:T(8,128)(2,1)}), bf16[32,8,1024]{2,1,0:T(8,128)(2,1)}, u32[]{:S(2)}, u32[]{:S(2)}) async-start(bf16[32,8,1024]{2,1,0:T(8,128)(2,1)} %broadcast_in_dim.27), calls=%async_computation.4 | async-start | bytes 1048576 | tf_op jit(solution)/shard_map/all_to_all | solution.py:297
  149.5 21.1 %copy-start.8 = (s32[8]{0:T(128)S(1)}, s32[8]{0:T(128)}, u32[]{:S(2)}) copy-start(s32[8]{0:T(128)} %copy-done.6) | copy-start | bytes 100
  149.5 7.8 %collective-permute-start.12 = (f32[16,1024]{1,0:T(8,128)S(1)}, f32[16,1024]{1,0:T(8,128)S(1)}, u32[]{:S(2)}, u32[]{:S(2)}) collective-permute-start(f32[16,1024]{1,0:T(8,128)S(1)} %convert_reduce_fusion), channel_id=1, source_target_pairs={{0,64},{64,128},{128,192},{192,0},{1,65},{65,129},{129,193},{193,1... | collective-permute-start | bytes 196616 | tf_op jit(solution)/shard_map/ppermute | solution.py:422
  150.9 6.4 %collective-permute-start.13 = (f32[16,1024]{1,0:T(8,128)S(1)}, f32[16,1024]{1,0:T(8,128)S(1)}, u32[]{:S(2)}, u32[]{:S(2)}) collective-permute-start(f32[16,1024]{1,0:T(8,128)S(1)} %convert_reduce_fusion), channel_id=1, source_target_pairs={{0,128},{64,192},{128,0},{192,64},{1,129},{65,193},{129,1},{193,65... | collective-permute-start | bytes 196616 | tf_op jit(solution)/shard_map/ppermute | solution.py:422
  153.5 3.8 %collective-permute-start.14 = (f32[16,1024]{1,0:T(8,128)S(1)}, f32[16,1024]{1,0:T(8,128)S(1)}, u32[]{:S(2)}, u32[]{:S(2)}) collective-permute-start(f32[16,1024]{1,0:T(8,128)S(1)} %convert_reduce_fusion), channel_id=1, source_target_pairs={{0,192},{64,0},{128,64},{192,128},{1,193},{65,1},{129,65},{193,129... | collective-permute-start | bytes 196616 | tf_op jit(solution)/shard_map/ppermute | solution.py:422
  166.5 4.1 %collective-permute-start.17 = (bf16[256,1024]{1,0:T(8,128)(2,1)}, bf16[256,1024]{1,0:T(8,128)(2,1)S(1)}, u32[]{:S(2)}, u32[]{:S(2)}) collective-permute-start(bf16[256,1024]{1,0:T(8,128)(2,1)} %bitcast.16.far_half), channel_id=1, source_target_pairs={{0,1},{1,0},{2,3},{3,2},{4,5},{5,4},{6,7},{7,6},{8,9},{9,8},{10,11... | collective-permute-start | bytes 1572872 | tf_op jit(solution)/shard_map/ppermute | solution.py:281

commit v5 on v4

--- a/solution.py
+++ b/solution.py
@@ -30,14 +30,14 @@
     return [lane < HEAD_DIM, lane >= HEAD_DIM]
 
 
-def local_forward(flags, q, own, core, chip, m_out, l_out, o_out):
+def local_forward(flags, q, own, core, chip_key, chip_value, m_out, l_out, o_out):
     seen = [None, flags[0] > 0, flags[1] > 0]
     for g in range(SPAN // 128):
         cols = pl.ds(g * 128, 128)
         queries = q[:, cols] * 0.125
         masks = half_masks(queries.shape)
-        keys = [ref[0, :, cols] for ref in (own, core, chip)]
-        vals = [ref[1, :, cols] for ref in (own, core, chip)]
+        keys = [own[0, :, cols], core[0, :, cols], chip_key[:, cols]]
+        vals = [own[1, :, cols], core[1, :, cols], chip_value[:, cols]]
         tops, sums, mixes = [], [], []
         for mask in masks:
             part = jnp.where(mask, queries, 0).astype(BF16)
@@ -112,7 +112,8 @@
 
 
 def local_backward(
-    flags, q, d, own, core, chip, lse_in, cen_in, dq_in, dq_out, own_out, core_out, chip_out
+    flags, q, d, own, core, chip_key, chip_value, lse_in, cen_in, dq_in,
+    dq_out, own_out, core_out, chip_out,
 ):
     seen = [None, flags[0] > 0, flags[1] > 0]
     for g in range(SPAN // 128):
@@ -120,8 +121,8 @@
         queries = q[:, cols] * 0.125
         grads = d[:, cols]
         masks = half_masks(queries.shape)
-        keys = [ref[0, :, cols] for ref in (own, core, chip)]
-        vals = [ref[1, :, cols] for ref in (own, core, chip)]
+        keys = [own[0, :, cols], core[0, :, cols], chip_key[:, cols]]
+        vals = [own[1, :, cols], core[1, :, cols], chip_value[:, cols]]
         lse, cens = lse_in[:, cols], cen_in[:, cols]
         parts = [jnp.where(m, queries, 0).astype(BF16) for m in masks]
         gparts = [jnp.where(m, grads, 0).astype(BF16) for m in masks]
@@ -202,7 +203,7 @@
 
 
 def local_backward_into(flags, *refs):
-    local_backward(flags, *refs[:8], *refs[12:])
+    local_backward(flags, *refs[:9], *refs[13:])
 
 
 def choose(flags, ids, own, one, two, three, mine_out, other_out, flags_out):
@@ -335,8 +336,8 @@
         1,
     )
     part = jnp.where(flags[7] > 0, mine, send(other, hop(dc=1)))
-    part, pair = lax.optimization_barrier((part, pair))
-    near = [pair, send(pair, CORE), send(pair, CHIP)]
+    part, pair, value = lax.optimization_barrier((part, pair, value))
+    near = [pair, send(pair, CORE), send(key, CHIP), send(value, CHIP)]
     share = pick(swap_z(part.reshape(NZ, eighth, width)), flags[6])
     share, near = lax.optimization_barrier((share, near))
 

time: 174 us -> 173 us (level)
  waiting for transfers between devices: 36.2 us -> 27.8 us
  starting transfers between devices: 45.9 us -> 52.9 us
    ppermute x15 -> x16, waiting for transfers between devices: 10.6 us -> 5.96 us  [send(): return lax.ppermute(value, 'region', pairs)]
    all_to_all x2, waiting for transfers between devices: 12 us -> 7.82 us  [swap_z(): lax.all_to_all(value, 'region', 0, 0, axis_index_groups=Z_GROUPS, tiled=T...]
    ppermute x15 -> x16, starting transfers between devices: 18.2 us -> 22.1 us  [send(): return lax.ppermute(value, 'region', pairs)]
    all_to_all x2, starting transfers between devices: 14.9 us -> 18.1 us  [gather_plane(): lax.all_to_all(jnp.broadcast_to(value[None], (count,) + value.shape), 're...]
  transfers between devices with their start and end apart: 22 -> 23, of which waited for: 10 -> 9; matrix products, arithmetic and copies ran while one was open for 6% -> 6% of each run, Pallas kernels for 17% -> 17%
where the time goes in v5:
time: 173 us; the launch traced here: 172 us
  starting transfers between devices  52.9 us (31%)
  Pallas kernels  51.4 us (30%)
  waiting for transfers between devices  27.8 us (16%)
  blocking collectives  19.7 us (11%)
  other arithmetic  5.94 us (3%)
  matrix products  5.16 us (3%)
  local copies, waits for them, and re-layouts  4.81 us (3%)
  between operations  4.3 us (2%)
    pallas_call x4, Pallas kernels, call(): pl.pallas_call(body, grid_spec=pltpu.PrefetchScalarGridSpec(num_scalar_pr...  44.9 us
    ppermute x16, starting transfers between devices, send(): return lax.ppermute(value, 'region', pairs)  22.1 us
    all_to_all x1, blocking collectives, on_device(): ids = lax.all_to_all(ids, 'region', 0, 0, tiled=True)  19.7 us
    all_to_all x2, starting transfers between devices, gather_plane(): lax.all_to_all(jnp.broadcast_to(value[None], (count,) + value.shape), 're...  18.1 us
    all_to_all x2, waiting for transfers between devices, gather_plane(): lax.all_to_all(jnp.broadcast_to(value[None], (count,) + value.shape), 're...  14 us
    all_to_all x2, waiting for transfers between devices, swap_z(): lax.all_to_all(value, 'region', 0, 0, axis_index_groups=Z_GROUPS, tiled=T...  7.82 us
    all_to_all x2, starting transfers between devices, swap_z(): lax.all_to_all(value, 'region', 0, 0, axis_index_groups=Z_GROUPS, tiled=T...  7.63 us
    pallas_call x4, Pallas kernels, simple(): pl.pallas_call(body, in_specs=[smem] * scalars + [vmem] * (len(ins) - sca...  6.4 us
  transfers between devices with their start and end apart: 23, of which 9 were waited for; matrix products, arithmetic and copies ran while one was open for 6% of the time, Pallas kernels for 17%

profile of v5, /device:TPU:1, one launch (start us, length us, event | category | flops | bytes accessed | tf_op | source)
XLA Modules:
  0.0 172.0 jit_solution(7901612560356937784)
XLA Ops:
  0.6 0.0 copy-start
  1.5 0.6 copy-done.7
  2.1 1.8 %prepare.1 = (s32[64,1,128]{2,1,0:T(1,128)S(1)}, s32[8]{0:T(128)S(1)}, bf16[2,256,1024]{2,1,0:T(8,128)(2,1)S(1)}, bf16[2,64,1024]{2,1,0:T(8,128)(2,1)S(1)}, bf16...) custom-call(s32[1]{0:T(128)} %bitcast.spot, ...), custom_call_target="tpu_custom_call" | custom-call | tf_op jit(solution)/shard_map/prepare/pallas_call | solution.py:195
  4.0 2.1 %collective-permute-start = (bf16[2,64,1024]{2,1,0:T(8,128)(2,1)S(1)}, bf16[2,64,1024]{2,1,0:T(8,128)(2,1)S(1)}, u32[]{:S(2)}, u32[]{:S(2)}) collective-permute-start(bf16[2,64,1024]{2,1,0:T(8,128)(2,1)S(1)} %get-tuple-element.80), channel_id=1, source_target_pairs={{0,2},{1,3},{2,4},{3,5},{4,6},{5,7},{6,0},{7,1},{8,10},{9,11},{10,... | collective-permute-start | bytes 786440 | tf_op jit(solution)/shard_map/ppermute | solution.py:282
  6.1 2.5 %collective-permute-start.1 = (bf16[2,64,1024]{2,1,0:T(8,128)(2,1)S(1)}, bf16[2,64,1024]{2,1,0:T(8,128)(2,1)S(1)}, u32[]{:S(2)}, u32[]{:S(2)}) collective-permute-start(bf16[2,64,1024]{2,1,0:T(8,128)(2,1)S(1)} %get-tuple-element.81), channel_id=1, source_target_pairs={{0,4},{1,5},{2,6},{3,7},{4,0},{5,1},{6,2},{7,3},{8,12},{9,13},{10,... | collective-permute-start | bytes 786440 | tf_op jit(solution)/shard_map/ppermute | solution.py:282
  8.5 1.2 collective-permute-start.2
  9.7 19.7 %all_to_all.25.ids = s32[64,1,128]{2,1,0:T(1,128)S(1)} all-to-all(s32[64,1,128]{2,1,0:T(1,128)S(1)} %get-tuple-element.78), channel_id=1, replica_groups=mesh['dp'=4,'region'=64] {'region'}, dimensions={0} | all-to-all | bytes 65536 | tf_op jit(solution)/shard_map/all_to_all | solution.py:330
  29.4 0.0 collective-permute-done.2.three
  29.4 1.4 choose.1
  30.9 0.8 collective-permute-start.3
  31.6 0.6 fusion.1
  32.9 0.7 broadcast_select_fusion
  33.5 0.1 collective-permute-start.4
  33.6 2.5 %collective-permute-start.5 = (bf16[256,1024]{1,0:T(8,128)(2,1)}, bf16[256,1024]{1,0:T(8,128)(2,1)}, u32[]{:S(2)}, u32[]{:S(2)}) collective-permute-start(bf16[256,1024]{1,0:T(8,128)(2,1)} %bitcast.1.key), channel_id=1, source_target_pairs={{1,2},{2,1},{3,4},{4,3},{5,6},{6,5},{7,8},{8,7},{9,10},{10,9},{11,... | collective-permute-start | bytes 1572872 | tf_op jit(solution)/shard_map/ppermute | solution.py:282
  36.1 3.1 %collective-permute-start.6 = (bf16[256,1024]{1,0:T(8,128)(2,1)}, bf16[256,1024]{1,0:T(8,128)(2,1)}, u32[]{:S(2)}, u32[]{:S(2)}) collective-permute-start(bf16[256,1024]{1,0:T(8,128)(2,1)} %bitcast.2.value), channel_id=1, source_target_pairs={{1,2},{2,1},{3,4},{4,3},{5,6},{6,5},{7,8},{8,7},{9,10},{10,9},{11,... | collective-permute-start | bytes 1572872 | tf_op jit(solution)/shard_map/ppermute | solution.py:282
  39.2 3.4 %all-to-all-start.1 = ((bf16[8,8,1024]{2,1,0:T(8,128)(2,1)}), bf16[8,8,1024]{2,1,0:T(8,128)(2,1)S(1)}, u32[]{:S(2)}, u32[]{:S(2)}) async-start(bf16[8,8,1024]{2,1,0:T(8,128)(2,1)} %bitcast.5), calls=%async_computation.1 | async-start | bytes 262144 | tf_op jit(solution)/shard_map/all_to_all | solution.py:290
  44.5 6.0 %all-to-all-done.1 = bf16[8,8,1024]{2,1,0:T(8,128)(2,1)S(1)} async-done(((bf16[8,8,1024]{2,1,0:T(8,128)(2,1)}), bf16[8,8,1024]{2,1,0:T(8,128)(2,1)S(1)}, u32[]{:S(2)}, u32[]{:S(2)}) %all-to-all-start.1) | async-done | bytes 131104 | tf_op jit(solution)/shard_map/all_to_all | solution.py:290
  50.5 0.0 collective-permute-done.5.chip_key.refs_4_
  50.5 0.0 collective-permute-done.6.chip_value.refs_5_
  50.6 0.0 collective-permute-done.4.core.refs_3_
  50.6 0.9 broadcast_in_dim.24
  51.4 9.8 %all-to-all-start.2 = ((bf16[32,8,1024]{2,1,0:T(8,128)(2,1)}), bf16[32,8,1024]{2,1,0:T(8,128)(2,1)}, u32[]{:S(2)}, u32[]{:S(2)}) async-start(bf16[32,8,1024]{2,1,0:T(8,128)(2,1)} %broadcast_in_dim.24), calls=%async_computation.2 | async-start | bytes 1048576 | tf_op jit(solution)/shard_map/all_to_all | solution.py:298
  61.3 2.6 %convolution_convert_fusion.1.d.refs_1_ = bf16[256,1024]{1,0:T(8,128)(2,1)} fusion(bf16[1024,1024]{1,0:T(8,128)(2,1)S(1)} %copy-done, bf16[1,256,1024]{2,1,0:T(8,128)(2,1)} %param.10), kind=kOutput, calls=%fused_computation.2 | convolution fusion | flops 537133056 | bytes 3145728 | tf_op jit(solution)/shard_map/dot_general | solution.py:354
  63.9 9.9 %local_forward.1 = (f32[256,1024]{1,0:T(8,128)}, f32[256,1024]{1,0:T(8,128)}, f32[256,1024]{1,0:T(8,128)}) custom-call(s32[8]{0:T(128)} %copy-done.4, bf16[256,1024]{1,0:T(8,128)(2,1)} %bitcast.29, bf16[2,256,1024]{2,1,0:T(8,128)(2,1)} %copy-done.2, bf16[2,256,1024]{2,1,0:T(8,128)(2,1)} %collective-permute-done.4.core.refs_3_, ...), custom_call_target="tpu_custom_call" | custom-call | flops 5000000000 | bytes 6815744 | tf_op jit(solution)/shard_map/local_forward/pallas_call | solution.py:250
  73.8 4.4 %all-to-all-done.2 = bf16[32,8,1024]{2,1,0:T(8,128)(2,1)} async-done(((bf16[32,8,1024]{2,1,0:T(8,128)(2,1)}), bf16[32,8,1024]{2,1,0:T(8,128)(2,1)}, u32[]{:S(2)}, u32[]{:S(2)}) %all-to-all-start.2) | async-done | bytes 524320 | tf_op jit(solution)/shard_map/all_to_all | solution.py:298
  78.1 0.6 collective-permute-start.7
  78.7 1.7 %collective-permute-done.7.rest = bf16[256,1024]{1,0:T(8,128)(2,1)S(1)} collective-permute-done((bf16[256,1024]{1,0:T(8,128)(2,1)}, bf16[256,1024]{1,0:T(8,128)(2,1)S(1)}, u32[]{:S(2)}, u32[]{:S(2)}) %collective-permute-start.7) | collective-permute-done | bytes 524320 | tf_op jit(solution)/shard_map/ppermute | solution.py:282
  80.5 0.8 copy-done.10
  81.3 15.3 %hub_block.1 = (bf16[256,1024]{1,0:T(8,128)(2,1)}, f32[256,1024]{1,0:T(8,128)}, f32[256,1024]{1,0:T(8,128)}, f32[256,1024]{1,0:T(8,128)}, bf16[256,1024]{1,0:T(8...) custom-call(s32[8]{0:T(128)} %copy-done.4, ...), custom_call_target="tpu_custom_call" | custom-call | flops 8999999488 | bytes 13631488 | tf_op jit(solution)/shard_map/hub_block/pallas_call | solution.py:250
  96.6 0.5 collective-permute-start.9
  97.1 0.3 collective-permute-start.8
  97.4 2.6 %convolution_convert_fusion = bf16[256,1024]{1,0:T(8,128)(2,1)} fusion(bf16[256,1024]{1,0:T(8,128)(2,1)} %get-tuple-element.105, bf16[1024,1024]{1,0:T(8,128)(2,1)S(1)} %copy-done), kind=kOutput, calls=%fused_computation.1 | convolution fusion | flops 537133056 | bytes 3145728 | tf_op jit(solution)/shard_map/dot_general | solution.py:25
  100.0 0.4 collective-permute-done.8
  100.4 0.0 collective-permute-done.9.turned
  100.4 0.8 add_pieces.1
  101.2 0.1 collective-permute-start.10
  101.3 1.9 %collective-permute-start.11 = (bf16[192,1024]{1,0:T(8,128)(2,1)S(1)}, bf16[192,1024]{1,0:T(8,128)(2,1)S(1)}, u32[]{:S(2)}, u32[]{:S(2)}) collective-permute-start(bf16[192,1024]{1,0:T(8,128)(2,1)S(1)} %get-tuple-element.118), channel_id=1, source_target_pairs={{0,4},{1,5},{2,6},{3,7},{4,0},{5,1},{6,2},{7,3},{8,12},{9,13},{10,... | collective-permute-start | bytes 1179656 | tf_op jit(solution)/shard_map/ppermute | solution.py:282
  103.2 1.4 collective-permute-start.12
  104.6 13.4 %local_backward.2 = (bf16[256,1024]{1,0:T(8,128)(2,1)}, f32[2,256,1024]{2,1,0:T(8,128)}, bf16[2,256,1024]{2,1,0:T(8,128)(2,1)}, bf16[2,256,1024]{2,1,0:T(8,128)(2,1)}) custom-call(s32[8]{0:T(128)} %copy-done.4, bf16[256,1024]{1,0:T(8,128)(2,1)} %bitcast.31, bf16[256,1024]{1,0:T(8,128)(2,1)} %convolution_convert_fusion.1.d.refs_1_, ...), custom_call_target="tpu_custom_call" | custom-call | flops 6000000000 | bytes 12058624 | tf_op jit(solution)/shard_map/local_backward/pallas_call | solution.py:250
  118.0 2.5 %collective-permute-done.11 = bf16[192,1024]{1,0:T(8,128)(2,1)S(1)} collective-permute-done((bf16[192,1024]{1,0:T(8,128)(2,1)S(1)}, bf16[192,1024]{1,0:T(8,128)(2,1)S(1)}, u32[]{:S(2)}, u32[]{:S(2)}) %collective-permute-start.11) | collective-permute-done | bytes 393248 | tf_op jit(solution)/shard_map/ppermute | solution.py:282
  120.5 1.0 collective-permute-done.12
  121.6 0.3 add_convert_fusion.1
  121.9 0.8 pad_maximum_fusion
  122.6 4.2 %all-to-all-start.3 = ((bf16[8,24,1024]{2,1,0:T(8,128)(2,1)}), bf16[8,24,1024]{2,1,0:T(8,128)(2,1)S(1)}, u32[]{:S(2)}, u32[]{:S(2)}) async-start(bf16[8,24,1024]{2,1,0:T(8,128)(2,1)} %pad_maximum_fusion), calls=%async_computation.3 | async-start | bytes 786432 | tf_op jit(solution)/shard_map/all_to_all | solution.py:290
  126.9 6.3 %local_backward.3 = (bf16[256,1024]{1,0:T(8,128)(2,1)}, f32[2,256,1024]{2,1,0:T(8,128)}, bf16[2,256,1024]{2,1,0:T(8,128)(2,1)}, bf16[2,256,1024]{2,1,0:T(8,128)(2,1)}) custom-call(s32[8]{0:T(128)} %copy-done.4, bf16[256,1024]{1,0:T(8,128)(2,1)} %bitcast.32, ...), custom_call_target="tpu_custom_call", output_to_operand_aliasing={{0}: (10, {}), {1}: (11, {}), {2}: (12, {}), {3}: (13, {})} | custom-call | flops 2000000000 | bytes 16777216 | tf_op jit(solution)/shard_map/local_backward/pallas_call | solution.py:250
  133.2 1.8 %collective-permute-start.16 = (bf16[2,256,1024]{2,1,0:T(8,128)(2,1)}, bf16[2,256,1024]{2,1,0:T(8,128)(2,1)S(1)}, u32[]{:S(2)}, u32[]{:S(2)}) collective-permute-start(bf16[2,256,1024]{2,1,0:T(8,128)(2,1)} %get-tuple-element.140), channel_id=1, source_target_pairs={{0,1},{1,0},{2,3},{3,2},{4,5},{5,4},{6,7},{7,6},{8,9},{9,8},{10,11... | collective-permute-start | bytes 3145736 | tf_op jit(solution)/shard_map/ppermute | solution.py:282
  135.0 2.4 %collective-permute-start.17 = (bf16[2,256,1024]{2,1,0:T(8,128)(2,1)}, bf16[2,256,1024]{2,1,0:T(8,128)(2,1)}, u32[]{:S(2)}, u32[]{:S(2)}) collective-permute-start(bf16[2,256,1024]{2,1,0:T(8,128)(2,1)} %get-tuple-element.141), channel_id=1, source_target_pairs={{1,2},{2,1},{3,4},{4,3},{5,6},{6,5},{7,8},{8,7},{9,10},{10,9},{11,... | collective-permute-start | bytes 3145736 | tf_op jit(solution)/shard_map/ppermute | solution.py:282
  137.4 1.8 %all-to-all-done.3 = bf16[8,24,1024]{2,1,0:T(8,128)(2,1)S(1)} async-done(((bf16[8,24,1024]{2,1,0:T(8,128)(2,1)}), bf16[8,24,1024]{2,1,0:T(8,128)(2,1)S(1)}, u32[]{:S(2)}, u32[]{:S(2)}) %all-to-all-start.3) | async-done | bytes 393248 | tf_op jit(solution)/shard_map/all_to_all | solution.py:290
  139.3 0.9 broadcast_in_dim.27
  140.2 8.3 %all-to-all-start.4 = ((bf16[32,8,1024]{2,1,0:T(8,128)(2,1)}), bf16[32,8,1024]{2,1,0:T(8,128)(2,1)}, u32[]{:S(2)}, u32[]{:S(2)}) async-start(bf16[32,8,1024]{2,1,0:T(8,128)(2,1)} %broadcast_in_dim.27), calls=%async_computation.4 | async-start | bytes 1048576 | tf_op jit(solution)/shard_map/all_to_all | solution.py:298
  148.5 0.0 copy-start.9
  148.5 1.4 collective-permute-start.13
  149.9 2.6 %collective-permute-start.14 = (f32[16,1024]{1,0:T(8,128)S(1)}, f32[16,1024]{1,0:T(8,128)S(1)}, u32[]{:S(2)}, u32[]{:S(2)}) collective-permute-start(f32[16,1024]{1,0:T(8,128)S(1)} %convert_reduce_fusion), channel_id=1, source_target_pairs={{0,128},{64,192},{128,0},{192,64},{1,129},{65,193},{129,1},{193,65... | collective-permute-start | bytes 196616 | tf_op jit(solution)/shard_map/ppermute | solution.py:423
  152.5 1.1 collective-permute-start.15
  153.6 0.0 collective-permute-done.16
  153.6 1.0 copy-done.8
  154.6 0.0 collective-permute-done.17
  154.6 2.7 %add_convert_fusion.base = bf16[2,256,1024]{2,1,0:T(8,128)(2,1)S(1)} fusion(bf16[2,256,1024]{2,1,0:T(8,128)(2,1)} %collective-permute-done.17, f32[2,256,1024]{2,1,0:T(8,128)} %get-tuple-element.139, bf16[2,256,1024]{2,1,0:T(8,128)(2,1)} %copy-done.8), kind=kLoop, calls=%fused_computation | loop fusion | flops 2621440 | bytes 5242880 | tf_op jit(solution)/shard_map/convert_element_type | solution.py:425
  157.3 0.0 collective-permute-done.13
  157.3 9.7 %all-to-all-done.4 = bf16[32,8,1024]{2,1,0:T(8,128)(2,1)} async-done(((bf16[32,8,1024]{2,1,0:T(8,128)(2,1)}), bf16[32,8,1024]{2,1,0:T(8,128)(2,1)}, u32[]{:S(2)}, u32[]{:S(2)}) %all-to-all-start.4) | async-done | bytes 524320 | tf_op jit(solution)/shard_map/all_to_all | solution.py:298
  167.0 1.0 collective-permute-start.18
  168.0 1.5 add_add_fusion
  169.5 0.3 collective-permute-done.18.far_rest
  169.7 2.3 %combine.1 = (bf16[256,1024]{1,0:T(8,128)(2,1)}, bf16[256,1024]{1,0:T(8,128)(2,1)}) custom-call(s32[8]{0:T(128)S(1)} %copy-done.6, bf16[2,256,1024]{2,1,0:T(8,128)(2,1)S(1)} %add_convert_fusion.base, bf16[256,1024]{1,0:T(8,128)(2,1)} %bitcast.16.far_half, bf16[256,1024]{1,0:T(8,128)(2,1)S(1)} %collective-permute-done.18.far_rest), custom_call_target="tpu_custom_call" | custom-call | tf_op jit(solution)/shard_map/combine/pallas_call | solution.py:195
  (28 shorter events, 0.1 us)
Async XLA Ops:
  0.6 60.6 %copy-start = (bf16[1024,1024]{1,0:T(8,128)(2,1)S(1)}, bf16[1024,1024]{1,0:T(8,128)(2,1)}, u32[]{:S(2)}) copy-start(bf16[1024,1024]{1,0:T(8,128)(2,1)} %param.11) | copy-start | bytes 6291460
  1.4 0.7 copy-start.7
  4.0 59.9 %copy-start.2 = (bf16[2,256,1024]{2,1,0:T(8,128)(2,1)}, bf16[2,256,1024]{2,1,0:T(8,128)(2,1)S(1)}, u32[]{:S(2)}) copy-start(bf16[2,256,1024]{2,1,0:T(8,128)(2,1)S(1)} %get-tuple-element.91.own.refs_2_) | copy-start | bytes 3145732
  4.0 25.5 %collective-permute-start = (bf16[2,64,1024]{2,1,0:T(8,128)(2,1)S(1)}, bf16[2,64,1024]{2,1,0:T(8,128)(2,1)S(1)}, u32[]{:S(2)}, u32[]{:S(2)}) collective-permute-start(bf16[2,64,1024]{2,1,0:T(8,128)(2,1)S(1)} %get-tuple-element.80), channel_id=1, source_target_pairs={{0,2},{1,3},{2,4},{3,5},{4,6},{5,7},{6,0},{7,1},{8,10},{9,11},{10,... | collective-permute-start | bytes 786440 | tf_op jit(solution)/shard_map/ppermute | solution.py:282
  6.1 23.3 %collective-permute-start.1 = (bf16[2,64,1024]{2,1,0:T(8,128)(2,1)S(1)}, bf16[2,64,1024]{2,1,0:T(8,128)(2,1)S(1)}, u32[]{:S(2)}, u32[]{:S(2)}) collective-permute-start(bf16[2,64,1024]{2,1,0:T(8,128)(2,1)S(1)} %get-tuple-element.81), channel_id=1, source_target_pairs={{0,4},{1,5},{2,6},{3,7},{4,0},{5,1},{6,2},{7,3},{8,12},{9,13},{10,... | collective-permute-start | bytes 786440 | tf_op jit(solution)/shard_map/ppermute | solution.py:282
  8.5 20.9 %collective-permute-start.2 = (bf16[2,64,1024]{2,1,0:T(8,128)(2,1)S(1)}, bf16[2,64,1024]{2,1,0:T(8,128)(2,1)S(1)}, u32[]{:S(2)}, u32[]{:S(2)}) collective-permute-start(bf16[2,64,1024]{2,1,0:T(8,128)(2,1)S(1)} %get-tuple-element.82), channel_id=1, source_target_pairs={{0,6},{1,7},{2,0},{3,1},{4,2},{5,3},{6,4},{7,5},{8,14},{9,15},{10,... | collective-permute-start | bytes 786440 | tf_op jit(solution)/shard_map/ppermute | solution.py:282
  30.8 33.0 %copy-start.4 = (s32[8]{0:T(128)}, s32[8]{0:T(128)S(1)}, u32[]{:S(2)}) copy-start(s32[8]{0:T(128)S(1)} %get-tuple-element.83.flags) | copy-start | bytes 100
  30.9 2.0 %collective-permute-start.3 = (bf16[64,1024]{1,0:T(8,128)(2,1)S(1)}, bf16[64,1024]{1,0:T(8,128)(2,1)S(1)}, u32[]{:S(2)}, u32[]{:S(2)}) collective-permute-start(bf16[64,1024]{1,0:T(8,128)(2,1)S(1)} %get-tuple-element.85), channel_id=1, source_target_pairs={{0,1},{1,0},{2,3},{3,2},{4,5},{5,4},{6,7},{7,6},{8,9},{9,8},{10,11... | collective-permute-start | bytes 393224 | tf_op jit(solution)/shard_map/ppermute | solution.py:282
  33.5 17.0 %collective-permute-start.4 = (bf16[2,256,1024]{2,1,0:T(8,128)(2,1)S(1)}, bf16[2,256,1024]{2,1,0:T(8,128)(2,1)}, u32[]{:S(2)}, u32[]{:S(2)}) collective-permute-start(bf16[2,256,1024]{2,1,0:T(8,128)(2,1)S(1)} %get-tuple-element.91.own.refs_2_), channel_id=1, source_target_pairs={{0,1},{1,0},{2,3},{3,2},{4,5},{5,4},{6,7},{7,6},{8,9},{9,8},{10,11... | collective-permute-start | bytes 3145736 | tf_op jit(solution)/shard_map/ppermute | solution.py:282
  33.6 16.9 %collective-permute-start.5 = (bf16[256,1024]{1,0:T(8,128)(2,1)}, bf16[256,1024]{1,0:T(8,128)(2,1)}, u32[]{:S(2)}, u32[]{:S(2)}) collective-permute-start(bf16[256,1024]{1,0:T(8,128)(2,1)} %bitcast.1.key), channel_id=1, source_target_pairs={{1,2},{2,1},{3,4},{4,3},{5,6},{6,5},{7,8},{8,7},{9,10},{10,9},{11,... | collective-permute-start | bytes 1572872 | tf_op jit(solution)/shard_map/ppermute | solution.py:282
  36.1 14.4 %collective-permute-start.6 = (bf16[256,1024]{1,0:T(8,128)(2,1)}, bf16[256,1024]{1,0:T(8,128)(2,1)}, u32[]{:S(2)}, u32[]{:S(2)}) collective-permute-start(bf16[256,1024]{1,0:T(8,128)(2,1)} %bitcast.2.value), channel_id=1, source_target_pairs={{1,2},{2,1},{3,4},{4,3},{5,6},{6,5},{7,8},{8,7},{9,10},{10,9},{11,... | collective-permute-start | bytes 1572872 | tf_op jit(solution)/shard_map/ppermute | solution.py:282
  39.2 11.3 %all-to-all-start.1 = ((bf16[8,8,1024]{2,1,0:T(8,128)(2,1)}), bf16[8,8,1024]{2,1,0:T(8,128)(2,1)S(1)}, u32[]{:S(2)}, u32[]{:S(2)}) async-start(bf16[8,8,1024]{2,1,0:T(8,128)(2,1)} %bitcast.5), calls=%async_computation.1 | async-start | bytes 262144 | tf_op jit(solution)/shard_map/all_to_all | solution.py:290
  51.4 26.7 %all-to-all-start.2 = ((bf16[32,8,1024]{2,1,0:T(8,128)(2,1)}), bf16[32,8,1024]{2,1,0:T(8,128)(2,1)}, u32[]{:S(2)}, u32[]{:S(2)}) async-start(bf16[32,8,1024]{2,1,0:T(8,128)(2,1)} %broadcast_in_dim.24), calls=%async_computation.2 | async-start | bytes 1048576 | tf_op jit(solution)/shard_map/all_to_all | solution.py:298
  78.1 2.4 %collective-permute-start.7 = (bf16[256,1024]{1,0:T(8,128)(2,1)}, bf16[256,1024]{1,0:T(8,128)(2,1)S(1)}, u32[]{:S(2)}, u32[]{:S(2)}) collective-permute-start(bf16[256,1024]{1,0:T(8,128)(2,1)} %bitcast.8.half), channel_id=1, source_target_pairs={{0,1},{1,0},{2,3},{3,2},{4,5},{5,4},{6,7},{7,6},{8,9},{9,8},{10,11... | collective-permute-start | bytes 1572872 | tf_op jit(solution)/shard_map/ppermute | solution.py:282
  80.5 0.8 copy-start.10
  96.6 3.7 %copy-start.1 = (f32[4,8,16,1024]{3,2,1,0:T(8,128)S(1)}, f32[4,8,16,1024]{3,2,1,0:T(8,128)}, u32[]{:S(2)}) copy-start(f32[4,8,16,1024]{3,2,1,0:T(8,128)} %get-tuple-element.109.kept) | copy-start | bytes 6291460
  96.6 3.7 %copy-start.3 = (bf16[256,1024]{1,0:T(8,128)(2,1)S(1)}, bf16[256,1024]{1,0:T(8,128)(2,1)}, u32[]{:S(2)}) copy-start(bf16[256,1024]{1,0:T(8,128)(2,1)} %get-tuple-element.107) | copy-start | bytes 1572868
  96.6 3.7 %copy-start.5 = (s32[8]{0:T(128)S(1)}, s32[8]{0:T(128)}, u32[]{:S(2)}) copy-start(s32[8]{0:T(128)} %copy-done.4) | copy-start | bytes 100
  96.6 3.7 %collective-permute-start.9 = (bf16[4,8,16,1024]{3,2,1,0:T(8,128)(2,1)}, bf16[4,8,16,1024]{3,2,1,0:T(8,128)(2,1)S(1)}, u32[]{:S(2)}, u32[]{:S(2)}) collective-permute-start(bf16[4,8,16,1024]{3,2,1,0:T(8,128)(2,1)} %get-tuple-element.104), channel_id=1, source_target_pairs={{0,1},{1,0},{2,3},{3,2},{4,5},{5,4},{6,7},{7,6},{8,9},{9,8},{10,11... | collective-permute-start | bytes 3145736 | tf_op jit(solution)/shard_map/ppermute | solution.py:282
  97.1 3.2 %collective-permute-start.8 = (bf16[256,1024]{1,0:T(8,128)(2,1)}, bf16[256,1024]{1,0:T(8,128)(2,1)S(1)}, u32[]{:S(2)}, u32[]{:S(2)}) collective-permute-start(bf16[256,1024]{1,0:T(8,128)(2,1)} %get-tuple-element.103), channel_id=1, source_target_pairs={{0,1},{1,0},{2,3},{3,2},{4,5},{5,4},{6,7},{7,6},{8,9},{9,8},{10,11... | collective-permute-start | bytes 1572872 | tf_op jit(solution)/shard_map/ppermute | solution.py:282
  101.2 16.8 %collective-permute-start.10 = (bf16[192,1024]{1,0:T(8,128)(2,1)S(1)}, bf16[192,1024]{1,0:T(8,128)(2,1)S(1)}, u32[]{:S(2)}, u32[]{:S(2)}) collective-permute-start(bf16[192,1024]{1,0:T(8,128)(2,1)S(1)} %get-tuple-element.117), channel_id=1, source_target_pairs={{0,2},{1,3},{2,4},{3,5},{4,6},{5,7},{6,0},{7,1},{8,10},{9,11},{10,... | collective-permute-start | bytes 1179656 | tf_op jit(solution)/shard_map/ppermute | solution.py:282
  101.3 19.2 %collective-permute-start.11 = (bf16[192,1024]{1,0:T(8,128)(2,1)S(1)}, bf16[192,1024]{1,0:T(8,128)(2,1)S(1)}, u32[]{:S(2)}, u32[]{:S(2)}) collective-permute-start(bf16[192,1024]{1,0:T(8,128)(2,1)S(1)} %get-tuple-element.118), channel_id=1, source_target_pairs={{0,4},{1,5},{2,6},{3,7},{4,0},{5,1},{6,2},{7,3},{8,12},{9,13},{10,... | collective-permute-start | bytes 1179656 | tf_op jit(solution)/shard_map/ppermute | solution.py:282
  103.2 18.3 %collective-permute-start.12 = (bf16[192,1024]{1,0:T(8,128)(2,1)S(1)}, bf16[192,1024]{1,0:T(8,128)(2,1)S(1)}, u32[]{:S(2)}, u32[]{:S(2)}) collective-permute-start(bf16[192,1024]{1,0:T(8,128)(2,1)S(1)} %get-tuple-element.119), channel_id=1, source_target_pairs={{0,6},{1,7},{2,0},{3,1},{4,2},{5,3},{6,4},{7,5},{8,14},{9,15},{10,... | collective-permute-start | bytes 1179656 | tf_op jit(solution)/shard_map/ppermute | solution.py:282
  122.6 16.6 %all-to-all-start.3 = ((bf16[8,24,1024]{2,1,0:T(8,128)(2,1)}), bf16[8,24,1024]{2,1,0:T(8,128)(2,1)S(1)}, u32[]{:S(2)}, u32[]{:S(2)}) async-start(bf16[8,24,1024]{2,1,0:T(8,128)(2,1)} %pad_maximum_fusion), calls=%async_computation.3 | async-start | bytes 786432 | tf_op jit(solution)/shard_map/all_to_all | solution.py:290
  133.2 20.3 %collective-permute-start.16 = (bf16[2,256,1024]{2,1,0:T(8,128)(2,1)}, bf16[2,256,1024]{2,1,0:T(8,128)(2,1)S(1)}, u32[]{:S(2)}, u32[]{:S(2)}) collective-permute-start(bf16[2,256,1024]{2,1,0:T(8,128)(2,1)} %get-tuple-element.140), channel_id=1, source_target_pairs={{0,1},{1,0},{2,3},{3,2},{4,5},{5,4},{6,7},{7,6},{8,9},{9,8},{10,11... | collective-permute-start | bytes 3145736 | tf_op jit(solution)/shard_map/ppermute | solution.py:282
  135.0 19.5 %collective-permute-start.17 = (bf16[2,256,1024]{2,1,0:T(8,128)(2,1)}, bf16[2,256,1024]{2,1,0:T(8,128)(2,1)}, u32[]{:S(2)}, u32[]{:S(2)}) collective-permute-start(bf16[2,256,1024]{2,1,0:T(8,128)(2,1)} %get-tuple-element.141), channel_id=1, source_target_pairs={{1,2},{2,1},{3,4},{4,3},{5,6},{6,5},{7,8},{8,7},{9,10},{10,9},{11,... | collective-permute-start | bytes 3145736 | tf_op jit(solution)/shard_map/ppermute | solution.py:282
  140.2 26.8 %all-to-all-start.4 = ((bf16[32,8,1024]{2,1,0:T(8,128)(2,1)}), bf16[32,8,1024]{2,1,0:T(8,128)(2,1)}, u32[]{:S(2)}, u32[]{:S(2)}) async-start(bf16[32,8,1024]{2,1,0:T(8,128)(2,1)} %broadcast_in_dim.27), calls=%async_computation.4 | async-start | bytes 1048576 | tf_op jit(solution)/shard_map/all_to_all | solution.py:298
  148.5 6.1 %copy-start.9 = (f32[16,1024]{1,0:T(8,128)}, f32[16,1024]{1,0:T(8,128)S(1)}, u32[]{:S(2)}) copy-start(f32[16,1024]{1,0:T(8,128)S(1)} %convert_reduce_fusion) | copy-start | bytes 196612
  148.5 21.2 %copy-start.6 = (s32[8]{0:T(128)S(1)}, s32[8]{0:T(128)}, u32[]{:S(2)}) copy-start(s32[8]{0:T(128)} %copy-done.4) | copy-start | bytes 100
  148.5 8.8 %collective-permute-start.13 = (f32[16,1024]{1,0:T(8,128)S(1)}, f32[16,1024]{1,0:T(8,128)S(1)}, u32[]{:S(2)}, u32[]{:S(2)}) collective-permute-start(f32[16,1024]{1,0:T(8,128)S(1)} %convert_reduce_fusion), channel_id=1, source_target_pairs={{0,64},{64,128},{128,192},{192,0},{1,65},{65,129},{129,193},{193,1... | collective-permute-start | bytes 196616 | tf_op jit(solution)/shard_map/ppermute | solution.py:423
  149.9 7.4 %collective-permute-start.14 = (f32[16,1024]{1,0:T(8,128)S(1)}, f32[16,1024]{1,0:T(8,128)S(1)}, u32[]{:S(2)}, u32[]{:S(2)}) collective-permute-start(f32[16,1024]{1,0:T(8,128)S(1)} %convert_reduce_fusion), channel_id=1, source_target_pairs={{0,128},{64,192},{128,0},{192,64},{1,129},{65,193},{129,1},{193,65... | collective-permute-start | bytes 196616 | tf_op jit(solution)/shard_map/ppermute | solution.py:423
  152.5 4.8 %collective-permute-start.15 = (f32[16,1024]{1,0:T(8,128)S(1)}, f32[16,1024]{1,0:T(8,128)S(1)}, u32[]{:S(2)}, u32[]{:S(2)}) collective-permute-start(f32[16,1024]{1,0:T(8,128)S(1)} %convert_reduce_fusion), channel_id=1, source_target_pairs={{0,192},{64,0},{128,64},{192,128},{1,193},{65,1},{129,65},{193,129... | collective-permute-start | bytes 196616 | tf_op jit(solution)/shard_map/ppermute | solution.py:423
  153.6 1.0 copy-start.8
  167.0 2.8 %collective-permute-start.18 = (bf16[256,1024]{1,0:T(8,128)(2,1)}, bf16[256,1024]{1,0:T(8,128)(2,1)S(1)}, u32[]{:S(2)}, u32[]{:S(2)}) collective-permute-start(bf16[256,1024]{1,0:T(8,128)(2,1)} %bitcast.16.far_half), channel_id=1, source_target_pairs={{0,1},{1,0},{2,3},{3,2},{4,5},{5,4},{6,7},{7,6},{8,9},{9,8},{10,11... | collective-permute-start | bytes 1572872 | tf_op jit(solution)/shard_map/ppermute | solution.py:282
